TPU v7x, 32 devices: a whole 2x2x4 slice. The times are simulated.
32 devices in a mesh: dp: 8 (over z, x), mp: 4 (over y, core).
Axes of the slice: x: 2, y: 2, z: 4, core: 2. Of those that a mesh axis runs over, the one named last changes fastest.
Arguments:
- tokens: bfloat16 [4096, 768], P('dp'), may hold values from -6 to 6
- time_embed: bfloat16 [32, 768], P('dp'), may hold values from -6 to 6
- segment_ids: int32 [32, 128], P('dp'), may hold values from 0 to 15, never falling along the last dimension, each value on 1 to 64 neighbouring positions
- norm1_gain: float32 [768], replicated, may hold values from 0.5 to 2
- norm1_bias: float32 [768], replicated, may hold values from -3 to 3
- qkv_weight: bfloat16 [3, 768, 768], P(None, None, 'mp'), may hold values from -0.21875 to 0.21875
- qv_bias: float32 [2, 768], P(None, 'mp'), may hold values from -3 to 3
- out_weight: bfloat16 [768, 768], P('mp'), may hold values from -0.875 to 0.875
- out_bias: float32 [768], replicated, may hold values from -3 to 3
- norm2_gain: float32 [768], replicated, may hold values from 0.5 to 2
- norm2_bias: float32 [768], replicated, may hold values from -3 to 3
- up_weight: bfloat16 [768, 3072], P(None, 'mp'), may hold values from -0.21875 to 0.21875
- up_bias: float32 [3072], P('mp'), may hold values from -3 to 3
- down_weight: bfloat16 [3072, 768], P('mp'), may hold values from -0.109375 to 0.109375
- down_bias: float32 [768], replicated, may hold values from -3 to 3
- cotangent: bfloat16 [4096, 768], P('dp'), may hold values from -6 to 6
Outputs:
- output: bfloat16 [4096, 768], P('dp')
- input_grad: bfloat16 [4096, 768], P('dp')
- time_grad: float32 [32, 768], P('dp')
- norm1_gain_grad: float32 [768], replicated
- norm1_bias_grad: float32 [768], replicated
- qkv_grad: float32 [3, 768, 768], P(None, None, 'mp')
- qv_bias_grad: float32 [2, 768], P(None, 'mp')
- out_weight_grad: float32 [768, 768], P('mp')
- out_bias_grad: float32 [768], replicated
- norm2_gain_grad: float32 [768], replicated
- norm2_bias_grad: float32 [768], replicated
- up_grad: float32 [768, 3072], P(None, 'mp')
- up_bias_grad: float32 [3072], P('mp')
- down_grad: float32 [3072, 768], P('mp')
- down_bias_grad: float32 [768], replicated
Inputs may be any that keep to these rules, and one draw needn't show every extreme that they name: `segment_ids`: within each packed row the ids never fall, each sentence has 1 to 64 positions, and some sentence of each row has exactly 64.
All inputs are finite; a program needn't handle non-finite values.
Results may differ from a plain program's by a relative error of at most 0.0093.
Values sent between devices are 32-bit elements; how exact they have to be, the bound alone decides.
A program may use at most 128 MiB of HBM per device.

v0:
```python
import jax
import jax.numpy as jnp
from jax import lax
from jax.sharding import PartitionSpec as P

HD = 64


def layer_norm(inputs, norm_gain, norm_shift):
    centred = inputs - jnp.mean(inputs, -1, keepdims=True)
    spread = jnp.mean(centred * centred, -1, keepdims=True)
    return centred * lax.rsqrt(spread + 1e-05) * norm_gain + norm_shift


def gelu_exact(inputs):
    return jax.nn.gelu(inputs, approximate=False)


def masked_scores(queries, keys_blk, labels_blk):
    scores = jnp.einsum(
        "rqhd,rkhd->rhqk", queries, keys_blk, preferred_element_type=jnp.float32
    ) * HD ** (-0.5)
    same_doc = (labels_blk[:, :, None] == labels_blk[:, None, :])[:, None]
    return jnp.where(same_doc, scores, -1e30)


def attention_block(pieces):
    queries, keys_blk, values_blk, labels_blk = pieces
    scores = masked_scores(queries, keys_blk, labels_blk)
    row_max = jnp.max(scores, -1, keepdims=True)
    weights = jnp.exp(scores - row_max)
    row_total = jnp.sum(weights, -1, keepdims=True)
    weights_low = (weights / row_total).astype(jnp.bfloat16)
    mixed_blk = jnp.einsum(
        "rhqk,rkhd->rqhd", weights_low, values_blk, preferred_element_type=jnp.float32
    )
    return (mixed_blk.astype(jnp.bfloat16), row_max[..., 0] + jnp.log(row_total[..., 0]))


def attention_back(pieces):
    queries, keys_blk, values_blk, labels_blk, log_total, grad_mixed = pieces
    scores = masked_scores(queries, keys_blk, labels_blk)
    probs = jnp.exp(scores - log_total[..., None])
    weights_low = probs.astype(jnp.bfloat16)
    grad_values = jnp.einsum(
        "rhqk,rqhd->rkhd", weights_low, grad_mixed, preferred_element_type=jnp.float32
    )
    grad_probs = jnp.einsum(
        "rqhd,rkhd->rhqk", grad_mixed, values_blk, preferred_element_type=jnp.float32
    )
    inner_sum = jnp.sum(probs * grad_probs, -1, keepdims=True)
    grad_scores = (probs * (grad_probs - inner_sum)).astype(jnp.bfloat16)
    grad_queries = jnp.einsum(
        "rhqk,rkhd->rqhd", grad_scores, keys_blk, preferred_element_type=jnp.float32
    ) * HD ** (-0.5)
    grad_keys = jnp.einsum(
        "rhqk,rqhd->rkhd", grad_scores, queries, preferred_element_type=jnp.float32
    ) * HD ** (-0.5)
    return (
        grad_queries.astype(jnp.bfloat16),
        grad_keys.astype(jnp.bfloat16),
        grad_values.astype(jnp.bfloat16),
    )


def pack_bucket(arrays, devices):
    flattened = jnp.concatenate([member.reshape(-1) for member in arrays])
    padding = -flattened.shape[0] % devices
    return flattened


def unpack_bucket(flattened, arrays):
    pieces = []
    offset = 0
    for member in arrays:
        extent = member.size
        pieces.append(flattened[offset : offset + extent].reshape(member.shape))
        offset = offset + extent
    return tuple(pieces)


def shards(
    tokens,
    time_embed,
    segment_ids,
    norm1_gain,
    norm1_bias,
    qkv_weight,
    qv_bias,
    out_weight,
    out_bias,
    norm2_gain,
    norm2_bias,
    up_weight,
    up_bias,
    down_weight,
    down_bias,
    cotangent,
):
    row_count, seq_len = segment_ids.shape
    feat_width = tokens.shape[1]
    dp_devices = lax.axis_size("dp")
    heads_local = qkv_weight.shape[2] // HD
    block_rows = min(4, row_count)
    blocks = row_count // block_rows
    split_shape = (blocks, block_rows, seq_len, heads_local, HD)
    start = tokens.astype(jnp.float32).reshape(row_count, seq_len, feat_width)
    start = (start + time_embed.astype(jnp.float32)[:, None, :]).reshape(
        row_count * seq_len, feat_width
    )
    normed1, norm1_back = jax.vjp(layer_norm, start, norm1_gain, norm1_bias)
    entry_low = normed1.astype(jnp.bfloat16)
    queries = (
        jnp.dot(entry_low, qkv_weight[0], preferred_element_type=jnp.float32) + qv_bias[0]
    ).astype(jnp.bfloat16)
    keys_all = jnp.dot(entry_low, qkv_weight[1], preferred_element_type=jnp.float32).astype(
        jnp.bfloat16
    )
    values_all = (
        jnp.dot(entry_low, qkv_weight[2], preferred_element_type=jnp.float32) + qv_bias[1]
    ).astype(jnp.bfloat16)
    labels = segment_ids.reshape(blocks, block_rows, seq_len)
    queries_blk = queries.reshape(split_shape)
    keys_blk = keys_all.reshape(split_shape)
    values_blk = values_all.reshape(split_shape)
    mixed_blk, log_total = lax.map(attention_block, (queries_blk, keys_blk, values_blk, labels))
    mixed_low = mixed_blk.reshape(row_count * seq_len, -1)
    attn_sum = lax.psum(jnp.dot(mixed_low, out_weight, preferred_element_type=jnp.float32), "mp")
    middle = start + (attn_sum + out_bias)
    normed2, norm2_back = jax.vjp(layer_norm, middle, norm2_gain, norm2_bias)
    entry2_low = normed2.astype(jnp.bfloat16)
    hidden_pre = jnp.dot(entry2_low, up_weight, preferred_element_type=jnp.float32) + up_bias
    activated, gelu_back = jax.vjp(gelu_exact, hidden_pre)
    act_low = activated.astype(jnp.bfloat16)
    mlp_sum = lax.psum(jnp.dot(act_low, down_weight, preferred_element_type=jnp.float32), "mp")
    result = (middle + (mlp_sum + down_bias)).astype(jnp.bfloat16)
    grad_float = cotangent.astype(jnp.float32)
    down_bias_grad = jnp.sum(grad_float, 0)
    down_grad = jnp.einsum("tf,td->fd", act_low, cotangent, preferred_element_type=jnp.float32)
    grad_act = jnp.einsum("td,fd->tf", cotangent, down_weight, preferred_element_type=jnp.float32)
    grad_pre = gelu_back(grad_act)[0].astype(jnp.bfloat16)
    up_bias_grad = jnp.sum(grad_pre.astype(jnp.float32), 0)
    up_grad = jnp.einsum("td,tf->df", entry2_low, grad_pre, preferred_element_type=jnp.float32)
    grad_entry2 = lax.psum(
        jnp.einsum("tf,df->td", grad_pre, up_weight, preferred_element_type=jnp.float32), "mp"
    )
    grad_middle, norm2_gain_grad, norm2_bias_grad = norm2_back(grad_entry2)
    grad_middle = grad_middle + grad_float
    mlp_grads = (norm2_gain_grad, norm2_bias_grad, up_grad, up_bias_grad, down_grad, down_bias_grad)
    grad_branch = grad_middle.astype(jnp.bfloat16)
    out_bias_grad = jnp.sum(grad_branch.astype(jnp.float32), 0)
    out_weight_grad = jnp.einsum(
        "te,td->ed", mixed_low, grad_branch, preferred_element_type=jnp.float32
    )
    grad_mixed = jnp.einsum(
        "td,ed->te", grad_branch, out_weight, preferred_element_type=jnp.float32
    )
    grad_mixed = grad_mixed.astype(jnp.bfloat16).reshape(split_shape)
    grad_queries, grad_keys, grad_values = lax.map(
        attention_back, (queries_blk, keys_blk, values_blk, labels, log_total, grad_mixed)
    )
    grad_stack = jnp.stack(
        [
            grad_queries.reshape(row_count * seq_len, -1),
            grad_keys.reshape(row_count * seq_len, -1),
            grad_values.reshape(row_count * seq_len, -1),
        ]
    )
    qkv_grad = jnp.einsum("td,ste->sde", entry_low, grad_stack, preferred_element_type=jnp.float32)
    stack_sums = jnp.sum(grad_stack.astype(jnp.float32), 1)
    qv_bias_grad = jnp.stack([stack_sums[0], stack_sums[2]])
    grad_entry = lax.psum(
        jnp.einsum("ste,sde->td", grad_stack, qkv_weight, preferred_element_type=jnp.float32), "mp"
    )
    grad_start, norm1_gain_grad, norm1_bias_grad = norm1_back(grad_entry)
    grad_start = grad_start + grad_middle
    input_grad = grad_start.astype(jnp.bfloat16)
    time_grad = jnp.sum(grad_start.reshape(row_count, seq_len, feat_width), 1)
    attn_grads = (
        norm1_gain_grad,
        norm1_bias_grad,
        qkv_grad,
        qv_bias_grad,
        out_weight_grad,
        out_bias_grad,
    )
    together = attn_grads + mlp_grads
    grads_flat = lax.psum_scatter(
        pack_bucket(together, dp_devices), "dp", scatter_dimension=0, tiled=True
    )
    together = unpack_bucket(lax.all_gather(grads_flat, "dp", axis=0, tiled=True), together)
    attn_grads = together[:6]
    mlp_grads = together[6:]
    return (
        result,
        input_grad,
        time_grad,
        attn_grads[0],
        attn_grads[1],
        attn_grads[2],
        attn_grads[3],
        attn_grads[4],
        attn_grads[5],
        mlp_grads[0],
        mlp_grads[1],
        mlp_grads[2],
        mlp_grads[3],
        mlp_grads[4],
        mlp_grads[5],
    )


def solution(mesh):
    placed = (
        P("dp", None),
        P("dp", None),
        P("dp", None),
        P(),
        P(),
        P(None, None, "mp"),
        P(None, "mp"),
        P("mp", None),
        P(),
        P(),
        P(),
        P(None, "mp"),
        P("mp"),
        P("mp", None),
        P(),
        P("dp", None),
    )
    return jax.shard_map(
        shards,
        mesh=mesh,
        in_specs=placed,
        out_specs=(
            P("dp", None),
            P("dp", None),
            P("dp", None),
            P(),
            P(),
            P(None, None, "mp"),
            P(None, "mp"),
            P("mp", None),
            P(),
            P(),
            P(),
            P(None, "mp"),
            P("mp"),
            P("mp", None),
            P(),
        ),
        check_vma=False,
    )
```

profile of v0, /device:TPU:0, one launch (start us, length us, event | category | flops | bytes accessed | tf_op | source)
XLA Modules:
  0.0 784.2 jit_solution(5615052537413363789)
XLA Ops:
  19.0 45.6 %all-reduce.9.cloned.1.call-done = f32[512,768]{1,0:T(8,128)} async-done(((f32[512,768]{1,0:T(8,128)}), f32[512,768]{1,0:T(8,128)}) %all-reduce.9.cloned.1.call-update) | async-done | bytes 1572880 | tf_op jit(solution)/shard_map/psum | solution.py:128
  69.1 5.7 convert_reduce_fusion.1
  84.2 36.6 %all-reduce.11.cloned.1.call-done = f32[512,768]{1,0:T(8,128)} async-done(((f32[512,768]{1,0:T(8,128)}), f32[512,768]{1,0:T(8,128)}) %all-reduce.11.cloned.1.call-update) | async-done | bytes 1572880 | tf_op jit(solution)/shard_map/psum | solution.py:144
  120.8 2.7 multiply_reduce_fusion
  134.2 3.3 convolution_bitcast_fusion.1
  138.7 2.4 fusion.48
  141.1 3.3 reshape.176
  144.5 3.3 fusion.62
  147.8 3.3 reshape.177
  151.1 3.0 convolution_bitcast_fusion
  154.1 2.9 copy.77
  157.0 3.5 reshape.173
  164.2 42.2 %all-reduce.17.cloned.1.call-done = (f32[512,768]{1,0:T(8,128)}, f32[512,768]{1,0:T(8,128)}) async-done(((f32[512,768]{1,0:T(8,128)}, f32[512,768]{1,0:T(8,128)}), (f32[512,768]{1,0:T(8,128)}, f32[512,768]{1,0:T(8,128)})) %all-reduce.17.cloned.1.call-update) | async-done | bytes 3145744 | tf_op jit(solution)/shard_map/psum | solution.py:135
  212.0 16.4 %dynamic-update-slice.3 = f32[1775232]{0:T(1024)} dynamic-update-slice(f32[1775232]{0:T(1024)} %constant_dynamic-update-slice_fusion.11, f32[442368]{0:T(1024)} %reshape.173, s32[]{} %constant.140) | dynamic-update-slice | bytes 3538948
  235.5 21.2 %dynamic-update-slice.9 = f32[1775232]{0:T(1024)} dynamic-update-slice(f32[1775232]{0:T(1024)} %constant_dynamic-update-slice_fusion.6, f32[589824]{0:T(1024)} %reshape.176, s32[]{} %constant.146) | dynamic-update-slice | bytes 4718596
  258.0 21.0 %dynamic-update-slice.11 = f32[1775232]{0:T(1024)} dynamic-update-slice(f32[1775232]{0:T(1024)} %constant_dynamic-update-slice_fusion.5, f32[589824]{0:T(1024)} %reshape.177, s32[]{} %constant.148) | dynamic-update-slice | bytes 4718596
  282.9 233.4 %all-reduce.15.cloned.1.call-done = f32[1775232]{0:T(1024)} async-done(((f32[1775232]{0:T(1024)}), f32[1775232]{0:T(1024)}) %all-reduce.15.cloned.1.call-update) | async-done | bytes 7100944
  516.3 3.1 broadcast.127
  519.4 3.0 dynamic-slice_dynamic-update-slice_fusion
  523.6 4.3 bitcast_reduce_fusion
  529.0 228.4 %all-reduce.13.cloned.1.call-done = f32[1775232]{0:T(1024)} async-done(((f32[1775232]{0:T(1024)}), f32[1775232]{0:T(1024)}) %all-reduce.13.cloned.1.call-update) | async-done | bytes 7100944
  757.4 4.1 fusion.55
  761.5 3.4 reshape.181
  766.5 2.8 slice.88
  (226 shorter events, 69.1 us)
Async XLA Ops:
  7.2 61.7 %copy-start = (bf16[768,768]{1,0:T(8,128)(2,1)S(1)}, bf16[768,768]{1,0:T(8,128)(2,1)}, u32[]{:S(2)}) copy-start(bf16[768,768]{1,0:T(8,128)(2,1)} %param.29) | copy-start | bytes 3538948
  7.2 57.4 %all-reduce.9.cloned.1.call-start = ((), (), s32[]{:S(2)}) async-start(), calls=%async_computation | async-start | bytes 3145728 | tf_op jit(solution)/shard_map/psum | solution.py:128
  19.0 101.8 %all-reduce.11.cloned.1.call-start = ((), (), s32[]{:S(2)}) async-start(), calls=%async_computation.1 | async-start | bytes 3145728 | tf_op jit(solution)/shard_map/psum | solution.py:144
  69.1 5.7 copy-start.21
  77.7 128.7 %all-reduce.17.cloned.1.call-start = ((), (), s32[]{:S(2)}) async-start(), calls=%async_computation.4 | async-start | bytes 6291456 | tf_op jit(solution)/shard_map/psum | solution.py:135
  84.2 39.3 %copy-start.43 = (f32[512]{0:T(512)S(1)}, f32[512]{0:T(512)}, u32[]{:S(2)}) copy-start(f32[512]{0:T(512)} %copy-done.42) | copy-start | bytes 6148
  84.2 39.4 %copy-start.38 = (f32[512]{0:T(512)S(1)}, f32[512]{0:T(512)}, u32[]{:S(2)}) copy-start(f32[512]{0:T(512)} %copy-done.37) | copy-start | bytes 6148
  84.2 39.4 %copy-start.47 = (f32[512]{0:T(512)S(1)}, f32[512]{0:T(512)}, u32[]{:S(2)}) copy-start(f32[512]{0:T(512)} %copy-done.46) | copy-start | bytes 6148
  84.2 39.4 %copy-start.54 = (f32[768]{0:T(1024)S(1)}, f32[768]{0:T(1024)}, u32[]{:S(2)}) copy-start(f32[768]{0:T(1024)} %param.25) | copy-start | bytes 9220
  137.6 378.7 %all-reduce.15.cloned.1.call-start = ((), (), s32[]{:S(2)}) async-start(), calls=%async_computation.3 | async-start | bytes 14204928
  157.0 4.9 copy-start.8
  157.0 4.9 copy-start.19
  160.6 45.9 %copy-start.32 = (f32[768]{0:T(1024)S(1)}, f32[768]{0:T(1024)}, u32[]{:S(2)}) copy-start(f32[768]{0:T(1024)} %param.19) | copy-start | bytes 9220
  163.1 45.3 %copy-start.41 = (f32[512]{0:T(512)S(1)}, f32[512]{0:T(512)}, u32[]{:S(2)}) copy-start(f32[512]{0:T(512)} %copy-done.40) | copy-start | bytes 6148
  163.1 45.4 %copy-start.34 = (f32[512]{0:T(512)S(1)}, f32[512]{0:T(512)}, u32[]{:S(2)}) copy-start(f32[512]{0:T(512)} %copy-done.33) | copy-start | bytes 6148
  212.0 19.6 %copy-start.52 = (f32[768]{0:T(1024)S(1)}, f32[768]{0:T(1024)}, u32[]{:S(2)}) copy-start(f32[768]{0:T(1024)} %get-tuple-element.108) | copy-start | bytes 9220
  212.0 20.9 %copy-start.51 = (f32[768]{0:T(1024)S(1)}, f32[768]{0:T(1024)}, u32[]{:S(2)}) copy-start(f32[768]{0:T(1024)} %get-tuple-element.96) | copy-start | bytes 9220
  212.0 22.2 %copy-start.50 = (f32[768]{0:T(1024)S(1)}, f32[768]{0:T(1024)}, u32[]{:S(2)}) copy-start(f32[768]{0:T(1024)} %get-tuple-element.100) | copy-start | bytes 9220
  235.5 21.2 %copy-start.59 = (f32[768]{0:T(1024)S(1)}, f32[768]{0:T(1024)}, u32[]{:S(2)}) copy-start(f32[768]{0:T(1024)} %get-tuple-element.105) | copy-start | bytes 9220
  258.0 21.0 %copy-start.49 = (f32[768]{0:T(1024)S(1)}, f32[768]{0:T(1024)}, u32[]{:S(2)}) copy-start(f32[768]{0:T(1024)} %get-tuple-element.125) | copy-start | bytes 9220
  280.4 477.1 %all-reduce.13.cloned.1.call-start = ((), (), s32[]{:S(2)}) async-start(), calls=%async_computation.2 | async-start | bytes 14204928
  523.6 4.3 copy-start.20
  523.6 4.3 copy-start.58
  771.1 6.6 copy-start.1
  (50 other events, 85.9 us)
Sparse Core Ops, SparseCore 0:
  19.1 45.5 all-reduce.8
  77.8 42.8 all-reduce.10
  137.7 68.6 all-reduce.16
  280.5 235.7 all-reduce.14
  522.6 234.7 all-reduce.12
where the time goes:
time: 789 us; the launch traced here: 784 us
  waiting for transfers between devices  586 us (74%)
  local copies, waits for them, and re-layouts  125 us (16%)
  matrix products  32.2 us (4%)
  other arithmetic  24 us (3%)
  between operations  15.9 us (2%)
    unnamed x7, waiting for transfers between devices  462 us
    unnamed x155, local copies, waits for them, and re-layouts  87.6 us
    psum x1, waiting for transfers between devices, shards(): lax.psum(jnp.dot(mixed_low, out_weight, preferred_element_type=jnp.float3...  45.6 us
    psum x1, waiting for transfers between devices, shards(): lax.psum(jnp.dot(act_low, down_weight, preferred_element_type=jnp.float32...  42.2 us
    psum x1, waiting for transfers between devices, shards(): lax.psum(jnp.einsum('tf,df->td', grad_pre, up_weight, preferred_element_t...  36.6 us
  transfers between devices with their start and end apart: 5, of which 5 were waited for; matrix products, arithmetic and copies ran while one was open for 5% of the time, Pallas kernels for 0%

commit v1 on v0

v1 whole, which is shorter than its diff:
```python
import functools

import jax
import jax.numpy as jnp
from jax import lax
from jax.experimental import pallas as pl
from jax.experimental.pallas import tpu as pltpu
from jax.sharding import PartitionSpec as P

HD = 64
SUB = 32
CH = 8
MESH = pl.DeviceIdType.MESH
F32 = jnp.float32
BF16 = jnp.bfloat16


def when(cond, fn):
    pl.when(cond)(fn)


def nt(a, b):
    return lax.dot_general(a, b, (((1,), (1,)), ((), ())), preferred_element_type=F32)


def tn(a, b):
    return lax.dot_general(a, b, (((0,), (0,)), ((), ())), preferred_element_type=F32)


def nn(a, b):
    return jnp.dot(a, b, preferred_element_type=F32)


def normed(v):
    centred = v - jnp.mean(v, -1, keepdims=True)
    spread = jnp.mean(centred * centred, -1, keepdims=True)
    scale = lax.rsqrt(spread + 1e-05)
    return centred * scale, scale


def colsum(v):
    return jnp.sum(v, 0, keepdims=True)


def kernel(n_dp, units, names, *refs):
    (tok, tim, seg, n1g, n1b, wqkv, qvb, wout, outb, n2g, n2b, wup, upb, wdn, dnb, cot) = refs[:16]
    out, ig, tg, fa_out, fb_out = refs[16:21]
    R = dict(zip(names, refs[21:]))
    timf, start, entry, q_s, k_s, v_s = (R[s] for s in ("timf", "start", "entry", "q", "k", "v"))
    probs, mixed_s, part, cr, ys, yr = (R[s] for s in ("probs", "mixed", "part", "cr", "ys", "yr"))
    tot, mid, e2, hp, act, gp = (R[s] for s in ("tot", "mid", "e2", "hp", "act", "gp"))
    gact, gmid, gbr, lta, ltb = (R[s] for s in ("gact", "gmid", "gbr", "lta", "ltb"))
    ga, gb, fa, fb = (R[s] for s in ("ga", "gb", "fa", "fb"))

    rows_n, seq = seg.shape
    width = tok.shape[1]
    half = width // 2
    loc = wout.shape[0]
    heads = loc // HD
    ff = wup.shape[1]
    UA, UB = units
    L = n_dp // 2
    D = L // 2
    root = D - 1
    dp = lax.axis_index("dp")
    mp = lax.axis_index("mp")
    core = mp % 2
    x = dp % 2
    z = dp // 2
    to_core = (dp, mp + 1 - 2 * core)
    to_y = (dp, (mp + 2) % 4)
    to_x = (dp + 1 - 2 * x, mp)
    zlo = jnp.maximum(z - 1, 0) * 2 + x
    zhi = jnp.minimum(z + 1, L - 1) * 2 + x

    barrier = pltpu.get_barrier_semaphore()
    for dev in (to_core, to_y, to_x):
        pl.semaphore_signal(barrier, 1, device_id=dev, device_id_type=MESH)
    when(z > 0, lambda: pl.semaphore_signal(barrier, 1, device_id=(zlo, mp), device_id_type=MESH))
    when(z < L - 1, lambda: pl.semaphore_signal(barrier, 1, device_id=(zhi, mp), device_id_type=MESH))

    def sl(r, n=seq):
        return pl.ds(pl.multiple_of(r * n, n), n)

    def sub(r, i):
        return pl.ds(pl.multiple_of(r * seq + i * SUB, SUB), SUB)

    mine = pl.ds(pl.multiple_of(core * half, 128), half)
    other = pl.ds(pl.multiple_of((1 - core) * half, 128), half)

    def remote(src, dst, ssem, rsem, dev):
        return pltpu.make_async_remote_copy(
            src_ref=src, dst_ref=dst, send_sem=ssem, recv_sem=rsem, device_id=dev, device_id_type=MESH
        )

    def core_copy(p, r):
        i = p * rows_n + r
        return remote(part.at[sl(r), other], cr.at[sl(r)], R["cs"].at[i], R["crs"].at[i], to_core)

    def y_copy(p, r):
        i = p * rows_n + r
        return remote(ys.at[sl(r)], yr.at[p % 2, sl(r)], R["yss"].at[i], R["yrs"].at[i], to_y)

    def ag_copy(p, r):
        i = p * rows_n + r
        return remote(tot.at[sl(r), mine], tot.at[sl(r), mine], R["gs"].at[i], R["grs"].at[i], to_core)

    def sum_b(p, r):
        core_copy(p, r).wait()
        ys[sl(r), :] = part[sl(r), mine] + cr[sl(r), :]
        y_copy(p, r).start()

    def sum_c(p, r):
        y_copy(p, r).wait()
        tot[sl(r), mine] = ys[sl(r), :] + yr[p % 2, sl(r), :]
        ag_copy(p, r).start()

    def sum_d(p, r):
        ag_copy(p, r).wait()

    def vec(ref):
        return ref[...]

    small = UA * 4 * CH - 4 * CH

    def small_add(i, v):
        ga[small + i : small + i + 1, :] += v

    lane = lax.broadcasted_iota(jnp.int32, (1, loc), 1)
    masks = [((lane >= h * HD) & (lane < (h + 1) * HD)).astype(F32) for h in range(heads)]

    def by_head(v):
        return jnp.concatenate([v * m.astype(BF16) for m in masks], 0)

    def from_heads(v):
        total = v[:seq] * masks[0]
        for h in range(1, heads):
            total = total + v[h * seq : (h + 1) * seq] * masks[h]
        return total

    def norm1(r):
        @pl.loop(0, seq // SUB)
        def _(i):
            s = sub(r, i)
            v = tok[s, :].astype(F32) + timf[pl.ds(r, 1), :]
            start[s, :] = v
            xhat, _ = normed(v)
            entry[s, :] = (xhat * n1g[...] + n1b[...]).astype(BF16)

    def project(r):
        e = entry[sl(r), :]
        q_s[sl(r), :] = (nn(e, wqkv[0]) + qvb[0:1, :]).astype(BF16)
        k_s[sl(r), :] = nn(e, wqkv[1]).astype(BF16)
        v_s[sl(r), :] = (nn(e, wqkv[2]) + qvb[1:2, :]).astype(BF16)

    def attend(r):
        labels = jnp.broadcast_to(seg[pl.ds(r, 1), :], (seq, seq))
        same = labels == labels.T
        same = jnp.concatenate([same.astype(F32)] * heads, 0) > 0.5
        scores = nt(by_head(q_s[sl(r), :]), k_s[sl(r), :]) * HD ** (-0.5)
        scores = jnp.where(same, scores, -1e30)
        w = jnp.exp(scores - jnp.max(scores, -1, keepdims=True))
        pr = w / jnp.sum(w, -1, keepdims=True)
        probs[sl(r, heads * seq), :] = pr
        mixed = from_heads(nn(pr.astype(BF16), v_s[sl(r), :])).astype(BF16)
        mixed_s[sl(r), :] = mixed
        part[sl(r), :] = nn(mixed, wout[...])
        core_copy(0, r).start()
        lta[ff : ff + loc, sl(r)] = mixed.T

    def grad_act(r):
        c = cot[sl(r), :]
        gact[sl(r), :] = nt(c, wdn[...])
        small_add(0, colsum(c.astype(F32)))

    def feed(r):
        @pl.loop(0, seq // SUB)
        def _(i):
            s = sub(r, i)
            v = start[s, :] + (tot[s, :] + outb[...])
            mid[s, :] = v
            xhat, _ = normed(v)
            e2[s, :] = (xhat * n2g[...] + n2b[...]).astype(BF16)

        hp[...] = nn(e2[sl(r), :], wup[...])

        @pl.loop(0, seq // SUB)
        def _(i):
            s = sub(r, i)
            u = hp[pl.ds(pl.multiple_of(i * SUB, SUB), SUB), :] + upb[...]
            cdf = 0.5 * (1.0 + lax.erf(u * 0.7071067811865476))
            act[s, :] = (u * cdf).astype(BF16)
            slope = cdf + u * (0.3989422804014327 * jnp.exp(-0.5 * u * u))
            g = (gact[s, :] * slope).astype(BF16)
            gp[s, :] = g
            small_add(1, colsum(g.astype(F32)))

        part[sl(r), :] = nt(gp[sl(r), :], wup[...])
        core_copy(1, r).start()
        lta[0:ff, sl(r)] = act[sl(r), :].T
        ltb[0:width, sl(r)] = e2[sl(r), :].T

    def back2(r):
        @pl.loop(0, seq // SUB)
        def _(i):
            s = sub(r, i)
            g = tot[s, :]
            xhat, scale = normed(mid[s, :])
            small_add(2, colsum(g * xhat))
            small_add(3, colsum(g))
            gx = g * n2g[...]
            gm = cot[s, :].astype(F32) + scale * (
                gx - jnp.mean(gx, -1, keepdims=True) - xhat * jnp.mean(gx * xhat, -1, keepdims=True)
            )
            gmid[s, :] = gm
            low = gm.astype(BF16)
            gbr[s, :] = low
            small_add(4, colsum(low.astype(F32)))

        g3 = by_head(nt(gbr[sl(r), :], wout[...]).astype(BF16))
        pr = probs[sl(r, heads * seq), :]
        grad_probs = nt(g3, v_s[sl(r), :])
        inner = jnp.sum(pr * grad_probs, -1, keepdims=True)
        ds = (pr * (grad_probs - inner)).astype(BF16)
        gq = (from_heads(nn(ds, k_s[sl(r), :])) * HD ** (-0.5)).astype(BF16)
        gk = (tn(ds, by_head(q_s[sl(r), :])) * HD ** (-0.5)).astype(BF16)
        gv = tn(pr.astype(BF16), g3).astype(BF16)
        part[sl(r), :] = nt(gq, wqkv[0]) + nt(gk, wqkv[1]) + nt(gv, wqkv[2])
        core_copy(2, r).start()
        lta[ff + loc : ff + 2 * loc, sl(r)] = gq.T
        ltb[width : width + loc, sl(r)] = gk.T
        ltb[width + loc : width + 2 * loc, sl(r)] = gv.T
        ga[small + 7 : small + 8, 0:loc] += colsum(gq.astype(F32))
        ga[small + 7 : small + 8, half : half + loc] += colsum(gv.astype(F32))

    def back1(r):
        tg[pl.ds(r, 1), :] = jnp.zeros((1, width), F32)

        @pl.loop(0, seq // SUB)
        def _(i):
            s = sub(r, i)
            g = tot[s, :]
            xhat, scale = normed(start[s, :])
            small_add(5, colsum(g * xhat))
            small_add(6, colsum(g))
            gy = g * n1g[...]
            gs = gmid[s, :] + scale * (
                gy - jnp.mean(gy, -1, keepdims=True) - xhat * jnp.mean(gy * xhat, -1, keepdims=True)
            )
            ig[s, :] = gs.astype(BF16)
            tg[pl.ds(r, 1), :] += colsum(gs)

    def down(r):
        part[sl(r), :] = nn(act[sl(r), :], wdn[...])
        core_copy(3, r).start()

    def finish(r):
        @pl.loop(0, seq // SUB)
        def _(i):
            s = sub(r, i)
            out[s, :] = (mid[s, :] + (tot[s, :] + dnb[...])).astype(BF16)

    blk = loc

    def weight_grads(j):
        s = pl.ds(pl.multiple_of(j * blk, blk), blk)
        late = ff // blk

        def a_early():
            ga[s, :] = nn(lta[s, :], cot[...])
            gb[s, :] = nn(ltb[s, :], gp[...])

        def a_out():
            ga[s, :] = nn(lta[s, :], gbr[...])

        def a_q():
            ga[s, :] = nn(lta[s, :], entry[...])

        def b_late():
            gb[s, :] = nn(ltb[s, :], entry[...])

        when(j < late, a_early)
        when(j == late, a_out)
        when(j == late + 1, a_q)
        when(j >= late, b_late)

    def ok(u, n):
        return (u >= 0) & (u < n)

    def a_own(u, d):
        return pl.ds(pl.multiple_of(u * 4 * CH + x * 2 * CH + d * CH, CH), CH)

    def a_slot(u):
        return pl.ds(pl.multiple_of(u * CH, CH), CH)

    def b_own(u, d):
        return pl.ds(pl.multiple_of(u * 4 * CH + d * 2 * CH, CH), 2 * CH)

    def b_slot(u):
        return pl.ds(pl.multiple_of(u * 2 * CH, CH), 2 * CH)

    def x_first(u):
        src = pl.ds(pl.multiple_of(u * 4 * CH + (1 - x) * 2 * CH, CH), 2 * CH)
        return remote(ga.at[src], R["xrb"].at[b_slot(u)], R["xs"].at[u], R["xr"].at[u], to_x)

    ways = []
    for d in (0, 1):
        w = z if d == 0 else L - 1 - z
        up = (zhi if d == 0 else zlo, mp)
        dn = (zlo if d == 0 else zhi, mp)
        ways.append((d, w, up, dn))

    def streams(kind, d, up, dn):
        if kind == "a":
            g, f, lo, hi, own, slot = ga, fa, R["arl"], R["arh"], a_own, a_slot
            s, lr, hr, bu, bd, br = (R[t] for t in ("ars", "arlr", "arhr", "abu", "abd", "abr"))
        else:
            g, f, lo, hi, own, slot = gb, fb, R["brl"], R["brh"], b_own, b_slot
            s, lr, hr, bu, bd, br = (R[t] for t in ("brs", "brlr", "brhr", "bbu", "bbd", "bbr"))

        def send_up(u):
            return remote(g.at[own(u, d)], lo.at[d, slot(u)], s.at[d, u], lr.at[d, u], up)

        def send_dn(u):
            return remote(g.at[own(u, d)], hi.at[d, slot(u)], s.at[d, u], hr.at[d, u], dn)

        def bcast_up(u):
            return remote(f.at[own(u, d)], f.at[own(u, d)], bu.at[d, u], br.at[d, u], up)

        def bcast_dn(u):
            return remote(f.at[own(u, d)], f.at[own(u, d)], bd.at[d, u], br.at[d, u], dn)

        return g, f, lo, hi, own, slot, send_up, send_dn, bcast_up, bcast_dn

    def x_last(u, d):
        s = a_own(u, d)
        return remote(fa.at[s], fa.at[s], R["xgs"].at[d, u], R["xgr"].at[d, u], to_x)

    def x_last_in(u, d):
        s = pl.ds(pl.multiple_of(u * 4 * CH + (1 - x) * 2 * CH + d * CH, CH), CH)
        return remote(fa.at[s], fa.at[s], R["xgs"].at[d, u], R["xgr"].at[d, u], to_x)

    def b_x(u, d):
        return remote(gb.at[b_own(u, d)], R["bxb"].at[d, b_slot(u)], R["bxs"].at[d, u], R["bxr"].at[d, u], to_x)

    def reduce_step(kind, d, w, up, dn, u):
        g, f, lo, hi, own, slot, send_up, send_dn, bcast_up, bcast_dn = streams(kind, d, up, dn)

        def from_low():
            send_up(u).wait_recv()
            g[own(u, d), :] += lo[d, slot(u), :]

        def from_high():
            send_dn(u).wait_recv()
            g[own(u, d), :] += hi[d, slot(u), :]

        when((w > 0) & (w <= root), from_low)
        when((w < L - 1) & (w >= root), from_high)
        when(w < root, lambda: send_up(u).start())
        when(w > root, lambda: send_dn(u).start())

    def root_step(kind, d, w, up, dn, u):
        g, f, lo, hi, own, slot, send_up, send_dn, bcast_up, bcast_dn = streams(kind, d, up, dn)
        if kind == "a":
            f[own(u, d), :] = g[own(u, d), :]
        else:
            b_x(u, d).wait_recv()
            f[own(u, d), :] = g[own(u, d), :] + R["bxb"][d, slot(u), :]
        bcast_up(u).start()
        when(w > 0, lambda: bcast_dn(u).start())
        if kind == "a":
            x_last(u, d).start()

    def spread_step(kind, d, w, up, dn, u):
        g, f, lo, hi, own, slot, send_up, send_dn, bcast_up, bcast_dn = streams(kind, d, up, dn)
        bcast_up(u).wait_recv()
        when((w > root) & (w < L - 1), lambda: bcast_up(u).start())
        when((w < root) & (w > 0), lambda: bcast_dn(u).start())
        if kind == "a":
            x_last(u, d).start()

    def dp_tick(t):
        when(t < UA, lambda: x_first(t).start())

        def x_add():
            u = t - 1
            x_first(u).wait_recv()
            s = pl.ds(pl.multiple_of(u * 4 * CH + x * 2 * CH, CH), 2 * CH)
            ga[s, :] += R["xrb"][b_slot(u), :]

        when(ok(t - 1, UA), x_add)
        for kind, n, first, gap in (("b", UB, 0, 1), ("a", UA, 1, 0)):
            for d, w, up, dn in ways:
                far = jnp.where(w <= root, w + 1, L - 1 - w)
                dist = jnp.abs(w - root)
                u = t - first - far
                when(ok(u, n), functools.partial(reduce_step, kind, d, w, up, dn, u))
                if kind == "b":
                    when(ok(u, n) & (w == root), lambda u=u, d=d: b_x(u, d).start())
                v = t - first - D - gap
                when(ok(v, n) & (w == root), functools.partial(root_step, kind, d, w, up, dn, v))
                v = t - first - D - gap - dist
                when(ok(v, n) & (w != root), functools.partial(spread_step, kind, d, w, up, dn, v))

    def dp_drain():
        @pl.loop(0, UA)
        def _(u):
            x_first(u).wait_send()
            for d, w, up, dn in ways:
                x_last(u, d).wait_send()
                x_last_in(u, d).wait_recv()

        for kind, n in (("a", UA), ("b", UB)):

            @pl.loop(0, n)
            def _(u):
                for d, w, up, dn in ways:
                    fs = streams(kind, d, up, dn)
                    when(w != root, lambda: fs[6](u).wait_send())
                    when((w >= root) & (w < L - 1), lambda: fs[8](u).wait_send())
                    when((w <= root) & (w > 0), lambda: fs[9](u).wait_send())
                    if kind == "b":
                        when(w == root, lambda: b_x(u, d).wait_send())

    timf[...] = tim[...].astype(F32)
    ga[small : small + 4 * CH, :] = jnp.zeros((4 * CH, width), F32)
    pl.loop(0, rows_n)(norm1)
    pl.loop(0, rows_n)(project)
    pl.semaphore_wait(barrier, 3 + jnp.minimum(z, 1) + jnp.minimum(L - 1 - z, 1))

    @pl.loop(0, rows_n)
    def _(r):
        attend(r)
        when(r > 0, lambda: sum_b(0, r - 1))

    sum_b(0, rows_n - 1)

    @pl.loop(0, rows_n)
    def _(r):
        grad_act(r)
        sum_c(0, r)
        sum_d(0, r)
        feed(r)
        sum_b(1, r)

    weight_grads(0)

    ticks = max(UA, UB) + 2 * D + 1
    per = blk // (4 * CH)
    blocks = (ff + 2 * loc) // blk

    @pl.loop(0, ticks)
    def _(t):
        dp_tick(t)

        def at(first, step, fn):
            r = (t - first) // step
            when((t >= first) & ((t - first) % step == 0) & (r < rows_n), lambda: fn(r))

        at(0, 2, lambda r: sum_c(1, r))

        def second(r):
            sum_d(1, r)
            back2(r)

        at(1, 2, second)
        at(2, 2, lambda r: sum_b(2, r))
        at(5, 2, lambda r: sum_c(2, r))

        def third(r):
            sum_d(2, r)
            back1(r)

        at(6, 2, third)
        at(9, 2, down)
        at(10, 2, lambda r: sum_b(3, r))
        at(13, 2, lambda r: sum_c(3, r))

        def fourth(r):
            sum_d(3, r)
            finish(r)

        at(14, 2, fourth)
        when((t % per == per - 2) & (t // per + 1 < blocks), lambda: weight_grads(t // per + 1))

    dp_drain()
    copies = [
        pltpu.make_async_copy(fa, fa_out, R["fin"].at[0]),
        pltpu.make_async_copy(fb, fb_out, R["fin"].at[1]),
    ]
    for copy in copies:
        copy.start()
    for copy in copies:
        copy.wait()


def shards(n_dp, *args):
    (tok, tim, seg, n1g, n1b, wqkv, qvb, wout, outb, n2g, n2b, wup, upb, wdn, dnb, cot) = args
    tokens, width = tok.shape
    rows_n, seq = seg.shape
    loc, ff = wout.shape[0], wup.shape[1]
    heads = loc // HD
    half = width // 2
    big = ff + 2 * loc
    UB = big // (4 * CH)
    UA = UB + 1
    vm = pltpu.VMEM
    dma = pltpu.SemaphoreType.DMA
    dp_sem = lambda n: dma((2, n))
    scratch = dict(
        timf=vm((rows_n, width), F32),
        start=vm((tokens, width), F32),
        entry=vm((tokens, width), BF16),
        q=vm((tokens, loc), BF16),
        k=vm((tokens, loc), BF16),
        v=vm((tokens, loc), BF16),
        probs=vm((heads * tokens, seq), F32),
        mixed=vm((tokens, loc), BF16),
        part=vm((tokens, width), F32),
        cr=vm((tokens, half), F32),
        ys=vm((tokens, half), F32),
        yr=vm((2, tokens, half), F32),
        tot=vm((tokens, width), F32),
        mid=vm((tokens, width), F32),
        e2=vm((tokens, width), BF16),
        hp=vm((seq, ff), F32),
        act=vm((tokens, ff), BF16),
        gp=vm((tokens, ff), BF16),
        gact=vm((tokens, ff), F32),
        gmid=vm((tokens, width), F32),
        gbr=vm((tokens, width), BF16),
        lta=vm((big, tokens), BF16),
        ltb=vm((big, tokens), BF16),
        ga=vm((UA * 4 * CH, width), F32),
        gb=vm((UB * 4 * CH, width), F32),
        fa=vm((UA * 4 * CH, width), F32),
        fb=vm((UB * 4 * CH, width), F32),
        xrb=vm((UA * 2 * CH, width), F32),
        arl=vm((2, UA * CH, width), F32),
        arh=vm((2, UA * CH, width), F32),
        brl=vm((2, UB * 2 * CH, width), F32),
        brh=vm((2, UB * 2 * CH, width), F32),
        bxb=vm((2, UB * 2 * CH, width), F32),
        **{s: dma((4 * rows_n,)) for s in ("cs", "crs", "yss", "yrs", "gs", "grs")},
        fin=dma((2,)),
        **{s: dma((UA,)) for s in ("xs", "xr")},
        **{s: dp_sem(UA) for s in ("ars", "arlr", "arhr", "abu", "abd", "abr", "xgs", "xgr")},
        **{s: dp_sem(UB) for s in ("brs", "brlr", "brhr", "bxs", "bxr", "bbu", "bbd", "bbr")},
    )
    row = lambda v: v.reshape(1, -1)
    any_spec = pl.BlockSpec(memory_space=pl.ANY)
    vm_spec = pl.BlockSpec(memory_space=pltpu.VMEM)
    out, ig, tg, fa, fb = pl.pallas_call(
        functools.partial(kernel, n_dp, (UA, UB), tuple(scratch)),
        out_shape=(
            jax.ShapeDtypeStruct((tokens, width), BF16),
            jax.ShapeDtypeStruct((tokens, width), BF16),
            jax.ShapeDtypeStruct((rows_n, width), F32),
            jax.ShapeDtypeStruct((UA * 4 * CH, width), F32),
            jax.ShapeDtypeStruct((UB * 4 * CH, width), F32),
        ),
        in_specs=[vm_spec] * 16,
        out_specs=(vm_spec, vm_spec, vm_spec, any_spec, any_spec),
        scratch_shapes=list(scratch.values()),
        compiler_params=pltpu.CompilerParams(
            collective_id=0, has_side_effects=True, vmem_limit_bytes=63 * 2**20
        ),
        cost_estimate=pl.CostEstimate(flops=6 * 10**9, bytes_accessed=20 * 10**6, transcendentals=0),
    )(
        tok, tim, seg, row(n1g), row(n1b), wqkv, qvb, wout, row(outb), row(n2g), row(n2b), wup, row(upb), wdn,
        row(dnb), cot,
    )
    sm = fa[big : big + 8]
    qkv_grad = jnp.stack([fa[ff + loc : big].T, fb[width : width + loc].T, fb[width + loc :].T])
    return (
        out,
        ig,
        tg,
        sm[5],
        sm[6],
        qkv_grad,
        jnp.stack([sm[7, :loc], sm[7, half : half + loc]]),
        fa[ff : ff + loc],
        sm[4],
        sm[2],
        sm[3],
        fb[:width],
        sm[1],
        fa[:ff],
        sm[0],
    )


def solution(mesh):
    placed = (
        P("dp", None),
        P("dp", None),
        P("dp", None),
        P(),
        P(),
        P(None, None, "mp"),
        P(None, "mp"),
        P("mp", None),
        P(),
        P(),
        P(),
        P(None, "mp"),
        P("mp"),
        P("mp", None),
        P(),
        P("dp", None),
    )
    return jax.shard_map(
        functools.partial(shards, mesh.shape["dp"]),
        mesh=mesh,
        in_specs=placed,
        out_specs=(
            P("dp", None),
            P("dp", None),
            P("dp", None),
            P(),
            P(),
            P(None, None, "mp"),
            P(None, "mp"),
            P("mp", None),
            P(),
            P(),
            P(),
            P(None, "mp"),
            P("mp"),
            P("mp", None),
            P(),
        ),
        check_vma=False,
    )
```

time: 789 us -> 228 us (0.29)
  waiting for transfers between devices: 586 us -> 0 us
  Pallas kernels: 0 us -> 202 us
  local copies, waits for them, and re-layouts: 125 us -> 23.2 us
  matrix products: 32.2 us -> 0 us
  other arithmetic: 24 us -> 1.91 us
  between operations: 15.9 us -> 0.68 us
    unnamed x7 -> x0, waiting for transfers between devices: 462 us -> none
    pallas_call x0 -> x1, Pallas kernels: none -> 202 us  [shards(): pl.pallas_call(functools.partial(kernel, n_dp, (UA, UB), tuple(scratch)),...]
    psum x3 -> x0, waiting for transfers between devices: 124 us -> none  [the longest x1 45.6 us: shards(): lax.psum(jnp.dot(mixed_low, out_weight, preferred_element_type=jnp.float3...]
    unnamed x155 -> x12, local copies, waits for them, and re-layouts: 87.6 us -> 4.76 us
    dot_general x20 -> x0, matrix products: 32.2 us -> none  [the longest x1 5.73 us: shards(): jnp.einsum('td,fd->tf', cotangent, down_weight, preferred_element_type=jn...]
    reduce_sum x12 -> x0, other arithmetic: 17.9 us -> none  [the longest x3 5.63 us: layer_norm(): return centred * lax.rsqrt(spread + 1e-05) * norm_gain + norm_shift]
    reshape x10 -> x7, local copies, waits for them, and re-layouts: 19.7 us -> 8.87 us  [shards(): row = lambda v: v.reshape(1, -1)]
  transfers between devices with their start and end apart: 5 -> 0, of which waited for: 5 -> 0; matrix products, arithmetic and copies ran while one was open for 5% -> 0% of each run, Pallas kernels for 0% -> 0%
where the time goes in v1:
time: 228 us
  Pallas kernels  202 us (89%)
  local copies, waits for them, and re-layouts  23.2 us (10%)
    pallas_call x1, Pallas kernels, shards(): pl.pallas_call(functools.partial(kernel, n_dp, (UA, UB), tuple(scratch)),...  202 us
    reshape x7, local copies, waits for them, and re-layouts, shards(): row = lambda v: v.reshape(1, -1)  8.87 us
    unnamed x12, local copies, waits for them, and re-layouts  4.76 us

profile of v1, /device:TPU:0, one launch (start us, length us, event | category | flops | bytes accessed | tf_op | source)
XLA Modules:
  0.0 227.7 jit_solution(2025583155030085296)
XLA Ops:
  0.6 1.3 reshape.51.refs_3_
  1.9 1.3 reshape.52.refs_4_
  3.2 1.3 reshape.53.refs_8_
  4.4 1.3 reshape.54.refs_9_
  5.7 1.3 reshape.55.refs_10_
  7.0 1.3 reshape.56.refs_12_
  8.2 1.3 reshape.57.refs_14_
  9.5 2.3 %copy.31.refs_5_ = bf16[3,768,192]{2,1,0:T(8,128)(2,1)} copy(bf16[3,768,192]{1,2,0:T(8,128)(2,1)} %param.21) | data formatting | bytes 1769472 | tf_op args[5]
  11.8 201.9 %shard_map.271 = (bf16[512,768]{1,0:T(8,128)(2,1)}, bf16[512,768]{1,0:T(8,128)(2,1)}, f32[4,768]{1,0:T(4,128)}, f32[1184,768]{1,0:T(8,128)}, f32[1152,768]{1,0:T(8,128)}) custom-call(bf16[512,768]{1,0:T(8,128)(2,1)} %refs_0_.1, bf16[4,768]{1,0:T(4,128)(2,1)} %refs_1_.1, s32[4,128]{1,0:T(4,128)} %refs_2_.1, f32[1,768]{1,0:T(1,128)} %reshape.51.refs_3_, ...), custom_call_target="tpu_custom_call" | custom-call | flops 6000000000 | bytes 20000000 | tf_op jit(solution)/shard_map/pallas_call | solution.py:553
  213.8 0.7 fusion.1
  214.5 0.6 pad_maximum_fusion.1
  215.1 1.7 slice_reduce_fusion
  216.7 1.3 slice_bitcast_fusion.1
  218.1 0.0 copy-start
  218.1 3.4 %slice.66 = f32[768,768]{1,0:T(8,128)} slice(f32[1152,768]{1,0:T(8,128)} %get-tuple-element.24), slice={[0:768], [0:768]} | slice | bytes 4718592 | tf_op jit(solution)/shard_map/slice | solution.py:587
  221.5 0.0 copy-done
  221.5 0.9 fusion
  222.3 1.6 slice.68
  223.9 1.3 pad_maximum_fusion
  225.2 0.1 copy-done.2
  225.3 0.9 copy.35
  226.2 0.9 copy.36
  227.1 0.0 copy-done.3
  227.1 0.6 copy.37
  (4 shorter events, 0.0 us)
Async XLA Ops:
  218.1 3.4 %copy-start = (f32[1184,768]{1,0:T(8,128)S(1)}, f32[1184,768]{1,0:T(8,128)}, u32[]{:S(2)}) copy-start(f32[1184,768]{1,0:T(8,128)} %get-tuple-element.23) | copy-start | bytes 10911748
  223.9 1.4 copy-start.2
  223.9 2.3 copy-start.1
  225.3 1.8 copy-start.3

commit v2 on v1

--- a/solution.py
+++ b/solution.py
@@ -10,6 +10,7 @@
 HD = 64
 SUB = 32
 CH = 8
+SENDS = 3
 MESH = pl.DeviceIdType.MESH
 F32 = jnp.float32
 BF16 = jnp.bfloat16
@@ -43,9 +44,11 @@
 
 
 def kernel(n_dp, units, names, *refs):
-    (tok, tim, seg, n1g, n1b, wqkv, qvb, wout, outb, n2g, n2b, wup, upb, wdn, dnb, cot) = refs[:16]
+    (tok, tim, seg, _, _, wqkv, qvb, wout, _, _, _, wup, _, wdn, _, cot) = refs[:16]
     out, ig, tg, fa_out, fb_out = refs[16:21]
     R = dict(zip(names, refs[21:]))
+    flat = [refs[i] for i in (3, 4, 8, 9, 10, 12, 14)]
+    n1g, n1b, outb, n2g, n2b, upb, dnb = (R["vecs"].at[pl.ds(i, 1)] for i in range(7))
     timf, start, entry, q_s, k_s, v_s = (R[s] for s in ("timf", "start", "entry", "q", "k", "v"))
     probs, mixed_s, part, cr, ys, yr = (R[s] for s in ("probs", "mixed", "part", "cr", "ys", "yr"))
     tot, mid, e2, hp, act, gp = (R[s] for s in ("tot", "mid", "e2", "hp", "act", "gp"))
@@ -94,16 +97,13 @@
         )
 
     def core_copy(p, r):
-        i = p * rows_n + r
-        return remote(part.at[sl(r), other], cr.at[sl(r)], R["cs"].at[i], R["crs"].at[i], to_core)
+        return remote(part.at[sl(r), other], cr.at[sl(r)], R["cs"].at[r], R["crs"].at[r], to_core)
 
     def y_copy(p, r):
-        i = p * rows_n + r
-        return remote(ys.at[sl(r)], yr.at[p % 2, sl(r)], R["yss"].at[i], R["yrs"].at[i], to_y)
+        return remote(ys.at[sl(r)], yr.at[p % 2, sl(r)], R["yss"].at[r], R["yrs"].at[p % 2, r], to_y)
 
     def ag_copy(p, r):
-        i = p * rows_n + r
-        return remote(tot.at[sl(r), mine], tot.at[sl(r), mine], R["gs"].at[i], R["grs"].at[i], to_core)
+        return remote(tot.at[sl(r), mine], tot.at[sl(r), mine], R["gs"].at[r], R["grs"].at[r], to_core)
 
     def sum_b(p, r):
         core_copy(p, r).wait()
@@ -149,9 +149,9 @@
 
     def project(r):
         e = entry[sl(r), :]
-        q_s[sl(r), :] = (nn(e, wqkv[0]) + qvb[0:1, :]).astype(BF16)
-        k_s[sl(r), :] = nn(e, wqkv[1]).astype(BF16)
-        v_s[sl(r), :] = (nn(e, wqkv[2]) + qvb[1:2, :]).astype(BF16)
+        q_s[sl(r), :] = (nt(e, wqkv[0]) + qvb[0:1, :]).astype(BF16)
+        k_s[sl(r), :] = nt(e, wqkv[1]).astype(BF16)
+        v_s[sl(r), :] = (nt(e, wqkv[2]) + qvb[1:2, :]).astype(BF16)
 
     def attend(r):
         labels = jnp.broadcast_to(seg[pl.ds(r, 1), :], (seq, seq))
@@ -225,7 +225,7 @@
         gq = (from_heads(nn(ds, k_s[sl(r), :])) * HD ** (-0.5)).astype(BF16)
         gk = (tn(ds, by_head(q_s[sl(r), :])) * HD ** (-0.5)).astype(BF16)
         gv = tn(pr.astype(BF16), g3).astype(BF16)
-        part[sl(r), :] = nt(gq, wqkv[0]) + nt(gk, wqkv[1]) + nt(gv, wqkv[2])
+        part[sl(r), :] = nn(gq, wqkv[0]) + nn(gk, wqkv[1]) + nn(gv, wqkv[2])
         core_copy(2, r).start()
         lta[ff + loc : ff + 2 * loc, sl(r)] = gq.T
         ltb[width : width + loc, sl(r)] = gk.T
@@ -290,18 +290,28 @@
     def a_own(u, d):
         return pl.ds(pl.multiple_of(u * 4 * CH + x * 2 * CH + d * CH, CH), CH)
 
+    W = R["xr"].shape[0]
+
     def a_slot(u):
-        return pl.ds(pl.multiple_of(u * CH, CH), CH)
+        return pl.ds(pl.multiple_of(u % W * CH, CH), CH)
 
     def b_own(u, d):
         return pl.ds(pl.multiple_of(u * 4 * CH + d * 2 * CH, CH), 2 * CH)
 
     def b_slot(u):
-        return pl.ds(pl.multiple_of(u * 2 * CH, CH), 2 * CH)
+        return pl.ds(pl.multiple_of(u % W * 2 * CH, CH), 2 * CH)
+
+    def go(copy, u):
+        when(u >= SENDS, lambda: copy(u - SENDS).wait_send())
+        copy(u).start()
+
+    def end(copy, n):
+        for u in range(n - min(SENDS, n), n):
+            copy(u).wait_send()
 
     def x_first(u):
         src = pl.ds(pl.multiple_of(u * 4 * CH + (1 - x) * 2 * CH, CH), 2 * CH)
-        return remote(ga.at[src], R["xrb"].at[b_slot(u)], R["xs"].at[u], R["xr"].at[u], to_x)
+        return remote(ga.at[src], R["xrb"].at[b_slot(u)], R["xs"].at[u % SENDS], R["xr"].at[u % W], to_x)
 
     ways = []
     for d in (0, 1):
@@ -313,41 +323,43 @@
     def streams(kind, d, up, dn):
         if kind == "a":
             g, f, lo, hi, own, slot = ga, fa, R["arl"], R["arh"], a_own, a_slot
-            s, lr, hr, bu, bd, br = (R[t] for t in ("ars", "arlr", "arhr", "abu", "abd", "abr"))
+            s, rr, bu, bd, br = (R[t] for t in ("ars", "arr", "abu", "abd", "abr"))
         else:
             g, f, lo, hi, own, slot = gb, fb, R["brl"], R["brh"], b_own, b_slot
-            s, lr, hr, bu, bd, br = (R[t] for t in ("brs", "brlr", "brhr", "bbu", "bbd", "bbr"))
+            s, rr, bu, bd, br = (R[t] for t in ("brs", "brr", "bbu", "bbd", "bbr"))
 
         def send_up(u):
-            return remote(g.at[own(u, d)], lo.at[d, slot(u)], s.at[d, u], lr.at[d, u], up)
+            return remote(g.at[own(u, d)], lo.at[d, slot(u)], s.at[d, u % SENDS], rr.at[d, u % W], up)
+
+        def send_up_root(u):
+            return remote(g.at[own(u, d)], lo.at[d, slot(u)], s.at[d, u % SENDS], br.at[d, u % W], up)
 
         def send_dn(u):
-            return remote(g.at[own(u, d)], hi.at[d, slot(u)], s.at[d, u], hr.at[d, u], dn)
+            return remote(g.at[own(u, d)], hi.at[d, slot(u)], s.at[d, u % SENDS], rr.at[d, u % W], dn)
 
         def bcast_up(u):
-            return remote(f.at[own(u, d)], f.at[own(u, d)], bu.at[d, u], br.at[d, u], up)
+            return remote(f.at[own(u, d)], f.at[own(u, d)], bu.at[d, u % SENDS], br.at[d, u % W], up)
 
         def bcast_dn(u):
-            return remote(f.at[own(u, d)], f.at[own(u, d)], bd.at[d, u], br.at[d, u], dn)
-
-        return g, f, lo, hi, own, slot, send_up, send_dn, bcast_up, bcast_dn
+            return remote(f.at[own(u, d)], f.at[own(u, d)], bd.at[d, u % SENDS], br.at[d, u % W], dn)
+
+        return g, f, lo, hi, own, slot, send_up, send_up_root, send_dn, bcast_up, bcast_dn
 
     def x_last(u, d):
         s = a_own(u, d)
-        return remote(fa.at[s], fa.at[s], R["xgs"].at[d, u], R["xgr"].at[d, u], to_x)
-
-    def x_last_in(u, d):
-        s = pl.ds(pl.multiple_of(u * 4 * CH + (1 - x) * 2 * CH + d * CH, CH), CH)
-        return remote(fa.at[s], fa.at[s], R["xgs"].at[d, u], R["xgr"].at[d, u], to_x)
+        return remote(fa.at[s], fa.at[s], R["xgs"].at[d, u % SENDS], R["xgr"].at[d, u % W], to_x)
 
     def b_x(u, d):
-        return remote(gb.at[b_own(u, d)], R["bxb"].at[d, b_slot(u)], R["bxs"].at[d, u], R["bxr"].at[d, u], to_x)
+        return remote(
+            gb.at[b_own(u, d)], R["bxb"].at[d, b_slot(u)], R["bxs"].at[d, u % SENDS], R["bxr"].at[d, u % W], to_x
+        )
 
     def reduce_step(kind, d, w, up, dn, u):
-        g, f, lo, hi, own, slot, send_up, send_dn, bcast_up, bcast_dn = streams(kind, d, up, dn)
+        g, f, lo, hi, own, slot, send_up, send_up_root, send_dn, bcast_up, bcast_dn = streams(kind, d, up, dn)
 
         def from_low():
-            send_up(u).wait_recv()
+            when(w < root, lambda: send_up(u).wait_recv())
+            when(w == root, lambda: send_up_root(u).wait_recv())
             g[own(u, d), :] += lo[d, slot(u), :]
 
         def from_high():
@@ -356,31 +368,32 @@
 
         when((w > 0) & (w <= root), from_low)
         when((w < L - 1) & (w >= root), from_high)
-        when(w < root, lambda: send_up(u).start())
-        when(w > root, lambda: send_dn(u).start())
+        when(w < root - 1, lambda: go(send_up, u))
+        when(w == root - 1, lambda: go(send_up_root, u))
+        when(w > root, lambda: go(send_dn, u))
 
     def root_step(kind, d, w, up, dn, u):
-        g, f, lo, hi, own, slot, send_up, send_dn, bcast_up, bcast_dn = streams(kind, d, up, dn)
+        g, f, lo, hi, own, slot, send_up, send_up_root, send_dn, bcast_up, bcast_dn = streams(kind, d, up, dn)
         if kind == "a":
             f[own(u, d), :] = g[own(u, d), :]
         else:
             b_x(u, d).wait_recv()
             f[own(u, d), :] = g[own(u, d), :] + R["bxb"][d, slot(u), :]
-        bcast_up(u).start()
-        when(w > 0, lambda: bcast_dn(u).start())
+        go(bcast_up, u)
+        when(w > 0, lambda: go(bcast_dn, u))
         if kind == "a":
-            x_last(u, d).start()
+            go(lambda i: x_last(i, d), u)
 
     def spread_step(kind, d, w, up, dn, u):
-        g, f, lo, hi, own, slot, send_up, send_dn, bcast_up, bcast_dn = streams(kind, d, up, dn)
+        g, f, lo, hi, own, slot, send_up, send_up_root, send_dn, bcast_up, bcast_dn = streams(kind, d, up, dn)
         bcast_up(u).wait_recv()
-        when((w > root) & (w < L - 1), lambda: bcast_up(u).start())
-        when((w < root) & (w > 0), lambda: bcast_dn(u).start())
+        when((w > root) & (w < L - 1), lambda: go(bcast_up, u))
+        when((w < root) & (w > 0), lambda: go(bcast_dn, u))
         if kind == "a":
-            x_last(u, d).start()
+            go(lambda i: x_last(i, d), u)
 
     def dp_tick(t):
-        when(t < UA, lambda: x_first(t).start())
+        when(t < UA, lambda: go(x_first, t))
 
         def x_add():
             u = t - 1
@@ -396,32 +409,32 @@
                 u = t - first - far
                 when(ok(u, n), functools.partial(reduce_step, kind, d, w, up, dn, u))
                 if kind == "b":
-                    when(ok(u, n) & (w == root), lambda u=u, d=d: b_x(u, d).start())
+                    when(ok(u, n) & (w == root), lambda u=u, d=d: go(lambda i: b_x(i, d), u))
                 v = t - first - D - gap
                 when(ok(v, n) & (w == root), functools.partial(root_step, kind, d, w, up, dn, v))
-                v = t - first - D - gap - dist
+                v = v - dist
                 when(ok(v, n) & (w != root), functools.partial(spread_step, kind, d, w, up, dn, v))
+                if kind == "a":
+                    v = v - 1
+                    when(ok(v, n), lambda v=v, d=d: x_last(v, d).wait_recv())
 
     def dp_drain():
-        @pl.loop(0, UA)
-        def _(u):
-            x_first(u).wait_send()
+        end(x_first, UA)
+        for kind, n in (("a", UA), ("b", UB)):
             for d, w, up, dn in ways:
-                x_last(u, d).wait_send()
-                x_last_in(u, d).wait_recv()
-
-        for kind, n in (("a", UA), ("b", UB)):
-
-            @pl.loop(0, n)
-            def _(u):
-                for d, w, up, dn in ways:
-                    fs = streams(kind, d, up, dn)
-                    when(w != root, lambda: fs[6](u).wait_send())
-                    when((w >= root) & (w < L - 1), lambda: fs[8](u).wait_send())
-                    when((w <= root) & (w > 0), lambda: fs[9](u).wait_send())
-                    if kind == "b":
-                        when(w == root, lambda: b_x(u, d).wait_send())
-
+                fs = streams(kind, d, up, dn)
+                when(w < root - 1, lambda: end(fs[6], n))
+                when(w == root - 1, lambda: end(fs[7], n))
+                when(w > root, lambda: end(fs[8], n))
+                when((w >= root) & (w < L - 1), lambda: end(fs[9], n))
+                when((w <= root) & (w > 0), lambda: end(fs[10], n))
+                if kind == "a":
+                    end(lambda i: x_last(i, d), n)
+                else:
+                    when(w == root, lambda: end(lambda i: b_x(i, d), n))
+
+    for i, ref in enumerate(flat):
+        R["vecs"][i : i + 1, :] = ref[...][None, :]
     timf[...] = tim[...].astype(F32)
     ga[small : small + 4 * CH, :] = jnp.zeros((4 * CH, width), F32)
     pl.loop(0, rows_n)(norm1)
@@ -445,7 +458,7 @@
 
     weight_grads(0)
 
-    ticks = max(UA, UB) + 2 * D + 1
+    ticks = max(UA, UB) + 2 * D + 2
     per = blk // (4 * CH)
     blocks = (ff + 2 * loc) // blk
 
@@ -506,8 +519,9 @@
     UA = UB + 1
     vm = pltpu.VMEM
     dma = pltpu.SemaphoreType.DMA
-    dp_sem = lambda n: dma((2, n))
+    W = n_dp // 2 + 4
     scratch = dict(
+        vecs=vm((8, width), F32),
         timf=vm((rows_n, width), F32),
         start=vm((tokens, width), F32),
         entry=vm((tokens, width), BF16),
@@ -535,19 +549,20 @@
         gb=vm((UB * 4 * CH, width), F32),
         fa=vm((UA * 4 * CH, width), F32),
         fb=vm((UB * 4 * CH, width), F32),
-        xrb=vm((UA * 2 * CH, width), F32),
-        arl=vm((2, UA * CH, width), F32),
-        arh=vm((2, UA * CH, width), F32),
-        brl=vm((2, UB * 2 * CH, width), F32),
-        brh=vm((2, UB * 2 * CH, width), F32),
-        bxb=vm((2, UB * 2 * CH, width), F32),
-        **{s: dma((4 * rows_n,)) for s in ("cs", "crs", "yss", "yrs", "gs", "grs")},
+        xrb=vm((W * 2 * CH, width), F32),
+        arl=vm((2, W * CH, width), F32),
+        arh=vm((2, W * CH, width), F32),
+        brl=vm((2, W * 2 * CH, width), F32),
+        brh=vm((2, W * 2 * CH, width), F32),
+        bxb=vm((2, W * 2 * CH, width), F32),
+        **{s: dma((rows_n,)) for s in ("cs", "crs", "yss", "gs", "grs")},
+        yrs=dma((2, rows_n)),
         fin=dma((2,)),
-        **{s: dma((UA,)) for s in ("xs", "xr")},
-        **{s: dp_sem(UA) for s in ("ars", "arlr", "arhr", "abu", "abd", "abr", "xgs", "xgr")},
-        **{s: dp_sem(UB) for s in ("brs", "brlr", "brhr", "bxs", "bxr", "bbu", "bbd", "bbr")},
+        xs=dma((SENDS,)),
+        xr=dma((W,)),
+        **{s: dma((2, SENDS)) for s in ("ars", "abu", "abd", "xgs", "brs", "bxs", "bbu", "bbd")},
+        **{s: dma((2, W)) for s in ("arr", "abr", "xgr", "brr", "bxr", "bbr")},
     )
-    row = lambda v: v.reshape(1, -1)
     any_spec = pl.BlockSpec(memory_space=pl.ANY)
     vm_spec = pl.BlockSpec(memory_space=pltpu.VMEM)
     out, ig, tg, fa, fb = pl.pallas_call(
@@ -567,28 +582,73 @@
         ),
         cost_estimate=pl.CostEstimate(flops=6 * 10**9, bytes_accessed=20 * 10**6, transcendentals=0),
     )(
-        tok, tim, seg, row(n1g), row(n1b), wqkv, qvb, wout, row(outb), row(n2g), row(n2b), wup, row(upb), wdn,
-        row(dnb), cot,
+        tok, tim, seg, n1g, n1b, wqkv.transpose(0, 2, 1), qvb, wout, outb, n2g, n2b, wup, upb, wdn, dnb, cot
     )
-    sm = fa[big : big + 8]
-    qkv_grad = jnp.stack([fa[ff + loc : big].T, fb[width : width + loc].T, fb[width + loc :].T])
-    return (
-        out,
-        ig,
-        tg,
-        sm[5],
-        sm[6],
-        qkv_grad,
-        jnp.stack([sm[7, :loc], sm[7, half : half + loc]]),
-        fa[ff : ff + loc],
-        sm[4],
-        sm[2],
-        sm[3],
-        fb[:width],
-        sm[1],
-        fa[:ff],
-        sm[0],
+    f32 = lambda *shape: jax.ShapeDtypeStruct(shape, F32)
+    moved = (
+        jax.ShapeDtypeStruct((tokens, width), BF16),
+        jax.ShapeDtypeStruct((tokens, width), BF16),
+        f32(rows_n, width),
+        f32(3, loc, width),
+        f32(loc, width),
+        f32(width, ff),
+        f32(ff, width),
     )
+    results = pl.pallas_call(
+        functools.partial(place, big),
+        out_shape=moved + (f32(2, loc), f32(ff)) + (f32(width),) * 6,
+        in_specs=[any_spec] * 5,
+        out_specs=(any_spec,) * 7 + (vm_spec,) * 8,
+        scratch_shapes=[
+            vm((8, width), F32),
+            vm((big, width), F32),
+            vm((big, width), F32),
+            vm((tokens, width), BF16),
+            vm((tokens, width), BF16),
+            vm((rows_n, width), F32),
+            dma((10,)),
+            dma((10,)),
+        ],
+        compiler_params=pltpu.CompilerParams(vmem_limit_bytes=63 * 2**20),
+    )(out, ig, tg, fa, fb)
+    out, ig, tg, qkv, outw, up, down, qvb, upb, downb, n2g, n2b, outb, n1g, n1b = results
+    return out, ig, tg, n1g, n1b, qkv.transpose(0, 2, 1), qvb, outw, outb, n2g, n2b, up, upb, down, downb
+
+
+def place(big, *refs):
+    out, ig, tg, fa, fb, out_o, ig_o, tg_o, qkv, outw, up, down, qvb, upb, downb = refs[:15]
+    n2g, n2b, outb, n1g, n1b, sm, va, vb, vo, vi, vt, sem, sem_o = refs[15:]
+    loc, ff = outw.shape[0], down.shape[0]
+    half = fa.shape[1] // 2
+    width = up.shape[0]
+    rows = [pl.ds(0, ff), pl.ds(ff, loc), pl.ds(ff + loc, loc)]
+    moves = [
+        (fa.at[rows[0]], va.at[rows[0]], down),
+        (fb.at[rows[0]], vb.at[rows[0]], up),
+        (fa.at[rows[1]], va.at[rows[1]], outw),
+        (fa.at[rows[2]], va.at[rows[2]], qkv.at[0]),
+        (fb.at[rows[1]], vb.at[rows[1]], qkv.at[1]),
+        (fb.at[rows[2]], vb.at[rows[2]], qkv.at[2]),
+        (out, vo, out_o),
+        (ig, vi, ig_o),
+        (tg, vt, tg_o),
+    ]
+    first = pltpu.make_async_copy(fa.at[pl.ds(big, 8)], sm, sem.at[9])
+    first.start()
+    loads = [pltpu.make_async_copy(a, v, sem.at[i]) for i, (a, v, b) in enumerate(moves)]
+    stores = [pltpu.make_async_copy(v, b, sem_o.at[i]) for i, (a, v, b) in enumerate(moves)]
+    for copy in loads:
+        copy.start()
+    for load, store in zip(loads, stores):
+        load.wait()
+        store.start()
+    first.wait()
+    for i, ref in enumerate((downb, upb, n2g, n2b, outb, n1g, n1b)):
+        ref[...] = sm[i : i + 1, :].reshape(ref.shape)
+    qvb[0:1, :] = sm[7:8, 0:loc]
+    qvb[1:2, :] = sm[7:8, half : half + loc]
+    for copy in stores:
+        copy.wait()
 
 
 def solution(mesh):

time: 228 us -> 199 us (0.87)
  local copies, waits for them, and re-layouts: 23.2 us -> 0 us
  Pallas kernels: 202 us -> 198 us
    pallas_call x1, Pallas kernels: 202 us -> 191 us  [shards(): pl.pallas_call(functools.partial(kernel, n_dp, (UA, UB), tuple(scratch)),...]
    reshape x7 -> x0, local copies, waits for them, and re-layouts: 8.87 us -> none  [shards(): row = lambda v: v.reshape(1, -1)]
    slice x5 -> x0, local copies, waits for them, and re-layouts: 8.21 us -> none  [the longest x1 3.37 us: shards(): fb[:width]]
    pallas_call x0 -> x1, Pallas kernels: none -> 7.27 us  [shards(): pl.pallas_call(functools.partial(place, big), out_shape=moved + (f32(2, l...]
    unnamed x12 -> x0, local copies, waits for them, and re-layouts: 4.76 us -> none
where the time goes in v2:
time: 199 us
  Pallas kernels  198 us (99%)
    pallas_call x1, Pallas kernels, shards(): pl.pallas_call(functools.partial(kernel, n_dp, (UA, UB), tuple(scratch)),...  191 us
    pallas_call x1, Pallas kernels, shards(): pl.pallas_call(functools.partial(place, big), out_shape=moved + (f32(2, l...  7.27 us

profile of v2, /device:TPU:0, one launch (start us, length us, event | category | flops | bytes accessed | tf_op | source)
XLA Modules:
  0.0 199.1 jit_solution(15510003471769582552)
XLA Ops:
  0.7 191.2 %shard_map.271 = (bf16[512,768]{1,0:T(8,128)(2,1)}, bf16[512,768]{1,0:T(8,128)(2,1)}, f32[4,768]{1,0:T(4,128)}, f32[1184,768]{1,0:T(8,128)}, f32[1152,768]{1,0:T(8,128)}) custom-call(bf16[512,768]{1,0:T(8,128)(2,1)} %refs_0_.1, bf16[4,768]{1,0:T(4,128)(2,1)} %refs_1_.1, s32[4,128]{1,0:T(4,128)} %refs_2_.1, f32[768]{0:T(1024)} %refs_3_.1, f32[768]{0:T(1024)} %refs_4_.1, ...), custom_call_target="tpu_custom_call" | custom-call | flops 6000000000 | bytes 20000000 | tf_op jit(solution)/shard_map/pallas_call | solution.py:568
  191.9 7.3 %shard_map.272 = (bf16[512,768]{1,0:T(8,128)(2,1)}, bf16[512,768]{1,0:T(8,128)(2,1)}, f32[4,768]{1,0:T(4,128)}, f32[3,192,768]{2,1,0:T(8,128)}, f32[192,768]{1,0...) custom-call(bf16[512,768]{1,0:T(8,128)(2,1)} %get-tuple-element.35.r, ...), custom_call_target="tpu_custom_call" | custom-call | tf_op jit(solution)/shard_map/pallas_call | solution.py:597

commit v3 on v2

v3 whole, which is shorter than its diff:
```python
import functools

import jax
import jax.numpy as jnp
from jax import lax
from jax.experimental import pallas as pl
from jax.experimental.pallas import tpu as pltpu
from jax.sharding import PartitionSpec as P

HD = 64
SUB = 32
CH = 8
SENDS = 4
MESH = pl.DeviceIdType.MESH
F32 = jnp.float32
BF16 = jnp.bfloat16


ARGS = ("tok", "tim", "seg", "n1g", "n1b", "wqkv", "qvb", "wout", "outb", "n2g", "n2b")
ARGS += ("wup", "upb", "wdn", "dnb", "cot")


def hop_ticks(line):
    return 2 if line <= 8 else 1


def when(cond, fn):
    pl.when(cond)(fn)


def nt(a, b):
    return lax.dot_general(a, b, (((1,), (1,)), ((), ())), preferred_element_type=F32)


def tn(a, b):
    return lax.dot_general(a, b, (((0,), (0,)), ((), ())), preferred_element_type=F32)


def nn(a, b):
    return jnp.dot(a, b, preferred_element_type=F32)


def normed(v):
    centred = v - jnp.mean(v, -1, keepdims=True)
    spread = jnp.mean(centred * centred, -1, keepdims=True)
    scale = lax.rsqrt(spread + 1e-05)
    return centred * scale, scale


def colsum(v):
    return jnp.sum(v, 0, keepdims=True)


def kernel(n_dp, units, names, *refs):
    out, ig, tg, f_out = refs[16:20]
    R = dict(zip(names, refs[20:]))
    order = ("tok", "tim", "n1g", "n1b", "wqkv", "qvb", "seg", "wout", "outb", "cot", "wdn")
    order += ("n2g", "n2b", "wup", "upb", "dnb")
    tok, tim, wqkv, qvb, seg, wout, cot, wdn, wup = (
        R[s] for s in ("tok", "tim", "wqkv", "qvb", "seg", "wout", "cot", "wdn", "wup")
    )
    loads = {
        name: pltpu.make_async_copy(refs[ARGS.index(name)], R[name], R["ins"].at[i]) for i, name in enumerate(order)
    }
    n1g, n1b, outb, n2g, n2b, upb, dnb = (R["vecs"].at[pl.ds(i, 1)] for i in range(7))
    timf, start, entry, q_s, k_s, v_s = (R[s] for s in ("timf", "start", "entry", "q", "k", "v"))
    probs, mixed_s, part, cr, ys, yr = (R[s] for s in ("probs", "mixed", "part", "cr", "ys", "yr"))
    tot, mid, e2, hp, act, gp = (R[s] for s in ("tot", "mid", "e2", "hp", "act", "gp"))
    gact, gmid, gbr, lt, g, f = (R[s] for s in ("gact", "gmid", "gbr", "lt", "g", "f"))

    rows_n, seq = seg.shape
    width = tok.shape[1]
    half = width // 2
    loc = wout.shape[0]
    heads = loc // HD
    ff = wup.shape[1]
    UA, UB = units
    L = n_dp // 2
    LAG = hop_ticks(L)
    D = L // 2
    root = D - 1
    dp = lax.axis_index("dp")
    mp = lax.axis_index("mp")
    core = mp % 2
    x = dp % 2
    z = dp // 2
    to_core = (dp, mp + 1 - 2 * core)
    to_y = (dp, (mp + 2) % 4)
    to_x = (dp + 1 - 2 * x, mp)
    zlo = jnp.maximum(z - 1, 0) * 2 + x
    zhi = jnp.minimum(z + 1, L - 1) * 2 + x

    barrier = pltpu.get_barrier_semaphore()
    for dev in (to_core, to_y, to_x):
        pl.semaphore_signal(barrier, 1, device_id=dev, device_id_type=MESH)
    when(z > 0, lambda: pl.semaphore_signal(barrier, 1, device_id=(zlo, mp), device_id_type=MESH))
    when(z < L - 1, lambda: pl.semaphore_signal(barrier, 1, device_id=(zhi, mp), device_id_type=MESH))

    def sl(r, n=seq):
        return pl.ds(pl.multiple_of(r * n, n), n)

    def sub(r, i):
        return pl.ds(pl.multiple_of(r * seq + i * SUB, SUB), SUB)

    mine = pl.ds(pl.multiple_of(core * half, 128), half)
    other = pl.ds(pl.multiple_of((1 - core) * half, 128), half)

    def remote(src, dst, ssem, rsem, dev):
        return pltpu.make_async_remote_copy(
            src_ref=src, dst_ref=dst, send_sem=ssem, recv_sem=rsem, device_id=dev, device_id_type=MESH
        )

    def core_copy(p, r):
        return remote(part.at[sl(r), other], cr.at[sl(r)], R["cs"].at[r], R["crs"].at[r], to_core)

    def y_copy(p, r):
        return remote(ys.at[sl(r)], yr.at[p % 2, sl(r)], R["yss"].at[r], R["yrs"].at[p % 2, r], to_y)

    def ag_copy(p, r):
        return remote(tot.at[sl(r), mine], tot.at[sl(r), mine], R["gs"].at[r], R["grs"].at[r], to_core)

    def sum_b(p, r):
        core_copy(p, r).wait()
        ys[sl(r), :] = part[sl(r), mine] + cr[sl(r), :]
        y_copy(p, r).start()

    def sum_c(p, r):
        y_copy(p, r).wait()
        tot[sl(r), mine] = ys[sl(r), :] + yr[p % 2, sl(r), :]
        ag_copy(p, r).start()

    def sum_d(p, r):
        ag_copy(p, r).wait()

    def vec(ref):
        return ref[...]

    small = 2 * ff + 4 * loc

    def small_add(i, v):
        g[small + i : small + i + 1, :] += v

    lane = lax.broadcasted_iota(jnp.int32, (1, loc), 1)
    masks = [((lane >= h * HD) & (lane < (h + 1) * HD)).astype(F32) for h in range(heads)]

    def by_head(v):
        return jnp.concatenate([v * m.astype(BF16) for m in masks], 0)

    def from_heads(v):
        total = v[:seq] * masks[0]
        for h in range(1, heads):
            total = total + v[h * seq : (h + 1) * seq] * masks[h]
        return total

    def norm1(r):
        @pl.loop(0, seq // SUB)
        def _(i):
            s = sub(r, i)
            v = tok[s, :].astype(F32) + timf[pl.ds(r, 1), :]
            start[s, :] = v
            xhat, _ = normed(v)
            entry[s, :] = (xhat * n1g[...] + n1b[...]).astype(BF16)

    def project(r):
        e = entry[sl(r), :]
        q_s[sl(r), :] = (nt(e, wqkv[0]) + qvb[0:1, :]).astype(BF16)
        k_s[sl(r), :] = nt(e, wqkv[1]).astype(BF16)
        v_s[sl(r), :] = (nt(e, wqkv[2]) + qvb[1:2, :]).astype(BF16)

    def attend(r):
        labels = jnp.broadcast_to(seg[pl.ds(r, 1), :], (seq, seq))
        same = labels == labels.T
        same = jnp.concatenate([same.astype(F32)] * heads, 0) > 0.5
        scores = nt(by_head(q_s[sl(r), :]), k_s[sl(r), :]) * HD ** (-0.5)
        scores = jnp.where(same, scores, -1e30)
        w = jnp.exp(scores - jnp.max(scores, -1, keepdims=True))
        pr = w / jnp.sum(w, -1, keepdims=True)
        probs[sl(r, heads * seq), :] = pr
        mixed = from_heads(nn(pr.astype(BF16), v_s[sl(r), :])).astype(BF16)
        mixed_s[sl(r), :] = mixed
        part[sl(r), :] = nn(mixed, wout[...])

        @pl.when(r == 0)
        def _():
            pl.semaphore_wait(barrier, 3 + jnp.minimum(z, 1) + jnp.minimum(L - 1 - z, 1))

        core_copy(0, r).start()
        lt[2 * ff : 2 * ff + loc, sl(r)] = mixed.T

    def grad_act(r):
        c = cot[sl(r), :]
        gact[sl(r), :] = nt(c, wdn[...])
        small_add(0, colsum(c.astype(F32)))

    def feed(r):
        @pl.loop(0, seq // SUB)
        def _(i):
            s = sub(r, i)
            v = start[s, :] + (tot[s, :] + outb[...])
            mid[s, :] = v
            xhat, _ = normed(v)
            e2[s, :] = (xhat * n2g[...] + n2b[...]).astype(BF16)

        hp[...] = nn(e2[sl(r), :], wup[...])

        @pl.loop(0, seq // SUB)
        def _(i):
            s = sub(r, i)
            u = hp[pl.ds(pl.multiple_of(i * SUB, SUB), SUB), :] + upb[...]
            cdf = 0.5 * (1.0 + lax.erf(u * 0.7071067811865476))
            act[s, :] = (u * cdf).astype(BF16)
            slope = cdf + u * (0.3989422804014327 * jnp.exp(-0.5 * u * u))
            pre = (gact[s, :] * slope).astype(BF16)
            gp[s, :] = pre
            small_add(1, colsum(pre.astype(F32)))

        part[sl(r), :] = nt(gp[sl(r), :], wup[...])
        core_copy(1, r).start()
        lt[0:ff, sl(r)] = act[sl(r), :].T
        lt[ff : 2 * ff, sl(r)] = e2[sl(r), :].T

    def back2(r):
        @pl.loop(0, seq // SUB)
        def _(i):
            s = sub(r, i)
            ge = tot[s, :]
            xhat, scale = normed(mid[s, :])
            small_add(2, colsum(ge * xhat))
            small_add(3, colsum(ge))
            gx = ge * n2g[...]
            gm = cot[s, :].astype(F32) + scale * (
                gx - jnp.mean(gx, -1, keepdims=True) - xhat * jnp.mean(gx * xhat, -1, keepdims=True)
            )
            gmid[s, :] = gm
            low = gm.astype(BF16)
            gbr[s, :] = low
            small_add(4, colsum(low.astype(F32)))

        g3 = by_head(nt(gbr[sl(r), :], wout[...]).astype(BF16))
        pr = probs[sl(r, heads * seq), :]
        grad_probs = nt(g3, v_s[sl(r), :])
        inner = jnp.sum(pr * grad_probs, -1, keepdims=True)
        ds = (pr * (grad_probs - inner)).astype(BF16)
        gq = (from_heads(nn(ds, k_s[sl(r), :])) * HD ** (-0.5)).astype(BF16)
        gk = (tn(ds, by_head(q_s[sl(r), :])) * HD ** (-0.5)).astype(BF16)
        gv = tn(pr.astype(BF16), g3).astype(BF16)
        part[sl(r), :] = nn(gq, wqkv[0]) + nn(gk, wqkv[1]) + nn(gv, wqkv[2])
        core_copy(2, r).start()
        late = 2 * ff + loc
        for i, v in enumerate((gq, gk, gv)):
            lt[late + i * loc : late + (i + 1) * loc, sl(r)] = v.T
        g[small + 7 : small + 8, 0:loc] += colsum(gq.astype(F32))
        g[small + 7 : small + 8, half : half + loc] += colsum(gv.astype(F32))

    def back1(r):
        tg[pl.ds(r, 1), :] = jnp.zeros((1, width), F32)

        @pl.loop(0, seq // SUB)
        def _(i):
            s = sub(r, i)
            ge = tot[s, :]
            xhat, scale = normed(start[s, :])
            small_add(5, colsum(ge * xhat))
            small_add(6, colsum(ge))
            gy = ge * n1g[...]
            gs = gmid[s, :] + scale * (
                gy - jnp.mean(gy, -1, keepdims=True) - xhat * jnp.mean(gy * xhat, -1, keepdims=True)
            )
            ig[s, :] = gs.astype(BF16)
            tg[pl.ds(r, 1), :] += colsum(gs)

    def down(r):
        part[sl(r), :] = nn(act[sl(r), :], wdn[...])
        core_copy(3, r).start()

    def finish(r):
        @pl.loop(0, seq // SUB)
        def _(i):
            s = sub(r, i)
            out[s, :] = (mid[s, :] + (tot[s, :] + dnb[...])).astype(BF16)

    blk = loc

    early = ff // blk

    def weight_grads(j):
        s = pl.ds(pl.multiple_of(j * blk, blk), blk)

        def by(right):
            def fn():
                g[s, :] = nn(lt[s, :], right[...])

            return fn

        when(j < early, by(cot))
        when((j >= early) & (j < 2 * early), by(gp))
        when(j == 2 * early, by(gbr))
        when(j > 2 * early, by(entry))

    def ok(u, n):
        return (u >= 0) & (u < n)

    def go(copy, u, depth):
        when(u >= depth, lambda: copy(u - depth).wait_send())
        copy(u).start()

    def end(copy, n, depth):
        for u in range(n - min(depth, n), n):
            copy(u).wait_send()

    def a_base(u):
        return (u // 3 * 5 + u % 3) * 4 * CH

    def x_slot(u):
        return pl.ds(pl.multiple_of(u % R["xr"].shape[0] * 2 * CH, CH), 2 * CH)

    def x_first(u):
        src = pl.ds(pl.multiple_of(a_base(u) + (1 - x) * 2 * CH, CH), 2 * CH)
        return remote(
            g.at[src], R["xrb"].at[x_slot(u)], R["xs"].at[u % SENDS], R["xr"].at[u % R["xr"].shape[0]], to_x
        )

    class Way:
        def __init__(self, kind, d):
            self.kind, self.d = kind, d
            self.two = kind != "a"
            self.w = z if d == 0 else L - 1 - z
            self.up = (zhi if d == 0 else zlo, mp)
            self.dn = (zlo if d == 0 else zhi, mp)
            self.root = 0 if kind == "c" else D - 1
            self.depth = L - 1 - self.root
            self.n = UB if self.two else UA
            self.first = {"a": LAG, "b": 0, "c": 1}[kind]
            self.stride = 3 if self.two else 1
            self.gap = LAG if self.two else 0
            self.rows = 2 * CH if self.two else CH
            self.lo, self.hi = R[kind + "lo"], R[kind + "hi"]
            self.sems = {t: R[kind + "_" + t] for t in ("s", "r", "u", "d", "t", "xs", "xr")}
            self.flight, self.W = self.sems["s"].shape[1], self.sems["r"].shape[1]

        def unit(self, t, offset):
            rel = t - self.first - offset
            return rel // self.stride, (rel >= 0) & (rel < self.n * self.stride) & (rel % self.stride == 0)

        def own(self, u):
            if self.two:
                base = (u * 5 + (3 if self.kind == "b" else 4)) * 4 * CH
            else:
                base = a_base(u) + x * 2 * CH
            return pl.ds(pl.multiple_of(base + self.d * self.rows, CH), self.rows)

        def slot(self, u):
            return pl.ds(pl.multiple_of(u % self.W * self.rows, CH), self.rows)

        def copy(self, src, dst, ssem, rsem, u, dev):
            return remote(
                src, dst, self.sems[ssem].at[self.d, u % self.flight], self.sems[rsem].at[self.d, u % self.W], dev
            )

        def send_up(self, u):
            return self.copy(g.at[self.own(u)], self.lo.at[self.d, self.slot(u)], "s", "r", u, self.up)

        def send_up_root(self, u):
            return self.copy(g.at[self.own(u)], self.lo.at[self.d, self.slot(u)], "s", "t", u, self.up)

        def send_dn(self, u):
            return self.copy(g.at[self.own(u)], self.hi.at[self.d, self.slot(u)], "s", "r", u, self.dn)

        def total_up(self, u):
            return self.copy(f.at[self.own(u)], f.at[self.own(u)], "u", "t", u, self.up)

        def total_dn(self, u):
            return self.copy(f.at[self.own(u)], f.at[self.own(u)], "d", "t", u, self.dn)

        def x_copy(self, u):
            if self.two:
                return self.copy(g.at[self.own(u)], R[self.kind + "xb"].at[self.d, self.slot(u)], "xs", "xr", u, to_x)
            return self.copy(f.at[self.own(u)], f.at[self.own(u)], "xs", "xr", u, to_x)

        def go(self, copy, u):
            go(copy, u, self.flight)

        def reduce(self, u):
            w, root, own = self.w, self.root, self.own(u)

            def from_low():
                when(w < root, lambda: self.send_up(u).wait_recv())
                when(w == root, lambda: self.send_up_root(u).wait_recv())
                g[own, :] += self.lo[self.d, self.slot(u), :]

            def from_high():
                self.send_dn(u).wait_recv()
                g[own, :] += self.hi[self.d, self.slot(u), :]

            if root > 0:
                when((w > 0) & (w <= root), from_low)
            when((w < L - 1) & (w >= root), from_high)
            if root > 1:
                when(w < root - 1, lambda: self.go(self.send_up, u))
            if root > 0:
                when(w == root - 1, lambda: self.go(self.send_up_root, u))
            when(w > root, lambda: self.go(self.send_dn, u))
            if self.two:
                when(w == root, lambda: self.go(self.x_copy, u))

        def turn(self, u):
            own = self.own(u)
            if self.two:
                self.x_copy(u).wait_recv()
                f[own, :] = g[own, :] + R[self.kind + "xb"][self.d, self.slot(u), :]
            else:
                f[own, :] = g[own, :]
            self.go(self.total_up, u)
            if self.root > 0:
                self.go(self.total_dn, u)
            if not self.two:
                self.go(self.x_copy, u)

        def spread(self, u):
            w, root = self.w, self.root
            self.total_up(u).wait_recv()
            when((w > root) & (w < L - 1), lambda: self.go(self.total_up, u))
            if root > 1:
                when((w < root) & (w > 0), lambda: self.go(self.total_dn, u))
            if not self.two:
                self.go(self.x_copy, u)

        def tick(self, t):
            w, root = self.w, self.root
            dist = jnp.abs(w - root) * LAG
            u, valid = self.unit(t, self.depth * LAG - dist)
            when(valid, lambda: self.reduce(u))
            v, valid_v = self.unit(t, self.depth * LAG + self.gap)
            when(valid_v & (w == root), lambda: self.turn(v))
            q, valid_q = self.unit(t, self.depth * LAG + self.gap + dist)
            when(valid_q & (w != root), lambda: self.spread(q))
            if not self.two:
                e, valid_e = self.unit(t, self.depth * LAG + self.gap + dist + LAG)
                when(valid_e, lambda: self.x_copy(e).wait_recv())

        def drain(self):
            w, root, n, flight = self.w, self.root, self.n, self.flight
            if root > 1:
                when(w < root - 1, lambda: end(self.send_up, n, flight))
            if root > 0:
                when(w == root - 1, lambda: end(self.send_up_root, n, flight))
                when((w <= root) & (w > 0), lambda: end(self.total_dn, n, flight))
            when(w > root, lambda: end(self.send_dn, n, flight))
            when((w >= root) & (w < L - 1), lambda: end(self.total_up, n, flight))
            if self.two:
                when(w == root, lambda: end(self.x_copy, n, flight))
            else:
                end(self.x_copy, n, flight)

    ways = [Way(kind, d) for kind in ("c", "b", "a") for d in (0, 1)]

    def dp_tick(t):
        when(t < UA, lambda: go(x_first, t, SENDS))

        def x_add():
            u = t - LAG
            x_first(u).wait_recv()
            s = pl.ds(pl.multiple_of(a_base(u) + x * 2 * CH, CH), 2 * CH)
            g[s, :] += R["xrb"][x_slot(u), :]

        when(ok(t - LAG, UA), x_add)
        for way in ways:
            way.tick(t)

    def dp_drain():
        end(x_first, UA, SENDS)
        for way in ways:
            way.drain()

    for copy in loads.values():
        copy.start()

    def vector(i, name):
        loads[name].wait()
        R["vecs"][i : i + 1, :] = R[name][...][None, :]

    g[small : small + 4 * CH, :] = jnp.zeros((4 * CH, width), F32)
    for name in ("tok", "tim"):
        loads[name].wait()
    timf[...] = tim[...].astype(F32)
    vector(0, "n1g")
    vector(1, "n1b")

    @pl.loop(0, rows_n)
    def _(r):
        norm1(r)

        @pl.when(r == 0)
        def _():
            for name in ("wqkv", "qvb", "seg", "wout"):
                loads[name].wait()

        project(r)
        attend(r)
        sum_b(0, r)

    for name in ("cot", "wdn", "wup"):
        loads[name].wait()
    for i, name in enumerate(("outb", "n2g", "n2b", "upb", "dnb")):
        vector(2 + i, name)

    @pl.loop(0, rows_n)
    def _(r):
        grad_act(r)
        when(r > 0, lambda: sum_b(1, r - 1))
        sum_c(0, r)
        sum_d(0, r)
        feed(r)

    weight_grads(jnp.int32(0))

    blocks = (2 * ff + 4 * loc) // blk
    per = blk // (4 * CH)
    a_last = LAG * (2 * D + 2)
    c_last = LAG * (2 * L - 1)
    ticks = max(UA + a_last, 3 * UB + c_last)

    def out_copy(j):
        s = pl.ds(j * blk, blk if j < blocks else 4 * CH)
        return pltpu.make_async_copy(f.at[s], f_out.at[s], R["fin"].at[j])

    @pl.loop(0, ticks)
    def _(t):
        dp_tick(t)

        def at(first, step, fn):
            r = (t - first) // step
            when((t >= first) & ((t - first) % step == 0) & (r < rows_n), lambda: fn(r))

        when(t == 0, lambda: sum_b(1, rows_n - 1))
        at(0, 2, lambda r: sum_c(1, r))

        def second(r):
            sum_d(1, r)
            back2(r)

        at(1, 2, second)
        at(2, 2, lambda r: sum_b(2, r))
        at(5, 2, lambda r: sum_c(2, r))

        def third(r):
            sum_d(2, r)
            back1(r)

        at(6, 2, third)
        at(9, 2, down)
        at(10, 2, lambda r: sum_b(3, r))
        at(13, 2, lambda r: sum_c(3, r))

        def fourth(r):
            sum_d(3, r)
            finish(r)

        at(14, 2, fourth)
        when((t % 3 == 1) & (t < 3 * blocks - 2), lambda: weight_grads((t + 2) // 3))
        for j in range(blocks):
            done = (per * (j + 1) - 1) // 5 * 3 + 2 + max(a_last, c_last)
            if done < ticks:
                when(t == done, lambda: out_copy(j).start())

    dp_drain()
    for j in range(blocks + 1):
        if j == blocks or (per * (j + 1) - 1) // 5 * 3 + 2 + max(a_last, c_last) >= ticks:
            out_copy(j).start()
    for j in range(blocks + 1):
        out_copy(j).wait()


def shards(n_dp, *args):
    (tok, tim, seg, n1g, n1b, wqkv, qvb, wout, outb, n2g, n2b, wup, upb, wdn, dnb, cot) = args
    tokens, width = tok.shape
    rows_n, seq = seg.shape
    loc, ff = wout.shape[0], wup.shape[1]
    heads = loc // HD
    half = width // 2
    big = 2 * ff + 4 * loc
    count = big // (4 * CH) + 1
    UB = count // 5
    UA = count - 2 * UB
    L = n_dp // 2
    LAG = hop_ticks(L)
    vm = pltpu.VMEM
    dma = pltpu.SemaphoreType.DMA
    W = LAG * (L + 1) + 2
    WB = LAG * (L + 1) // 3 + 3
    WC = LAG * (2 * L - 1) // 3 + 3
    total = count * 4 * CH
    slots = lambda w, rows: vm((2, w * rows, width), F32)
    flat = lambda n: vm((n,), F32)
    scratch = dict(
        tok=vm((tokens, width), BF16),
        cot=vm((tokens, width), BF16),
        wqkv=vm((3, loc, width), BF16),
        wout=vm((loc, width), BF16),
        wup=vm((width, ff), BF16),
        wdn=vm((ff, width), BF16),
        ins=dma((16,)),
        tim=vm((rows_n, width), BF16),
        seg=vm((rows_n, seq), jnp.int32),
        qvb=vm((2, loc), F32),
        **{s: flat(width) for s in ("n1g", "n1b", "outb", "n2g", "n2b", "dnb")},
        upb=flat(ff),
        vecs=vm((8, width), F32),
        timf=vm((rows_n, width), F32),
        start=vm((tokens, width), F32),
        entry=vm((tokens, width), BF16),
        q=vm((tokens, loc), BF16),
        k=vm((tokens, loc), BF16),
        v=vm((tokens, loc), BF16),
        probs=vm((heads * tokens, seq), F32),
        mixed=vm((tokens, loc), BF16),
        part=vm((tokens, width), F32),
        cr=vm((tokens, half), F32),
        ys=vm((tokens, half), F32),
        yr=vm((2, tokens, half), F32),
        tot=vm((tokens, width), F32),
        mid=vm((tokens, width), F32),
        e2=vm((tokens, width), BF16),
        hp=vm((seq, ff), F32),
        act=vm((tokens, ff), BF16),
        gp=vm((tokens, ff), BF16),
        gact=vm((tokens, ff), F32),
        gmid=vm((tokens, width), F32),
        gbr=vm((tokens, width), BF16),
        lt=vm((big, tokens), BF16),
        g=vm((total, width), F32),
        f=vm((total, width), F32),
        xrb=vm((W * 2 * CH, width), F32),
        alo=slots(W, CH),
        ahi=slots(W, CH),
        blo=slots(WB, 2 * CH),
        bhi=slots(WB, 2 * CH),
        bxb=slots(WB, 2 * CH),
        clo=slots(1, 2 * CH),
        chi=slots(WC, 2 * CH),
        cxb=slots(WC, 2 * CH),
        **{s: dma((rows_n,)) for s in ("cs", "crs", "yss", "gs", "grs")},
        yrs=dma((2, rows_n)),
        fin=dma((big // loc + 1,)),
        xs=dma((SENDS,)),
        xr=dma((W,)),
        **{k + "_" + s: dma((2, SENDS if k == "a" else 2)) for k in "abc" for s in ("s", "u", "d", "xs")},
        **{k + "_" + s: dma((2, w)) for k, w in (("a", W), ("b", WB), ("c", WC)) for s in ("r", "t", "xr")},
    )
    any_spec = pl.BlockSpec(memory_space=pl.ANY)
    vm_spec = pl.BlockSpec(memory_space=pltpu.VMEM)
    out, ig, tg, f = pl.pallas_call(
        functools.partial(kernel, n_dp, (UA, UB), tuple(scratch)),
        out_shape=(
            jax.ShapeDtypeStruct((tokens, width), BF16),
            jax.ShapeDtypeStruct((tokens, width), BF16),
            jax.ShapeDtypeStruct((rows_n, width), F32),
            jax.ShapeDtypeStruct((total, width), F32),
        ),
        in_specs=[any_spec] * 16,
        out_specs=(vm_spec, vm_spec, vm_spec, any_spec),
        scratch_shapes=list(scratch.values()),
        compiler_params=pltpu.CompilerParams(
            collective_id=0, has_side_effects=True, vmem_limit_bytes=63 * 2**20
        ),
        cost_estimate=pl.CostEstimate(flops=6 * 10**9, bytes_accessed=20 * 10**6, transcendentals=0),
    )(
        tok, tim, seg, n1g, n1b, wqkv.transpose(0, 2, 1), qvb, wout, outb, n2g, n2b, wup, upb, wdn, dnb, cot
    )
    f32 = lambda *shape: jax.ShapeDtypeStruct(shape, F32)
    moved = (
        jax.ShapeDtypeStruct((tokens, width), BF16),
        jax.ShapeDtypeStruct((tokens, width), BF16),
        f32(rows_n, width),
        f32(3, loc, width),
        f32(loc, width),
        f32(width, ff),
        f32(ff, width),
    )
    results = pl.pallas_call(
        functools.partial(place, big),
        out_shape=moved + (f32(2, loc), f32(ff)) + (f32(width),) * 6,
        in_specs=[any_spec] * 4,
        out_specs=(any_spec,) * 7 + (vm_spec,) * 8,
        scratch_shapes=[
            vm((8, width), F32),
            vm((big, width), F32),
            vm((tokens, width), BF16),
            vm((tokens, width), BF16),
            vm((rows_n, width), F32),
            dma((10,)),
            dma((10,)),
        ],
        compiler_params=pltpu.CompilerParams(vmem_limit_bytes=63 * 2**20),
    )(out, ig, tg, f)
    out, ig, tg, qkv, outw, up, down, qvb, upb, downb, n2g, n2b, outb, n1g, n1b = results
    return out, ig, tg, n1g, n1b, qkv.transpose(0, 2, 1), qvb, outw, outb, n2g, n2b, up, upb, down, downb


def place(big, *refs):
    out, ig, tg, f, out_o, ig_o, tg_o, qkv, outw, up, down, qvb, upb, downb = refs[:14]
    n2g, n2b, outb, n1g, n1b, sm, buf, vo, vi, vt, sem, sem_o = refs[14:]
    loc, ff = outw.shape[0], down.shape[0]
    half = f.shape[1] // 2
    moves = []
    row = 0
    for n, ref in ((ff, down), (ff, up), (loc, outw), (loc, qkv.at[0]), (loc, qkv.at[1]), (loc, qkv.at[2])):
        s = pl.ds(row, n)
        moves.append((f.at[s], buf.at[s], ref))
        row += n
    moves += [(out, vo, out_o), (ig, vi, ig_o), (tg, vt, tg_o)]
    first = pltpu.make_async_copy(f.at[pl.ds(big, 8)], sm, sem.at[9])
    first.start()
    loads = [pltpu.make_async_copy(a, v, sem.at[i]) for i, (a, v, b) in enumerate(moves)]
    stores = [pltpu.make_async_copy(v, b, sem_o.at[i]) for i, (a, v, b) in enumerate(moves)]
    for copy in loads:
        copy.start()
    for load, store in zip(loads, stores):
        load.wait()
        store.start()
    first.wait()
    for i, ref in enumerate((downb, upb, n2g, n2b, outb, n1g, n1b)):
        ref[...] = sm[i : i + 1, :].reshape(ref.shape)
    qvb[0:1, :] = sm[7:8, 0:loc]
    qvb[1:2, :] = sm[7:8, half : half + loc]
    for copy in stores:
        copy.wait()


def solution(mesh):
    placed = (
        P("dp", None),
        P("dp", None),
        P("dp", None),
        P(),
        P(),
        P(None, None, "mp"),
        P(None, "mp"),
        P("mp", None),
        P(),
        P(),
        P(),
        P(None, "mp"),
        P("mp"),
        P("mp", None),
        P(),
        P("dp", None),
    )
    return jax.shard_map(
        functools.partial(shards, mesh.shape["dp"]),
        mesh=mesh,
        in_specs=placed,
        out_specs=(
            P("dp", None),
            P("dp", None),
            P("dp", None),
            P(),
            P(),
            P(None, None, "mp"),
            P(None, "mp"),
            P("mp", None),
            P(),
            P(),
            P(),
            P(None, "mp"),
            P("mp"),
            P("mp", None),
            P(),
        ),
        check_vma=False,
    )
```

time: 199 us -> 176 us (0.88)
  Pallas kernels: 198 us -> 175 us
    pallas_call x1, Pallas kernels: 191 us -> 168 us  [shards(): pl.pallas_call(functools.partial(kernel, n_dp, (UA, UB), tuple(scratch)),...]
where the time goes in v3:
time: 176 us
  Pallas kernels  175 us (99%)
    pallas_call x1, Pallas kernels, shards(): pl.pallas_call(functools.partial(kernel, n_dp, (UA, UB), tuple(scratch)),...  168 us
    pallas_call x1, Pallas kernels, shards(): pl.pallas_call(functools.partial(place, big), out_shape=moved + (f32(2, l...  7.27 us

profile of v3, /device:TPU:0, one launch (start us, length us, event | category | flops | bytes accessed | tf_op | source)
XLA Modules:
  0.0 175.8 jit_solution(15362164342555161210)
XLA Ops:
  0.7 167.9 %shard_map.271 = (bf16[512,768]{1,0:T(8,128)(2,1)}, bf16[512,768]{1,0:T(8,128)(2,1)}, f32[4,768]{1,0:T(4,128)}, f32[2336,768]{1,0:T(8,128)}) custom-call(bf16[512,768]{1,0:T(8,128)(2,1)} %refs_0_.1, bf16[4,768]{1,0:T(4,128)(2,1)} %refs_1_.1, s32[4,128]{1,0:T(4,128)} %refs_2_.1, f32[768]{0:T(1024)} %refs_3_.1, f32[768]{0:T(1024)} %refs_4_.1, ...), custom_call_target="tpu_custom_call" | custom-call | flops 6000000000 | bytes 20000000 | tf_op jit(solution)/shard_map/pallas_call | solution.py:652
  168.5 7.3 %shard_map.272 = (bf16[512,768]{1,0:T(8,128)(2,1)}, bf16[512,768]{1,0:T(8,128)(2,1)}, f32[4,768]{1,0:T(4,128)}, f32[3,192,768]{2,1,0:T(8,128)}, f32[192,768]{1,0...) custom-call(bf16[512,768]{1,0:T(8,128)(2,1)} %get-tuple-element.34.r, ...), custom_call_target="tpu_custom_call" | custom-call | tf_op jit(solution)/shard_map/pallas_call | solution.py:680

commit v4 on v3

--- a/solution.py
+++ b/solution.py
@@ -8,7 +8,7 @@
 from jax.sharding import PartitionSpec as P
 
 HD = 64
-SUB = 32
+SUB = 128
 CH = 8
 SENDS = 4
 MESH = pl.DeviceIdType.MESH
@@ -52,7 +52,7 @@
 
 
 def kernel(n_dp, units, names, *refs):
-    out, ig, tg, f_out = refs[16:20]
+    out_o, ig_o, tg_o, f_out = refs[16:20]
     R = dict(zip(names, refs[20:]))
     order = ("tok", "tim", "n1g", "n1b", "wqkv", "qvb", "seg", "wout", "outb", "cot", "wdn")
     order += ("n2g", "n2b", "wup", "upb", "dnb")
@@ -66,6 +66,7 @@
     timf, start, entry, q_s, k_s, v_s = (R[s] for s in ("timf", "start", "entry", "q", "k", "v"))
     probs, mixed_s, part, cr, ys, yr = (R[s] for s in ("probs", "mixed", "part", "cr", "ys", "yr"))
     tot, mid, e2, hp, act, gp = (R[s] for s in ("tot", "mid", "e2", "hp", "act", "gp"))
+    out, ig, tg = (R[s] for s in ("out", "ig", "tg"))
     gact, gmid, gbr, lt, g, f = (R[s] for s in ("gact", "gmid", "gbr", "lt", "g", "f"))
 
     rows_n, seq = seg.shape
@@ -74,7 +75,7 @@
     loc = wout.shape[0]
     heads = loc // HD
     ff = wup.shape[1]
-    UA, UB = units
+    UA, UB, UC = units
     L = n_dp // 2
     LAG = hop_ticks(L)
     D = L // 2
@@ -329,7 +330,7 @@
             self.dn = (zlo if d == 0 else zhi, mp)
             self.root = 0 if kind == "c" else D - 1
             self.depth = L - 1 - self.root
-            self.n = UB if self.two else UA
+            self.n = {"a": UA, "b": UB, "c": UC}[kind]
             self.first = {"a": LAG, "b": 0, "c": 1}[kind]
             self.stride = 3 if self.two else 1
             self.gap = LAG if self.two else 0
@@ -344,7 +345,7 @@
 
         def own(self, u):
             if self.two:
-                base = (u * 5 + (3 if self.kind == "b" else 4)) * 4 * CH
+                base = jnp.minimum(u * 5 + (3 if self.kind == "b" else 4), UA + UB + UC - 1) * 4 * CH
             else:
                 base = a_base(u) + x * 2 * CH
             return pl.ds(pl.multiple_of(base + self.d * self.rows, CH), self.rows)
@@ -517,13 +518,18 @@
     blocks = (2 * ff + 4 * loc) // blk
     per = blk // (4 * CH)
     a_last = LAG * (2 * D + 2)
-    c_last = LAG * (2 * L - 1)
-    ticks = max(UA + a_last, 3 * UB + c_last)
+    b_last, c_last = LAG * (L + 1), LAG * (2 * L - 1)
+    ticks = max(UA + a_last, 3 * UB - 2 + b_last, 3 * UC - 1 + c_last)
 
     def out_copy(j):
         s = pl.ds(j * blk, blk if j < blocks else 4 * CH)
         return pltpu.make_async_copy(f.at[s], f_out.at[s], R["fin"].at[j])
 
+    done_copies = [
+        pltpu.make_async_copy(a, b, R["fin"].at[blocks + 1 + i])
+        for i, (a, b) in enumerate(((ig, ig_o), (tg, tg_o), (out, out_o)))
+    ]
+
     @pl.loop(0, ticks)
     def _(t):
         dp_tick(t)
@@ -533,30 +539,36 @@
             when((t >= first) & ((t - first) % step == 0) & (r < rows_n), lambda: fn(r))
 
         when(t == 0, lambda: sum_b(1, rows_n - 1))
-        at(0, 2, lambda r: sum_c(1, r))
+        at(2, 3, lambda r: sum_c(1, r))
 
         def second(r):
             sum_d(1, r)
             back2(r)
 
-        at(1, 2, second)
-        at(2, 2, lambda r: sum_b(2, r))
-        at(5, 2, lambda r: sum_c(2, r))
+        at(3, 3, second)
+        at(4, 3, lambda r: sum_b(2, r))
+        at(10, 3, lambda r: sum_c(2, r))
 
         def third(r):
             sum_d(2, r)
             back1(r)
 
-        at(6, 2, third)
-        at(9, 2, down)
-        at(10, 2, lambda r: sum_b(3, r))
-        at(13, 2, lambda r: sum_c(3, r))
+        at(11, 3, third)
+        at(12, 3, down)
+        at(13, 3, lambda r: sum_b(3, r))
+        at(18, 3, lambda r: sum_c(3, r))
 
         def fourth(r):
             sum_d(3, r)
             finish(r)
 
-        at(14, 2, fourth)
+        at(19, 3, fourth)
+
+        @pl.when(t == 19 + 3 * rows_n)
+        def _():
+            for copy in done_copies:
+                copy.start()
+
         when((t % 3 == 1) & (t < 3 * blocks - 2), lambda: weight_grads((t + 2) // 3))
         for j in range(blocks):
             done = (per * (j + 1) - 1) // 5 * 3 + 2 + max(a_last, c_last)
@@ -567,8 +579,8 @@
     for j in range(blocks + 1):
         if j == blocks or (per * (j + 1) - 1) // 5 * 3 + 2 + max(a_last, c_last) >= ticks:
             out_copy(j).start()
-    for j in range(blocks + 1):
-        out_copy(j).wait()
+    for copy in done_copies + [out_copy(j) for j in range(blocks + 1)]:
+        copy.wait()
 
 
 def shards(n_dp, *args):
@@ -580,15 +592,17 @@
     half = width // 2
     big = 2 * ff + 4 * loc
     count = big // (4 * CH) + 1
-    UB = count // 5
-    UA = count - 2 * UB
+    UC = count // 5
+    UB = UC + (count % 5) // 3
+    UA = count - UB - UC
     L = n_dp // 2
     LAG = hop_ticks(L)
     vm = pltpu.VMEM
     dma = pltpu.SemaphoreType.DMA
-    W = LAG * (L + 1) + 2
-    WB = LAG * (L + 1) // 3 + 3
-    WC = LAG * (2 * L - 1) // 3 + 3
+    W = LAG * L + 2
+    WX = 2 * LAG + 2
+    WB = LAG * (L + 1) // 3 + 2
+    WC = LAG * (2 * L - 1) // 3 + 2
     total = count * 4 * CH
     slots = lambda w, rows: vm((2, w * rows, width), F32)
     flat = lambda n: vm((n,), F32)
@@ -627,10 +641,13 @@
         gact=vm((tokens, ff), F32),
         gmid=vm((tokens, width), F32),
         gbr=vm((tokens, width), BF16),
+        out=vm((tokens, width), BF16),
+        ig=vm((tokens, width), BF16),
+        tg=vm((rows_n, width), F32),
         lt=vm((big, tokens), BF16),
         g=vm((total, width), F32),
         f=vm((total, width), F32),
-        xrb=vm((W * 2 * CH, width), F32),
+        xrb=vm((WX * 2 * CH, width), F32),
         alo=slots(W, CH),
         ahi=slots(W, CH),
         blo=slots(WB, 2 * CH),
@@ -641,16 +658,16 @@
         cxb=slots(WC, 2 * CH),
         **{s: dma((rows_n,)) for s in ("cs", "crs", "yss", "gs", "grs")},
         yrs=dma((2, rows_n)),
-        fin=dma((big // loc + 1,)),
+        fin=dma((big // loc + 4,)),
         xs=dma((SENDS,)),
-        xr=dma((W,)),
+        xr=dma((WX,)),
         **{k + "_" + s: dma((2, SENDS if k == "a" else 2)) for k in "abc" for s in ("s", "u", "d", "xs")},
         **{k + "_" + s: dma((2, w)) for k, w in (("a", W), ("b", WB), ("c", WC)) for s in ("r", "t", "xr")},
     )
     any_spec = pl.BlockSpec(memory_space=pl.ANY)
     vm_spec = pl.BlockSpec(memory_space=pltpu.VMEM)
     out, ig, tg, f = pl.pallas_call(
-        functools.partial(kernel, n_dp, (UA, UB), tuple(scratch)),
+        functools.partial(kernel, n_dp, (UA, UB, UC), tuple(scratch)),
         out_shape=(
             jax.ShapeDtypeStruct((tokens, width), BF16),
             jax.ShapeDtypeStruct((tokens, width), BF16),
@@ -658,7 +675,7 @@
             jax.ShapeDtypeStruct((total, width), F32),
         ),
         in_specs=[any_spec] * 16,
-        out_specs=(vm_spec, vm_spec, vm_spec, any_spec),
+        out_specs=(any_spec,) * 4,
         scratch_shapes=list(scratch.values()),
         compiler_params=pltpu.CompilerParams(
             collective_id=0, has_side_effects=True, vmem_limit_bytes=63 * 2**20

time: 176 us -> 164 us (0.932)
  Pallas kernels: 175 us -> 164 us
    pallas_call x1, Pallas kernels: 168 us -> 156 us  [shards(): pl.pallas_call(functools.partial(kernel, n_dp, (UA, UB, UC), tuple(scratc...]
where the time goes in v4:
time: 164 us
  Pallas kernels  164 us (100%)
    pallas_call x1, Pallas kernels, shards(): pl.pallas_call(functools.partial(kernel, n_dp, (UA, UB, UC), tuple(scratc...  156 us
    pallas_call x1, Pallas kernels, shards(): pl.pallas_call(functools.partial(place, big), out_shape=moved + (f32(2, l...  7.27 us

profile of v4, /device:TPU:0, one launch (start us, length us, event | category | flops | bytes accessed | tf_op | source)
XLA Modules:
  0.0 164.3 jit_solution(12936193654943549646)
XLA Ops:
  0.7 156.3 %shard_map.271 = (bf16[512,768]{1,0:T(8,128)(2,1)}, bf16[512,768]{1,0:T(8,128)(2,1)}, f32[4,768]{1,0:T(4,128)}, f32[2336,768]{1,0:T(8,128)}) custom-call(bf16[512,768]{1,0:T(8,128)(2,1)} %refs_0_.1, bf16[4,768]{1,0:T(4,128)(2,1)} %refs_1_.1, s32[4,128]{1,0:T(4,128)} %refs_2_.1, f32[768]{0:T(1024)} %refs_3_.1, f32[768]{0:T(1024)} %refs_4_.1, ...), custom_call_target="tpu_custom_call" | custom-call | flops 6000000000 | bytes 20000000 | tf_op jit(solution)/shard_map/pallas_call | solution.py:669
  157.0 7.3 %shard_map.272 = (bf16[512,768]{1,0:T(8,128)(2,1)}, bf16[512,768]{1,0:T(8,128)(2,1)}, f32[4,768]{1,0:T(4,128)}, f32[3,192,768]{2,1,0:T(8,128)}, f32[192,768]{1,0...) custom-call(bf16[512,768]{1,0:T(8,128)(2,1)} %get-tuple-element.34.r, ...), custom_call_target="tpu_custom_call" | custom-call | tf_op jit(solution)/shard_map/pallas_call | solution.py:697

commit v5 on v4

--- a/solution.py
+++ b/solution.py
@@ -22,6 +22,10 @@
 
 def hop_ticks(line):
     return 2 if line <= 8 else 1
+
+
+def direct_units(line):
+    return (2, 0, 1) if line <= 8 else (0, 0, 0)
 
 
 def when(cond, fn):
@@ -78,6 +82,7 @@
     UA, UB, UC = units
     L = n_dp // 2
     LAG = hop_ticks(L)
+    DIRECT = direct_units(L)
     D = L // 2
     root = D - 1
     dp = lax.axis_index("dp")
@@ -96,6 +101,7 @@
         pl.semaphore_signal(barrier, 1, device_id=dev, device_id_type=MESH)
     when(z > 0, lambda: pl.semaphore_signal(barrier, 1, device_id=(zlo, mp), device_id_type=MESH))
     when(z < L - 1, lambda: pl.semaphore_signal(barrier, 1, device_id=(zhi, mp), device_id_type=MESH))
+    greeted = 3 + jnp.minimum(z, 1) + jnp.minimum(L - 1 - z, 1)
 
     def sl(r, n=seq):
         return pl.ds(pl.multiple_of(r * n, n), n)
@@ -183,7 +189,7 @@
 
         @pl.when(r == 0)
         def _():
-            pl.semaphore_wait(barrier, 3 + jnp.minimum(z, 1) + jnp.minimum(L - 1 - z, 1))
+            pl.semaphore_wait(barrier, greeted)
 
         core_copy(0, r).start()
         lt[2 * ff : 2 * ff + loc, sl(r)] = mixed.T
@@ -338,6 +344,20 @@
             self.lo, self.hi = R[kind + "lo"], R[kind + "hi"]
             self.sems = {t: R[kind + "_" + t] for t in ("s", "r", "u", "d", "t", "xs", "xr")}
             self.flight, self.W = self.sems["s"].shape[1], self.sems["r"].shape[1]
+            self.normal = self.n - DIRECT["abc".index(kind)]
+
+        def column(self, w):
+            return ((w if self.d == 0 else L - 1 - w) * 2 + x, mp)
+
+        def straight(self, u, w):
+            own = self.own(u)
+            ssem, rsem = R[self.kind + "_q"].at[self.d, w], self.sems["t"].at[self.d, u % self.W]
+            return remote(f.at[own], f.at[own], ssem, rsem, self.column(w))
+
+        def straight_all(self, u, what):
+            for w in range(L):
+                if w != self.root:
+                    getattr(self.straight(u, w), what)()
 
         def unit(self, t, offset):
             rel = t - self.first - offset
@@ -411,9 +431,21 @@
                 f[own, :] = g[own, :] + R[self.kind + "xb"][self.d, self.slot(u), :]
             else:
                 f[own, :] = g[own, :]
-            self.go(self.total_up, u)
-            if self.root > 0:
-                self.go(self.total_dn, u)
+
+            def near():
+                self.go(self.total_up, u)
+                if self.root > 0:
+                    self.go(self.total_dn, u)
+
+            def far():
+                when(u > self.normal, lambda: self.straight_all(u - 1, "wait_send"))
+                self.straight_all(u, "start")
+
+            if self.normal < self.n:
+                when(u < self.normal, near)
+                when(u >= self.normal, far)
+            else:
+                near()
             if not self.two:
                 self.go(self.x_copy, u)
 
@@ -433,21 +465,36 @@
             when(valid, lambda: self.reduce(u))
             v, valid_v = self.unit(t, self.depth * LAG + self.gap)
             when(valid_v & (w == root), lambda: self.turn(v))
-            q, valid_q = self.unit(t, self.depth * LAG + self.gap + dist)
-            when(valid_q & (w != root), lambda: self.spread(q))
+            after = self.depth * LAG + self.gap
+            q, valid_q = self.unit(t, after + dist)
+            when(valid_q & (w != root) & (q < self.normal), lambda: self.spread(q))
             if not self.two:
-                e, valid_e = self.unit(t, self.depth * LAG + self.gap + dist + LAG)
-                when(valid_e, lambda: self.x_copy(e).wait_recv())
+                e, valid_e = self.unit(t, after + dist + LAG)
+                when(valid_e & (e < self.normal), lambda: self.x_copy(e).wait_recv())
+            if self.normal < self.n:
+                h, valid_h = self.unit(t, after + LAG)
+
+                def arrive():
+                    self.total_up(h).wait_recv()
+                    if not self.two:
+                        self.go(self.x_copy, h)
+
+                when(valid_h & (h >= self.normal) & (w != root), arrive)
+                if not self.two:
+                    i, valid_i = self.unit(t, after + jnp.minimum(dist, LAG) + LAG)
+                    when(valid_i & (i >= self.normal), lambda: self.x_copy(i).wait_recv())
 
         def drain(self):
             w, root, n, flight = self.w, self.root, self.n, self.flight
+            if self.normal < n:
+                when(w == root, lambda: self.straight_all(n - 1, "wait_send"))
             if root > 1:
                 when(w < root - 1, lambda: end(self.send_up, n, flight))
             if root > 0:
                 when(w == root - 1, lambda: end(self.send_up_root, n, flight))
-                when((w <= root) & (w > 0), lambda: end(self.total_dn, n, flight))
+                when((w <= root) & (w > 0), lambda: end(self.total_dn, self.normal, flight))
             when(w > root, lambda: end(self.send_dn, n, flight))
-            when((w >= root) & (w < L - 1), lambda: end(self.total_up, n, flight))
+            when((w >= root) & (w < L - 1), lambda: end(self.total_up, self.normal, flight))
             if self.two:
                 when(w == root, lambda: end(self.x_copy, n, flight))
             else:
@@ -519,7 +566,14 @@
     per = blk // (4 * CH)
     a_last = LAG * (2 * D + 2)
     b_last, c_last = LAG * (L + 1), LAG * (2 * L - 1)
-    ticks = max(UA + a_last, 3 * UB - 2 + b_last, 3 * UC - 1 + c_last)
+    ends = []
+    for n, k, stride, first, late, soon in (
+        (UA, DIRECT[0], 1, 0, a_last, LAG * (D + 3)),
+        (UB, DIRECT[1], 3, 0, b_last, LAG * (D + 2)),
+        (UC, DIRECT[2], 3, 1, c_last, LAG * (L + 1)),
+    ):
+        ends += [first + stride * (n - k - 1) + late, first + stride * (n - 1) + soon if k else 0]
+    ticks = max(ends) + 1
 
     def out_copy(j):
         s = pl.ds(j * blk, blk if j < blocks else 4 * CH)
@@ -661,6 +715,7 @@
         fin=dma((big // loc + 4,)),
         xs=dma((SENDS,)),
         xr=dma((WX,)),
+        **{k + "_q": dma((2, L)) for k, n in zip("abc", direct_units(L)) if n},
         **{k + "_" + s: dma((2, SENDS if k == "a" else 2)) for k in "abc" for s in ("s", "u", "d", "xs")},
         **{k + "_" + s: dma((2, w)) for k, w in (("a", W), ("b", WB), ("c", WC)) for s in ("r", "t", "xr")},
     )

time: 164 us -> 165 us (level)
  no operation moved by 1% of the time
where the time goes in v5:
time: 165 us; the launch traced here: 164 us
  Pallas kernels  164 us (99%)
    pallas_call x1, Pallas kernels, shards(): pl.pallas_call(functools.partial(kernel, n_dp, (UA, UB, UC), tuple(scratc...  157 us
    pallas_call x1, Pallas kernels, shards(): pl.pallas_call(functools.partial(place, big), out_shape=moved + (f32(2, l...  7.27 us

profile of v5, /device:TPU:0, one launch (start us, length us, event | category | flops | bytes accessed | tf_op | source)
XLA Modules:
  0.0 164.5 jit_solution(7916796679662989417)
XLA Ops:
  0.7 156.5 %shard_map.271 = (bf16[512,768]{1,0:T(8,128)(2,1)}, bf16[512,768]{1,0:T(8,128)(2,1)}, f32[4,768]{1,0:T(4,128)}, f32[2336,768]{1,0:T(8,128)}) custom-call(bf16[512,768]{1,0:T(8,128)(2,1)} %refs_0_.1, bf16[4,768]{1,0:T(4,128)(2,1)} %refs_1_.1, s32[4,128]{1,0:T(4,128)} %refs_2_.1, f32[768]{0:T(1024)} %refs_3_.1, f32[768]{0:T(1024)} %refs_4_.1, ...), custom_call_target="tpu_custom_call" | custom-call | flops 6000000000 | bytes 20000000 | tf_op jit(solution)/shard_map/pallas_call | solution.py:724
  157.2 7.3 %shard_map.272 = (bf16[512,768]{1,0:T(8,128)(2,1)}, bf16[512,768]{1,0:T(8,128)(2,1)}, f32[4,768]{1,0:T(4,128)}, f32[3,192,768]{2,1,0:T(8,128)}, f32[192,768]{1,0...) custom-call(bf16[512,768]{1,0:T(8,128)(2,1)} %get-tuple-element.34.r, ...), custom_call_target="tpu_custom_call" | custom-call | tf_op jit(solution)/shard_map/pallas_call | solution.py:752

commit v6 on v4

--- a/solution.py
+++ b/solution.py
@@ -10,6 +10,8 @@
 HD = 64
 SUB = 128
 CH = 8
+PRE = False
+EACH = 4 if PRE else 3
 SENDS = 4
 MESH = pl.DeviceIdType.MESH
 F32 = jnp.float32
@@ -26,6 +28,18 @@
 
 def when(cond, fn):
     pl.when(cond)(fn)
+
+
+def rem(a, n):
+    return lax.rem(a, jnp.int32(n))
+
+
+def div(a, n):
+    return lax.div(a, jnp.int32(n))
+
+
+def two_power(n):
+    return 1 << (n - 1).bit_length()
 
 
 def nt(a, b):
@@ -78,8 +92,7 @@
     UA, UB, UC = units
     L = n_dp // 2
     LAG = hop_ticks(L)
-    D = L // 2
-    root = D - 1
+    H = L // 2
     dp = lax.axis_index("dp")
     mp = lax.axis_index("mp")
     core = mp % 2
@@ -88,6 +101,11 @@
     to_core = (dp, mp + 1 - 2 * core)
     to_y = (dp, (mp + 2) % 4)
     to_x = (dp + 1 - 2 * x, mp)
+    last = jnp.minimum(z, L - 1 - z)
+    side = div(z, H)
+    cross = jnp.where(last == H - 1, 1, 0)
+    to_in = ((z + 1 - 2 * side) * 2 + x, mp)
+    to_out = (jnp.clip(z - 1 + 2 * side, 0, L - 1) * 2 + x, mp)
     zlo = jnp.maximum(z - 1, 0) * 2 + x
     zhi = jnp.minimum(z + 1, L - 1) * 2 + x
 
@@ -96,6 +114,7 @@
         pl.semaphore_signal(barrier, 1, device_id=dev, device_id_type=MESH)
     when(z > 0, lambda: pl.semaphore_signal(barrier, 1, device_id=(zlo, mp), device_id_type=MESH))
     when(z < L - 1, lambda: pl.semaphore_signal(barrier, 1, device_id=(zhi, mp), device_id_type=MESH))
+    greeted = 3 + jnp.minimum(z, 1) + jnp.minimum(L - 1 - z, 1)
 
     def sl(r, n=seq):
         return pl.ds(pl.multiple_of(r * n, n), n)
@@ -183,7 +202,7 @@
 
         @pl.when(r == 0)
         def _():
-            pl.semaphore_wait(barrier, 3 + jnp.minimum(z, 1) + jnp.minimum(L - 1 - z, 1))
+            pl.semaphore_wait(barrier, greeted)
 
         core_copy(0, r).start()
         lt[2 * ff : 2 * ff + loc, sl(r)] = mixed.T
@@ -298,9 +317,6 @@
         when(j == 2 * early, by(gbr))
         when(j > 2 * early, by(entry))
 
-    def ok(u, n):
-        return (u >= 0) & (u < n)
-
     def go(copy, u, depth):
         when(u >= depth, lambda: copy(u - depth).wait_send())
         copy(u).start()
@@ -309,169 +325,320 @@
         for u in range(n - min(depth, n), n):
             copy(u).wait_send()
 
-    def a_base(u):
-        return (u // 3 * 5 + u % 3) * 4 * CH
+    PU = 2 * loc // (4 * CH) if PRE else 0
+    PG = PU // EACH
+    AF = LAG + (1 if PRE else 0)
+
+    def base_of(u):
+        return (PU + u) * 4 * CH
+
+    def later(u):
+        return base_of(2 * PG + div(u - PU, EACH) * (EACH + 2) + rem(u - PU, EACH))
+
+    def b_base(u, i):
+        rest = 2 * PG + (u - PG) * (EACH + 2) + EACH
+        u = jnp.where(u < PG, u * 2, rest) if PG else rest
+        return base_of(jnp.minimum(u + i, UA + UB + UC - PU - 1))
+
+    def a_base(u, owner):
+        rest = later(u) + owner * 2 * CH
+        return jnp.where(u < PU, owner * loc + u * 2 * CH, rest) if PU else rest
 
     def x_slot(u):
-        return pl.ds(pl.multiple_of(u % R["xr"].shape[0] * 2 * CH, CH), 2 * CH)
+        return pl.ds(pl.multiple_of(rem(u, R["xr"].shape[0]) * 2 * CH, CH), 2 * CH)
 
     def x_first(u):
-        src = pl.ds(pl.multiple_of(a_base(u) + (1 - x) * 2 * CH, CH), 2 * CH)
+        src = pl.ds(pl.multiple_of(later(u) + (1 - x) * 2 * CH, CH), 2 * CH)
         return remote(
-            g.at[src], R["xrb"].at[x_slot(u)], R["xs"].at[u % SENDS], R["xr"].at[u % R["xr"].shape[0]], to_x
+            g.at[src], R["xrb"].at[x_slot(u)], R["xs"].at[rem(u, SENDS)], R["xr"].at[rem(u, R["xr"].shape[0])], to_x
         )
 
-    class Way:
-        def __init__(self, kind, d):
-            self.kind, self.d = kind, d
-            self.two = kind != "a"
-            self.w = z if d == 0 else L - 1 - z
-            self.up = (zhi if d == 0 else zlo, mp)
-            self.dn = (zlo if d == 0 else zhi, mp)
-            self.root = 0 if kind == "c" else D - 1
-            self.depth = L - 1 - self.root
-            self.n = {"a": UA, "b": UB, "c": UC}[kind]
-            self.first = {"a": LAG, "b": 0, "c": 1}[kind]
-            self.stride = 3 if self.two else 1
-            self.gap = LAG if self.two else 0
-            self.rows = 2 * CH if self.two else CH
-            self.lo, self.hi = R[kind + "lo"], R[kind + "hi"]
-            self.sems = {t: R[kind + "_" + t] for t in ("s", "r", "u", "d", "t", "xs", "xr")}
-            self.flight, self.W = self.sems["s"].shape[1], self.sems["r"].shape[1]
+    def cot_x(i):
+        s = core * 2 + i
+        return remote(R["cotf"].at[i], R["cotr"].at[s], R["cxs"].at[i], R["cxr"].at[i], to_x)
+
+    def cot_c(i):
+        s = core * 2 + i
+        return remote(R["cotr"].at[s], R["cotr"].at[s], R["ccs"].at[i], R["ccr"].at[i], to_core)
+
+    def act_x(r):
+        return remote(R["actf"].at[r], R["actr"].at[r], R["axs"].at[r], R["axr"].at[r], to_x)
+
+    def cot_out():
+        loads["cot"].wait()
+        n = R["cotf"].shape[1]
+        for i in range(2):
+            s = pl.ds(pl.multiple_of((core * 2 + i) * n, n), n)
+            R["cotf"][i] = cot[s, :].astype(F32)
+            cot_x(i).start()
+
+    def cot_on():
+        for i in range(2):
+            cot_x(i).wait()
+            cot_c(i).start()
+
+    def act_out(r):
+        s = pl.ds(pl.multiple_of((1 - x) * loc, loc), loc)
+        R["actf"][r] = lt[s, sl(r)].astype(F32)
+        act_x(r).start()
+
+    def pair_grads():
+        for i in range(2):
+            cot_c(i).wait()
+        cotx, n = R["cotx"], R["cotf"].shape[1]
+        for i in range(4):
+            cotx[i * n : (i + 1) * n, :] = R["cotr"][i].astype(BF16)
+        for r in range(rows_n):
+            act_x(r).wait()
+            R["ltx"][:, r * seq : (r + 1) * seq] = R["actr"][r].astype(BF16)
+        s = pl.ds(pl.multiple_of(x * loc, loc), loc)
+        g[s, :] = nn(lt[s, :], cot[...]) + nn(R["ltx"][...], cotx[...])
+
+    def rows_at(base, n):
+        return pl.ds(pl.multiple_of(base, CH), n)
+
+    class Line:
+        def __init__(self, kind, n, first, stride, depth):
+            self.kind, self.n, self.first, self.stride, self.depth = kind, n, first, stride, depth
 
         def unit(self, t, offset):
             rel = t - self.first - offset
-            return rel // self.stride, (rel >= 0) & (rel < self.n * self.stride) & (rel % self.stride == 0)
-
+            if self.stride == 1:
+                return rel, (rel >= 0) & (rel < self.n)
+            return div(rel, self.stride), (rel >= 0) & (rel < self.n * self.stride) & (rem(rel, self.stride) == 0)
+
+        def sem(self, name, i, u):
+            ref = R[self.kind + "_" + name]
+            return ref.at[i, rem(u, ref.shape[1])]
+
+        def slot(self, u, rows):
+            return rows_at(rem(u, R[self.kind + "_r"].shape[1]) * rows, rows)
+
+        def go(self, copy, u):
+            go(copy, u, self.depth)
+
+        def end(self, copy):
+            end(copy, self.n, self.depth)
+
+    class A(Line):
         def own(self, u):
-            if self.two:
-                base = jnp.minimum(u * 5 + (3 if self.kind == "b" else 4), UA + UB + UC - 1) * 4 * CH
-            else:
-                base = a_base(u) + x * 2 * CH
-            return pl.ds(pl.multiple_of(base + self.d * self.rows, CH), self.rows)
-
-        def slot(self, u):
-            return pl.ds(pl.multiple_of(u % self.W * self.rows, CH), self.rows)
-
-        def copy(self, src, dst, ssem, rsem, u, dev):
-            return remote(
-                src, dst, self.sems[ssem].at[self.d, u % self.flight], self.sems[rsem].at[self.d, u % self.W], dev
-            )
-
-        def send_up(self, u):
-            return self.copy(g.at[self.own(u)], self.lo.at[self.d, self.slot(u)], "s", "r", u, self.up)
-
-        def send_up_root(self, u):
-            return self.copy(g.at[self.own(u)], self.lo.at[self.d, self.slot(u)], "s", "t", u, self.up)
-
-        def send_dn(self, u):
-            return self.copy(g.at[self.own(u)], self.hi.at[self.d, self.slot(u)], "s", "r", u, self.dn)
-
-        def total_up(self, u):
-            return self.copy(f.at[self.own(u)], f.at[self.own(u)], "u", "t", u, self.up)
-
-        def total_dn(self, u):
-            return self.copy(f.at[self.own(u)], f.at[self.own(u)], "d", "t", u, self.dn)
+            return rows_at(a_base(u, x), 2 * CH)
+
+        def inward(self, u):
+            dst = R["abuf"].at[cross, self.slot(u, 2 * CH)]
+            return remote(g.at[self.own(u)], dst, self.sem("s", 0, u), self.sem("r", cross, u), to_in)
+
+        def arrived(self, u, i):
+            buf = R["abuf"].at[i, self.slot(u, 2 * CH)]
+            remote(buf, buf, self.sem("s", 0, u), self.sem("r", i, u), to_in).wait_recv()
+            return buf
+
+        def outward(self, u):
+            own = self.own(u)
+            return remote(f.at[own], f.at[own], self.sem("u", 0, u), self.sem("t", 0, u), to_out)
+
+        def x_last(self, u):
+            own = self.own(u)
+            return remote(f.at[own], f.at[own], self.sem("xs", 0, u), self.sem("xr", 0, u), to_x)
+
+        def tick(self, t):
+            u, valid_u = self.unit(t, last * LAG)
+
+            def reduce():
+                def add():
+                    g[self.own(u), :] += self.arrived(u, 0)[...]
+
+                if H > 1:
+                    when(last > 0, add)
+                self.go(self.inward, u)
+
+            when(valid_u, reduce)
+            v, valid_v = self.unit(t, (2 * H - 1 - last) * LAG)
+
+            def finish():
+                def turn():
+                    f[self.own(v), :] = g[self.own(v), :] + self.arrived(v, 1)[...]
+
+                when(last == H - 1, turn)
+                if H > 1:
+                    when(last < H - 1, lambda: self.outward(v).wait_recv())
+                    when(last > 0, lambda: self.go(self.outward, v))
+                self.go(self.x_last, v)
+
+            when(valid_v, finish)
+            e, valid_e = self.unit(t, (2 * H - last) * LAG)
+            when(valid_e, lambda: self.x_last(e).wait_recv())
+
+        def drain(self):
+            self.end(self.inward)
+            self.end(self.x_last)
+            if H > 1:
+                when(last > 0, lambda: self.end(self.outward))
+
+    class B(Line):
+        def all(self, u):
+            return rows_at(b_base(u, 0), 4 * CH)
+
+        def half(self, u, i):
+            return rows_at(b_base(u, 0) + i * 2 * CH, 2 * CH)
+
+        def inward(self, u):
+            dst = R["bbuf"].at[self.slot(u, 4 * CH)]
+            return remote(g.at[self.all(u)], dst, self.sem("s", 0, u), self.sem("r", 0, u), to_in)
+
+        def swap(self, u):
+            dst = R["bsw"].at[self.slot(u, 2 * CH)]
+            return remote(g.at[self.half(u, 1 - side)], dst, self.sem("s", 0, u), self.sem("r", 1, u), to_in)
 
         def x_copy(self, u):
-            if self.two:
-                return self.copy(g.at[self.own(u)], R[self.kind + "xb"].at[self.d, self.slot(u)], "xs", "xr", u, to_x)
-            return self.copy(f.at[self.own(u)], f.at[self.own(u)], "xs", "xr", u, to_x)
-
-        def go(self, copy, u):
-            go(copy, u, self.flight)
-
-        def reduce(self, u):
-            w, root, own = self.w, self.root, self.own(u)
-
-            def from_low():
-                when(w < root, lambda: self.send_up(u).wait_recv())
-                when(w == root, lambda: self.send_up_root(u).wait_recv())
-                g[own, :] += self.lo[self.d, self.slot(u), :]
-
-            def from_high():
-                self.send_dn(u).wait_recv()
-                g[own, :] += self.hi[self.d, self.slot(u), :]
-
-            if root > 0:
-                when((w > 0) & (w <= root), from_low)
-            when((w < L - 1) & (w >= root), from_high)
-            if root > 1:
-                when(w < root - 1, lambda: self.go(self.send_up, u))
-            if root > 0:
-                when(w == root - 1, lambda: self.go(self.send_up_root, u))
-            when(w > root, lambda: self.go(self.send_dn, u))
-            if self.two:
-                when(w == root, lambda: self.go(self.x_copy, u))
-
-        def turn(self, u):
-            own = self.own(u)
-            if self.two:
-                self.x_copy(u).wait_recv()
-                f[own, :] = g[own, :] + R[self.kind + "xb"][self.d, self.slot(u), :]
-            else:
-                f[own, :] = g[own, :]
-            self.go(self.total_up, u)
-            if self.root > 0:
-                self.go(self.total_dn, u)
-            if not self.two:
-                self.go(self.x_copy, u)
-
-        def spread(self, u):
-            w, root = self.w, self.root
-            self.total_up(u).wait_recv()
-            when((w > root) & (w < L - 1), lambda: self.go(self.total_up, u))
-            if root > 1:
-                when((w < root) & (w > 0), lambda: self.go(self.total_dn, u))
-            if not self.two:
-                self.go(self.x_copy, u)
+            dst = R["bxb"].at[self.slot(u, 2 * CH)]
+            return remote(g.at[self.half(u, side)], dst, self.sem("xs", 0, u), self.sem("xr", 0, u), to_x)
+
+        def back(self, u):
+            own = self.half(u, side)
+            return remote(f.at[own], f.at[own], self.sem("d", 0, u), self.sem("r", 2, u), to_in)
+
+        def outward(self, u):
+            own = self.all(u)
+            return remote(f.at[own], f.at[own], self.sem("u", 0, u), self.sem("t", 0, u), to_out)
 
         def tick(self, t):
-            w, root = self.w, self.root
-            dist = jnp.abs(w - root) * LAG
-            u, valid = self.unit(t, self.depth * LAG - dist)
-            when(valid, lambda: self.reduce(u))
-            v, valid_v = self.unit(t, self.depth * LAG + self.gap)
-            when(valid_v & (w == root), lambda: self.turn(v))
-            q, valid_q = self.unit(t, self.depth * LAG + self.gap + dist)
-            when(valid_q & (w != root), lambda: self.spread(q))
-            if not self.two:
-                e, valid_e = self.unit(t, self.depth * LAG + self.gap + dist + LAG)
-                when(valid_e, lambda: self.x_copy(e).wait_recv())
+            u, valid_u = self.unit(t, last * LAG)
+
+            def reduce():
+                def add():
+                    self.inward(u).wait_recv()
+                    g[self.all(u), :] += R["bbuf"][self.slot(u, 4 * CH), :]
+
+                if H > 1:
+                    when(last > 0, add)
+                    when(last < H - 1, lambda: self.go(self.inward, u))
+                when(last == H - 1, lambda: self.go(self.swap, u))
+
+            when(valid_u, reduce)
+            middle = last == H - 1
+            i, valid_i = self.unit(t, H * LAG)
+
+            def over():
+                self.swap(i).wait_recv()
+                g[self.half(i, side), :] += R["bsw"][self.slot(i, 2 * CH), :]
+                self.go(self.x_copy, i)
+
+            when(valid_i & middle, over)
+            j, valid_j = self.unit(t, (H + 1) * LAG)
+
+            def total():
+                self.x_copy(j).wait_recv()
+                own = self.half(j, side)
+                f[own, :] = g[own, :] + R["bxb"][self.slot(j, 2 * CH), :]
+                self.go(self.back, j)
+
+            when(valid_j & middle, total)
+            v, valid_v = self.unit(t, (2 * H + 1 - last) * LAG)
+
+            def finish():
+                when(middle, lambda: self.back(v).wait_recv())
+                if H > 1:
+                    when(last < H - 1, lambda: self.outward(v).wait_recv())
+                    when(last > 0, lambda: self.go(self.outward, v))
+
+            when(valid_v, finish)
 
         def drain(self):
-            w, root, n, flight = self.w, self.root, self.n, self.flight
-            if root > 1:
-                when(w < root - 1, lambda: end(self.send_up, n, flight))
-            if root > 0:
-                when(w == root - 1, lambda: end(self.send_up_root, n, flight))
-                when((w <= root) & (w > 0), lambda: end(self.total_dn, n, flight))
-            when(w > root, lambda: end(self.send_dn, n, flight))
-            when((w >= root) & (w < L - 1), lambda: end(self.total_up, n, flight))
-            if self.two:
-                when(w == root, lambda: end(self.x_copy, n, flight))
-            else:
-                end(self.x_copy, n, flight)
-
-    ways = [Way(kind, d) for kind in ("c", "b", "a") for d in (0, 1)]
+            def ends():
+                for copy in (self.swap, self.x_copy, self.back):
+                    self.end(copy)
+
+            when(last == H - 1, ends)
+            if H > 1:
+                when(last < H - 1, lambda: self.end(self.inward))
+                when(last > 0, lambda: self.end(self.outward))
+
+    class C(Line):
+        def own(self, u, d):
+            return rows_at(b_base(u, 1) + d * 2 * CH, 2 * CH)
+
+        def place(self, d):
+            w = z if d == 0 else L - 1 - z
+            return w, (zhi if d == 0 else zlo, mp), (zlo if d == 0 else zhi, mp)
+
+        def copies(self, d):
+            w, up, dn = self.place(d)
+            own = lambda u: self.own(u, d)
+            slot = lambda u: self.slot(u, 2 * CH)
+
+            def send(u):
+                return remote(g.at[own(u)], R["cbuf"].at[d, slot(u)], self.sem("s", d, u), self.sem("r", d, u), dn)
+
+            def x_copy(u):
+                return remote(g.at[own(u)], R["cxb"].at[d, slot(u)], self.sem("xs", d, u), self.sem("xr", d, u), to_x)
+
+            def spread(u):
+                return remote(f.at[own(u)], f.at[own(u)], self.sem("u", d, u), self.sem("t", d, u), up)
+
+            return w, send, x_copy, spread
+
+        def tick(self, t):
+            for d in (0, 1):
+                w, send, x_copy, spread = self.copies(d)
+                u, valid_u = self.unit(t, (L - 1 - w) * LAG)
+
+                def reduce():
+                    def add():
+                        send(u).wait_recv()
+                        g[self.own(u, d), :] += R["cbuf"][d, self.slot(u, 2 * CH), :]
+
+                    when(w < L - 1, add)
+                    when(w > 0, lambda: self.go(send, u))
+                    when(w == 0, lambda: self.go(x_copy, u))
+
+                when(valid_u, reduce)
+                v, valid_v = self.unit(t, (L + w) * LAG)
+
+                def finish():
+                    def turn():
+                        x_copy(v).wait_recv()
+                        own = self.own(v, d)
+                        f[own, :] = g[own, :] + R["cxb"][d, self.slot(v, 2 * CH), :]
+
+                    when(w == 0, turn)
+                    when(w > 0, lambda: spread(v).wait_recv())
+                    when(w < L - 1, lambda: self.go(spread, v))
+
+                when(valid_v, finish)
+
+        def drain(self):
+            for d in (0, 1):
+                w, send, x_copy, spread = self.copies(d)
+                when(w > 0, lambda: self.end(send))
+                when(w == 0, lambda: self.end(x_copy))
+                when(w < L - 1, lambda: self.end(spread))
+
+    lines = [C("c", UC, 0, EACH, 2), B("b", UB, 1, EACH, 2), A("a", UA, AF, 1, SENDS)]
 
     def dp_tick(t):
-        when(t < UA, lambda: go(x_first, t, SENDS))
+        u = t - (AF - LAG)
+
+        def x_send():
+            when(u >= PU + SENDS, lambda: x_first(u - SENDS).wait_send())
+            x_first(u).start()
+
+        when((u >= PU) & (u < UA), x_send)
+        v = t - AF
 
         def x_add():
-            u = t - LAG
-            x_first(u).wait_recv()
-            s = pl.ds(pl.multiple_of(a_base(u) + x * 2 * CH, CH), 2 * CH)
-            g[s, :] += R["xrb"][x_slot(u), :]
-
-        when(ok(t - LAG, UA), x_add)
-        for way in ways:
-            way.tick(t)
+            x_first(v).wait_recv()
+            s = rows_at(a_base(v, x), 2 * CH)
+            g[s, :] += R["xrb"][x_slot(v), :]
+
+        when((v >= PU) & (v < UA), x_add)
+        for line in lines:
+            line.tick(t)
 
     def dp_drain():
         end(x_first, UA, SENDS)
-        for way in ways:
-            way.drain()
+        for line in lines:
+            line.drain()
 
     for copy in loads.values():
         copy.start()
@@ -499,8 +666,10 @@
         project(r)
         attend(r)
         sum_b(0, r)
-
-    for name in ("cot", "wdn", "wup"):
+        if PRE:
+            when(r == 0, cot_out)
+
+    for name in ("wdn", "wup") if PRE else ("cot", "wdn", "wup"):
         loads[name].wait()
     for i, name in enumerate(("outb", "n2g", "n2b", "upb", "dnb")):
         vector(2 + i, name)
@@ -512,14 +681,24 @@
         sum_c(0, r)
         sum_d(0, r)
         feed(r)
-
-    weight_grads(jnp.int32(0))
+        if PRE:
+            act_out(r)
+
+    if PRE:
+        cot_on()
+    weight_grads(jnp.int32(2 if PRE else 0))
 
     blocks = (2 * ff + 4 * loc) // blk
-    per = blk // (4 * CH)
-    a_last = LAG * (2 * D + 2)
-    b_last, c_last = LAG * (L + 1), LAG * (2 * L - 1)
-    ticks = max(UA + a_last, 3 * UB - 2 + b_last, 3 * UC - 1 + c_last)
+    a_last = AF + LAG * 2 * H
+    b_last, c_last = 1 + LAG * (2 * H + 1), LAG * (2 * L - 1)
+    ticks = max(UA - 1 + a_last, EACH * (UB - 1) + b_last, EACH * (UC - 1) + c_last) + 1
+
+    def done(j):
+        if PRE:
+            start = PU - 1 if j <= 2 else EACH * (j + 1) - 1
+        else:
+            start = (6 * j + 5) // (EACH + 2) * EACH + EACH - 1
+        return start + max(a_last, b_last, c_last)
 
     def out_copy(j):
         s = pl.ds(j * blk, blk if j < blocks else 4 * CH)
@@ -547,37 +726,40 @@
 
         at(3, 3, second)
         at(4, 3, lambda r: sum_b(2, r))
-        at(10, 3, lambda r: sum_c(2, r))
+        at(12, 3, lambda r: sum_c(2, r))
 
         def third(r):
             sum_d(2, r)
             back1(r)
 
-        at(11, 3, third)
-        at(12, 3, down)
-        at(13, 3, lambda r: sum_b(3, r))
-        at(18, 3, lambda r: sum_c(3, r))
+        at(13, 3, third)
+        at(14, 3, down)
+        at(15, 3, lambda r: sum_b(3, r))
+        at(21, 3, lambda r: sum_c(3, r))
 
         def fourth(r):
             sum_d(3, r)
             finish(r)
 
-        at(19, 3, fourth)
-
-        @pl.when(t == 19 + 3 * rows_n)
+        at(22, 3, fourth)
+
+        @pl.when(t == 22 + 3 * rows_n)
         def _():
             for copy in done_copies:
                 copy.start()
 
-        when((t % 3 == 1) & (t < 3 * blocks - 2), lambda: weight_grads((t + 2) // 3))
+        if PRE:
+            when(t == AF - 1, pair_grads)
+            when((rem(t, 4) == 2) & (t >= 6) & (t < 4 * blocks - 6), lambda: weight_grads(div(t + 6, 4)))
+        else:
+            when((rem(t, 3) == 1) & (t < 3 * blocks - 2), lambda: weight_grads(div(t + 2, 3)))
         for j in range(blocks):
-            done = (per * (j + 1) - 1) // 5 * 3 + 2 + max(a_last, c_last)
-            if done < ticks:
-                when(t == done, lambda: out_copy(j).start())
+            if done(j) < ticks:
+                when(t == done(j), lambda: out_copy(j).start())
 
     dp_drain()
     for j in range(blocks + 1):
-        if j == blocks or (per * (j + 1) - 1) // 5 * 3 + 2 + max(a_last, c_last) >= ticks:
+        if j == blocks or done(j) >= ticks:
             out_copy(j).start()
     for copy in done_copies + [out_copy(j) for j in range(blocks + 1)]:
         copy.wait()
@@ -592,19 +774,19 @@
     half = width // 2
     big = 2 * ff + 4 * loc
     count = big // (4 * CH) + 1
-    UC = count // 5
-    UB = UC + (count % 5) // 3
+    PU = 2 * loc // (4 * CH) if PRE else 0
+    rest = count - PU - 2 * (PU // EACH)
+    UC = PU // EACH + rest // (EACH + 2)
+    UB = UC + rest % (EACH + 2) // EACH
     UA = count - UB - UC
     L = n_dp // 2
     LAG = hop_ticks(L)
     vm = pltpu.VMEM
     dma = pltpu.SemaphoreType.DMA
-    W = LAG * L + 2
-    WX = 2 * LAG + 2
-    WB = LAG * (L + 1) // 3 + 2
-    WC = LAG * (2 * L - 1) // 3 + 2
+    W = two_power(max(LAG * (L - 1) + 1, 2 * LAG + 2))
+    WB = two_power(LAG * (L + 1) // EACH + 1)
+    WC = two_power(LAG * (2 * L - 1) // EACH + 1)
     total = count * 4 * CH
-    slots = lambda w, rows: vm((2, w * rows, width), F32)
     flat = lambda n: vm((n,), F32)
     scratch = dict(
         tok=vm((tokens, width), BF16),
@@ -647,23 +829,38 @@
         lt=vm((big, tokens), BF16),
         g=vm((total, width), F32),
         f=vm((total, width), F32),
-        xrb=vm((WX * 2 * CH, width), F32),
-        alo=slots(W, CH),
-        ahi=slots(W, CH),
-        blo=slots(WB, 2 * CH),
-        bhi=slots(WB, 2 * CH),
-        bxb=slots(WB, 2 * CH),
-        clo=slots(1, 2 * CH),
-        chi=slots(WC, 2 * CH),
-        cxb=slots(WC, 2 * CH),
+        xrb=vm((W * 2 * CH, width), F32),
+        abuf=vm((2, W * 2 * CH, width), F32),
+        bbuf=vm((WB * 4 * CH, width), F32),
+        bsw=vm((WB * 2 * CH, width), F32),
+        bxb=vm((WB * 2 * CH, width), F32),
+        cbuf=vm((2, WC * 2 * CH, width), F32),
+        cxb=vm((2, WC * 2 * CH, width), F32),
         **{s: dma((rows_n,)) for s in ("cs", "crs", "yss", "gs", "grs")},
         yrs=dma((2, rows_n)),
         fin=dma((big // loc + 4,)),
         xs=dma((SENDS,)),
-        xr=dma((WX,)),
-        **{k + "_" + s: dma((2, SENDS if k == "a" else 2)) for k in "abc" for s in ("s", "u", "d", "xs")},
-        **{k + "_" + s: dma((2, w)) for k, w in (("a", W), ("b", WB), ("c", WC)) for s in ("r", "t", "xr")},
+        xr=dma((W,)),
+        **{"a_" + s: dma((1, SENDS)) for s in ("s", "u", "xs")},
+        a_r=dma((2, W)),
+        **{"a_" + s: dma((1, W)) for s in ("t", "xr")},
+        **{"b_" + s: dma((1, 2)) for s in ("s", "u", "d", "xs")},
+        b_r=dma((3, WB)),
+        **{"b_" + s: dma((1, WB)) for s in ("t", "xr")},
+        **{"c_" + s: dma((2, 2)) for s in ("s", "u", "xs")},
+        **{"c_" + s: dma((2, WC)) for s in ("r", "t", "xr")},
     )
+    if PRE:
+        scratch.update(
+            cotf=vm((2, tokens // 4, width), F32),
+            cotr=vm((4, tokens // 4, width), F32),
+            cotx=vm((tokens, width), BF16),
+            actf=vm((rows_n, loc, seq), F32),
+            actr=vm((rows_n, loc, seq), F32),
+            ltx=vm((loc, tokens), BF16),
+            **{s: dma((2,)) for s in ("cxs", "cxr", "ccs", "ccr")},
+            **{s: dma((rows_n,)) for s in ("axs", "axr")},
+        )
     any_spec = pl.BlockSpec(memory_space=pl.ANY)
     vm_spec = pl.BlockSpec(memory_space=pltpu.VMEM)
     out, ig, tg, f = pl.pallas_call(

time: 164 us -> 163 us (level)
  Pallas kernels: 164 us -> 162 us
where the time goes in v6:
time: 163 us
  Pallas kernels  162 us (99%)
    pallas_call x1, Pallas kernels, shards(): pl.pallas_call(functools.partial(kernel, n_dp, (UA, UB, UC), tuple(scratc...  155 us
    pallas_call x1, Pallas kernels, shards(): pl.pallas_call(functools.partial(place, big), out_shape=moved + (f32(2, l...  7.27 us

profile of v6, /device:TPU:0, one launch (start us, length us, event | category | flops | bytes accessed | tf_op | source)
XLA Modules:
  0.0 163.1 jit_solution(14467434571547511460)
XLA Ops:
  0.7 155.2 %shard_map.271 = (bf16[512,768]{1,0:T(8,128)(2,1)}, bf16[512,768]{1,0:T(8,128)(2,1)}, f32[4,768]{1,0:T(4,128)}, f32[2336,768]{1,0:T(8,128)}) custom-call(bf16[512,768]{1,0:T(8,128)(2,1)} %refs_0_.1, bf16[4,768]{1,0:T(4,128)(2,1)} %refs_1_.1, s32[4,128]{1,0:T(4,128)} %refs_2_.1, f32[768]{0:T(1024)} %refs_3_.1, f32[768]{0:T(1024)} %refs_4_.1, ...), custom_call_target="tpu_custom_call" | custom-call | flops 6000000000 | bytes 20000000 | tf_op jit(solution)/shard_map/pallas_call | solution.py:866
  155.9 7.3 %shard_map.272 = (bf16[512,768]{1,0:T(8,128)(2,1)}, bf16[512,768]{1,0:T(8,128)(2,1)}, f32[4,768]{1,0:T(4,128)}, f32[3,192,768]{2,1,0:T(8,128)}, f32[192,768]{1,0...) custom-call(bf16[512,768]{1,0:T(8,128)(2,1)} %get-tuple-element.34.r, ...), custom_call_target="tpu_custom_call" | custom-call | tf_op jit(solution)/shard_map/pallas_call | solution.py:894

commit v7 on v6

--- a/solution.py
+++ b/solution.py
@@ -10,8 +10,8 @@
 HD = 64
 SUB = 128
 CH = 8
-PRE = False
-EACH = 4 if PRE else 3
+W_PIECES = 3
+EACH = 3
 SENDS = 4
 MESH = pl.DeviceIdType.MESH
 F32 = jnp.float32
@@ -198,14 +198,71 @@
         probs[sl(r, heads * seq), :] = pr
         mixed = from_heads(nn(pr.astype(BF16), v_s[sl(r), :])).astype(BF16)
         mixed_s[sl(r), :] = mixed
-        part[sl(r), :] = nn(mixed, wout[...])
-
-        @pl.when(r == 0)
-        def _():
-            pl.semaphore_wait(barrier, greeted)
-
-        core_copy(0, r).start()
-        lt[2 * ff : 2 * ff + loc, sl(r)] = mixed.T
+        turned = mixed.T
+        lt[2 * ff : 2 * ff + loc, sl(r)] = turned
+        mixa[mp, r] = turned.astype(F32)
+        m_core(r).start()
+        m_y(r).start()
+
+    wf, wall, mixa = R["wf"], R["wall"], R["mixa"]
+    mp_y, mp_c = rem(mp + 2, 4), mp + 1 - 2 * core
+    mine_0, other_0 = mp - core, mp_y - core
+    hl = loc // 2
+    pr_n = hl // W_PIECES
+
+    def w_core():
+        return remote(wf.at[mp], wf.at[mp], R["wcs"], R["wcr"], to_core)
+
+    def w_rows(start, n):
+        return pl.ds(pl.multiple_of(start, CH), n)
+
+    def w_y(i):
+        s = w_rows(x * hl + i * pr_n, pr_n)
+        return remote(wf.at[mp, s], wf.at[mp, s], R["wys"].at[i], R["wyr"].at[i], to_y)
+
+    def w_x(i):
+        s = w_rows(x * hl + i * pr_n, pr_n)
+        return remote(wf.at[mp_y, s], wf.at[mp_y, s], R["wxs"].at[i], R["wxr"].at[i], to_x)
+
+    def w_share(h):
+        s = w_rows((x + h - 2 * x * h) * hl, hl)
+        return remote(wf.at[mp_y, s], wf.at[mp_y, s], R["whs"].at[h], R["whr"].at[h], to_core)
+
+    def m_core(r):
+        return remote(mixa.at[mp, r], mixa.at[mp, r], R["cs"].at[r], R["crs"].at[r], to_core)
+
+    def m_y(r):
+        return remote(mixa.at[mp, r], mixa.at[mp, r], R["yss"].at[r], R["yrs"].at[0, r], to_y)
+
+    def m_share(r):
+        return remote(mixa.at[mp_y, r], mixa.at[mp_y, r], R["gs"].at[r], R["grs"].at[r], to_core)
+
+    def weights_out():
+        loads["wout"].wait()
+        wf[mp] = wout[...].astype(F32)
+        pl.semaphore_wait(barrier, greeted)
+        for i in range(W_PIECES):
+            w_y(i).start()
+        w_core().start()
+
+    def weights_on(i):
+        w_y(i).wait()
+        w_x(i).start()
+
+    def pair_sum(m, r):
+        return tn(mixa[m, r].astype(BF16), wall[m]) + tn(mixa[m + 1, r].astype(BF16), wall[m + 1])
+
+    def near_part(r):
+        m_core(r).wait()
+        part[sl(r), :] = pair_sum(mine_0, r)
+
+    def across(r):
+        m_y(r).wait()
+        m_share(r).start()
+
+    def far_part(r):
+        m_share(r).wait()
+        tot[sl(r), :] = part[sl(r), :] + pair_sum(other_0, r)
 
     def grad_act(r):
         c = cot[sl(r), :]
@@ -325,24 +382,19 @@
         for u in range(n - min(depth, n), n):
             copy(u).wait_send()
 
-    PU = 2 * loc // (4 * CH) if PRE else 0
-    PG = PU // EACH
-    AF = LAG + (1 if PRE else 0)
+    AF = LAG
 
     def base_of(u):
-        return (PU + u) * 4 * CH
+        return u * 4 * CH
 
     def later(u):
-        return base_of(2 * PG + div(u - PU, EACH) * (EACH + 2) + rem(u - PU, EACH))
+        return base_of(div(u, EACH) * (EACH + 2) + rem(u, EACH))
 
     def b_base(u, i):
-        rest = 2 * PG + (u - PG) * (EACH + 2) + EACH
-        u = jnp.where(u < PG, u * 2, rest) if PG else rest
-        return base_of(jnp.minimum(u + i, UA + UB + UC - PU - 1))
+        return base_of(jnp.minimum(u * (EACH + 2) + EACH + i, UA + UB + UC - 1))
 
     def a_base(u, owner):
-        rest = later(u) + owner * 2 * CH
-        return jnp.where(u < PU, owner * loc + u * 2 * CH, rest) if PU else rest
+        return later(u) + owner * 2 * CH
 
     def x_slot(u):
         return pl.ds(pl.multiple_of(rem(u, R["xr"].shape[0]) * 2 * CH, CH), 2 * CH)
@@ -352,47 +404,6 @@
         return remote(
             g.at[src], R["xrb"].at[x_slot(u)], R["xs"].at[rem(u, SENDS)], R["xr"].at[rem(u, R["xr"].shape[0])], to_x
         )
-
-    def cot_x(i):
-        s = core * 2 + i
-        return remote(R["cotf"].at[i], R["cotr"].at[s], R["cxs"].at[i], R["cxr"].at[i], to_x)
-
-    def cot_c(i):
-        s = core * 2 + i
-        return remote(R["cotr"].at[s], R["cotr"].at[s], R["ccs"].at[i], R["ccr"].at[i], to_core)
-
-    def act_x(r):
-        return remote(R["actf"].at[r], R["actr"].at[r], R["axs"].at[r], R["axr"].at[r], to_x)
-
-    def cot_out():
-        loads["cot"].wait()
-        n = R["cotf"].shape[1]
-        for i in range(2):
-            s = pl.ds(pl.multiple_of((core * 2 + i) * n, n), n)
-            R["cotf"][i] = cot[s, :].astype(F32)
-            cot_x(i).start()
-
-    def cot_on():
-        for i in range(2):
-            cot_x(i).wait()
-            cot_c(i).start()
-
-    def act_out(r):
-        s = pl.ds(pl.multiple_of((1 - x) * loc, loc), loc)
-        R["actf"][r] = lt[s, sl(r)].astype(F32)
-        act_x(r).start()
-
-    def pair_grads():
-        for i in range(2):
-            cot_c(i).wait()
-        cotx, n = R["cotx"], R["cotf"].shape[1]
-        for i in range(4):
-            cotx[i * n : (i + 1) * n, :] = R["cotr"][i].astype(BF16)
-        for r in range(rows_n):
-            act_x(r).wait()
-            R["ltx"][:, r * seq : (r + 1) * seq] = R["actr"][r].astype(BF16)
-        s = pl.ds(pl.multiple_of(x * loc, loc), loc)
-        g[s, :] = nn(lt[s, :], cot[...]) + nn(R["ltx"][...], cotx[...])
 
     def rows_at(base, n):
         return pl.ds(pl.multiple_of(base, CH), n)
@@ -617,13 +628,7 @@
     lines = [C("c", UC, 0, EACH, 2), B("b", UB, 1, EACH, 2), A("a", UA, AF, 1, SENDS)]
 
     def dp_tick(t):
-        u = t - (AF - LAG)
-
-        def x_send():
-            when(u >= PU + SENDS, lambda: x_first(u - SENDS).wait_send())
-            x_first(u).start()
-
-        when((u >= PU) & (u < UA), x_send)
+        when(t < UA, lambda: go(x_first, t, SENDS))
         v = t - AF
 
         def x_add():
@@ -631,7 +636,7 @@
             s = rows_at(a_base(v, x), 2 * CH)
             g[s, :] += R["xrb"][x_slot(v), :]
 
-        when((v >= PU) & (v < UA), x_add)
+        when((v >= 0) & (v < UA), x_add)
         for line in lines:
             line.tick(t)
 
@@ -660,33 +665,45 @@
 
         @pl.when(r == 0)
         def _():
-            for name in ("wqkv", "qvb", "seg", "wout"):
+            for name in ("wqkv", "qvb", "seg"):
                 loads[name].wait()
 
         project(r)
+        when(r == 0, weights_out)
         attend(r)
-        sum_b(0, r)
-        if PRE:
-            when(r == 0, cot_out)
-
-    for name in ("wdn", "wup") if PRE else ("cot", "wdn", "wup"):
+        for i in range(W_PIECES - 1):
+            when(r == rows_n - W_PIECES + 1 + i, lambda: weights_on(i))
+
+    for name in ("cot", "wdn", "wup"):
         loads[name].wait()
     for i, name in enumerate(("outb", "n2g", "n2b", "upb", "dnb")):
         vector(2 + i, name)
+    pl.loop(0, rows_n)(grad_act)
+    weights_on(W_PIECES - 1)
+    w_share(0).start()
+    w_core().wait()
+    for i in range(2):
+        wall[mine_0 + i] = wf[mine_0 + i].astype(BF16)
+    pl.loop(0, rows_n)(near_part)
+    ahead = min(2, rows_n)
+    for r in range(ahead):
+        across(r)
+    for i in range(W_PIECES):
+        w_x(i).wait()
+    w_share(1).start()
+    for h in range(2):
+        w_share(h).wait()
+    for i in range(2):
+        wall[other_0 + i] = wf[other_0 + i].astype(BF16)
 
     @pl.loop(0, rows_n)
     def _(r):
-        grad_act(r)
+        far_part(r)
+        feed(r)
+        when(r + ahead < rows_n, lambda: across(r + ahead))
         when(r > 0, lambda: sum_b(1, r - 1))
-        sum_c(0, r)
-        sum_d(0, r)
-        feed(r)
-        if PRE:
-            act_out(r)
-
-    if PRE:
-        cot_on()
-    weight_grads(jnp.int32(2 if PRE else 0))
+
+    weight_grads(jnp.int32(0))
 
     blocks = (2 * ff + 4 * loc) // blk
     a_last = AF + LAG * 2 * H
@@ -694,10 +711,7 @@
     ticks = max(UA - 1 + a_last, EACH * (UB - 1) + b_last, EACH * (UC - 1) + c_last) + 1
 
     def done(j):
-        if PRE:
-            start = PU - 1 if j <= 2 else EACH * (j + 1) - 1
-        else:
-            start = (6 * j + 5) // (EACH + 2) * EACH + EACH - 1
+        start = (6 * j + 5) // (EACH + 2) * EACH + EACH - 1
         return start + max(a_last, b_last, c_last)
 
     def out_copy(j):
@@ -748,11 +762,7 @@
             for copy in done_copies:
                 copy.start()
 
-        if PRE:
-            when(t == AF - 1, pair_grads)
-            when((rem(t, 4) == 2) & (t >= 6) & (t < 4 * blocks - 6), lambda: weight_grads(div(t + 6, 4)))
-        else:
-            when((rem(t, 3) == 1) & (t < 3 * blocks - 2), lambda: weight_grads(div(t + 2, 3)))
+        when((rem(t, 3) == 1) & (t < 3 * blocks - 2), lambda: weight_grads(div(t + 2, 3)))
         for j in range(blocks):
             if done(j) < ticks:
                 when(t == done(j), lambda: out_copy(j).start())
@@ -774,10 +784,8 @@
     half = width // 2
     big = 2 * ff + 4 * loc
     count = big // (4 * CH) + 1
-    PU = 2 * loc // (4 * CH) if PRE else 0
-    rest = count - PU - 2 * (PU // EACH)
-    UC = PU // EACH + rest // (EACH + 2)
-    UB = UC + rest % (EACH + 2) // EACH
+    UC = count // (EACH + 2)
+    UB = UC + count % (EACH + 2) // EACH
     UA = count - UB - UC
     L = n_dp // 2
     LAG = hop_ticks(L)
@@ -836,6 +844,13 @@
         bxb=vm((WB * 2 * CH, width), F32),
         cbuf=vm((2, WC * 2 * CH, width), F32),
         cxb=vm((2, WC * 2 * CH, width), F32),
+        wf=vm((4, loc, width), F32),
+        wall=vm((4, loc, width), BF16),
+        mixa=vm((4, rows_n, loc, seq), F32),
+        wcs=dma,
+        wcr=dma,
+        **{s: dma((W_PIECES,)) for s in ("wys", "wyr", "wxs", "wxr")},
+        **{s: dma((2,)) for s in ("whs", "whr")},
         **{s: dma((rows_n,)) for s in ("cs", "crs", "yss", "gs", "grs")},
         yrs=dma((2, rows_n)),
         fin=dma((big // loc + 4,)),
@@ -850,17 +865,6 @@
         **{"c_" + s: dma((2, 2)) for s in ("s", "u", "xs")},
         **{"c_" + s: dma((2, WC)) for s in ("r", "t", "xr")},
     )
-    if PRE:
-        scratch.update(
-            cotf=vm((2, tokens // 4, width), F32),
-            cotr=vm((4, tokens // 4, width), F32),
-            cotx=vm((tokens, width), BF16),
-            actf=vm((rows_n, loc, seq), F32),
-            actr=vm((rows_n, loc, seq), F32),
-            ltx=vm((loc, tokens), BF16),
-            **{s: dma((2,)) for s in ("cxs", "cxr", "ccs", "ccr")},
-            **{s: dma((rows_n,)) for s in ("axs", "axr")},
-        )
     any_spec = pl.BlockSpec(memory_space=pl.ANY)
     vm_spec = pl.BlockSpec(memory_space=pltpu.VMEM)
     out, ig, tg, f = pl.pallas_call(
@@ -895,15 +899,17 @@
         functools.partial(place, big),
         out_shape=moved + (f32(2, loc), f32(ff)) + (f32(width),) * 6,
         in_specs=[any_spec] * 4,
-        out_specs=(any_spec,) * 7 + (vm_spec,) * 8,
+        out_specs=(any_spec,) * 15,
         scratch_shapes=[
             vm((8, width), F32),
             vm((big, width), F32),
             vm((tokens, width), BF16),
             vm((tokens, width), BF16),
             vm((rows_n, width), F32),
-            dma((10,)),
-            dma((10,)),
+            vm((2, loc), F32),
+            *[vm((width,), F32)] * 7,
+            dma((18,)),
+            dma((26,)),
         ],
         compiler_params=pltpu.CompilerParams(vmem_limit_bytes=63 * 2**20),
     )(out, ig, tg, f)
@@ -913,30 +919,40 @@
 
 def place(big, *refs):
     out, ig, tg, f, out_o, ig_o, tg_o, qkv, outw, up, down, qvb, upb, downb = refs[:14]
-    n2g, n2b, outb, n1g, n1b, sm, buf, vo, vi, vt, sem, sem_o = refs[14:]
+    n2g, n2b, outb, n1g, n1b, sm, buf, vo, vi, vt, vq = refs[14:25]
+    flat = refs[25:32]
+    sem, sem_o = refs[32:]
     loc, ff = outw.shape[0], down.shape[0]
     half = f.shape[1] // 2
-    moves = []
+    moves = [(tg, vt, tg_o)]
     row = 0
     for n, ref in ((ff, down), (ff, up), (loc, outw), (loc, qkv.at[0]), (loc, qkv.at[1]), (loc, qkv.at[2])):
-        s = pl.ds(row, n)
-        moves.append((f.at[s], buf.at[s], ref))
-        row += n
-    moves += [(out, vo, out_o), (ig, vi, ig_o), (tg, vt, tg_o)]
-    first = pltpu.make_async_copy(f.at[pl.ds(big, 8)], sm, sem.at[9])
+        step = max(n * 12 // (2 * ff + 4 * loc), 1)
+        for i in range(step):
+            s = pl.ds(row, n // step)
+            moves.append((f.at[s], buf.at[s], ref.at[pl.ds(i * (n // step), n // step)]))
+            row += n // step
+    moves += [(out, vo, out_o), (ig, vi, ig_o)]
+    first = pltpu.make_async_copy(f.at[pl.ds(big, 8)], sm, sem.at[len(moves)])
     first.start()
     loads = [pltpu.make_async_copy(a, v, sem.at[i]) for i, (a, v, b) in enumerate(moves)]
     stores = [pltpu.make_async_copy(v, b, sem_o.at[i]) for i, (a, v, b) in enumerate(moves)]
-    for copy in loads:
+    for copy in loads[:20]:
         copy.start()
-    for load, store in zip(loads, stores):
+    first.wait()
+    small = (downb, upb, n2g, n2b, outb, n1g, n1b)
+    for i, ref in enumerate(flat):
+        ref[...] = sm[i : i + 1, :].reshape(ref.shape)
+    vq[0:1, :] = sm[7:8, 0:loc]
+    vq[1:2, :] = sm[7:8, half : half + loc]
+    for ref, o in zip(flat + (vq,), small + (qvb,)):
+        stores.append(pltpu.make_async_copy(ref, o, sem_o.at[len(stores)]))
+        stores[-1].start()
+    for i, load in enumerate(loads):
         load.wait()
-        store.start()
-    first.wait()
-    for i, ref in enumerate((downb, upb, n2g, n2b, outb, n1g, n1b)):
-        ref[...] = sm[i : i + 1, :].reshape(ref.shape)
-    qvb[0:1, :] = sm[7:8, 0:loc]
-    qvb[1:2, :] = sm[7:8, half : half + loc]
+        if i + 20 < len(loads):
+            loads[i + 20].start()
+        stores[i].start()
     for copy in stores:
         copy.wait()
 

time: 163 us -> 160 us (0.982)
  Pallas kernels: 162 us -> 159 us
    pallas_call x1, Pallas kernels: 155 us -> 152 us  [shards(): pl.pallas_call(functools.partial(kernel, n_dp, (UA, UB, UC), tuple(scratc...]
where the time goes in v7:
time: 160 us
  Pallas kernels  159 us (99%)
    pallas_call x1, Pallas kernels, shards(): pl.pallas_call(functools.partial(kernel, n_dp, (UA, UB, UC), tuple(scratc...  152 us
    pallas_call x1, Pallas kernels, shards(): pl.pallas_call(functools.partial(place, big), out_shape=moved + (f32(2, l...  7.03 us

profile of v7, /device:TPU:0, one launch (start us, length us, event | category | flops | bytes accessed | tf_op | source)
XLA Modules:
  0.0 160.0 jit_solution(15144209634154835130)
XLA Ops:
  0.7 152.3 %shard_map.271 = (bf16[512,768]{1,0:T(8,128)(2,1)}, bf16[512,768]{1,0:T(8,128)(2,1)}, f32[4,768]{1,0:T(4,128)}, f32[2336,768]{1,0:T(8,128)}) custom-call(bf16[512,768]{1,0:T(8,128)(2,1)} %refs_0_.1, bf16[4,768]{1,0:T(4,128)(2,1)} %refs_1_.1, s32[4,128]{1,0:T(4,128)} %refs_2_.1, f32[768]{0:T(1024)} %refs_3_.1, f32[768]{0:T(1024)} %refs_4_.1, ...), custom_call_target="tpu_custom_call" | custom-call | flops 6000000000 | bytes 20000000 | tf_op jit(solution)/shard_map/pallas_call | solution.py:870
  152.9 7.0 %shard_map.272 = (bf16[512,768]{1,0:T(8,128)(2,1)}, bf16[512,768]{1,0:T(8,128)(2,1)}, f32[4,768]{1,0:T(4,128)}, f32[3,192,768]{2,1,0:T(8,128)}, f32[192,768]{1,0...) custom-call(bf16[512,768]{1,0:T(8,128)(2,1)} %get-tuple-element.34.r, ...), custom_call_target="tpu_custom_call" | custom-call | tf_op jit(solution)/shard_map/pallas_call | solution.py:898

commit v8 on v7

--- a/solution.py
+++ b/solution.py
@@ -291,9 +291,11 @@
             gp[s, :] = pre
             small_add(1, colsum(pre.astype(F32)))
 
+        lt[0:ff, sl(r)] = act[sl(r), :].T
+
+    def feed_on(r):
         part[sl(r), :] = nt(gp[sl(r), :], wup[...])
         core_copy(1, r).start()
-        lt[0:ff, sl(r)] = act[sl(r), :].T
         lt[ff : 2 * ff, sl(r)] = e2[sl(r), :].T
 
     def back2(r):
@@ -701,7 +703,6 @@
         far_part(r)
         feed(r)
         when(r + ahead < rows_n, lambda: across(r + ahead))
-        when(r > 0, lambda: sum_b(1, r - 1))
 
     weight_grads(jnp.int32(0))
 
@@ -731,33 +732,34 @@
             r = (t - first) // step
             when((t >= first) & ((t - first) % step == 0) & (r < rows_n), lambda: fn(r))
 
-        when(t == 0, lambda: sum_b(1, rows_n - 1))
-        at(2, 3, lambda r: sum_c(1, r))
+        at(1, 1, lambda r: sum_b(1, r))
+        at(0, 1, feed_on)
+        at(5, 3, lambda r: sum_c(1, r))
 
         def second(r):
             sum_d(1, r)
             back2(r)
 
-        at(3, 3, second)
-        at(4, 3, lambda r: sum_b(2, r))
-        at(12, 3, lambda r: sum_c(2, r))
+        at(6, 3, second)
+        at(7, 3, lambda r: sum_b(2, r))
+        at(13, 3, lambda r: sum_c(2, r))
 
         def third(r):
             sum_d(2, r)
             back1(r)
 
-        at(13, 3, third)
-        at(14, 3, down)
-        at(15, 3, lambda r: sum_b(3, r))
-        at(21, 3, lambda r: sum_c(3, r))
+        at(14, 3, third)
+        at(15, 3, down)
+        at(16, 3, lambda r: sum_b(3, r))
+        at(22, 3, lambda r: sum_c(3, r))
 
         def fourth(r):
             sum_d(3, r)
             finish(r)
 
-        at(22, 3, fourth)
-
-        @pl.when(t == 22 + 3 * rows_n)
+        at(23, 3, fourth)
+
+        @pl.when(t == 23 + 3 * rows_n)
         def _():
             for copy in done_copies:
                 copy.start()

time: 160 us -> 159 us (level)
  no operation moved by 1% of the time
where the time goes in v8:
time: 159 us
  Pallas kernels  158 us (99%)
    pallas_call x1, Pallas kernels, shards(): pl.pallas_call(functools.partial(kernel, n_dp, (UA, UB, UC), tuple(scratc...  151 us
    pallas_call x1, Pallas kernels, shards(): pl.pallas_call(functools.partial(place, big), out_shape=moved + (f32(2, l...  7.03 us

profile of v8, /device:TPU:0, one launch (start us, length us, event | category | flops | bytes accessed | tf_op | source)
XLA Modules:
  0.0 158.6 jit_solution(6095042338402383162)
XLA Ops:
  0.7 150.9 %shard_map.271 = (bf16[512,768]{1,0:T(8,128)(2,1)}, bf16[512,768]{1,0:T(8,128)(2,1)}, f32[4,768]{1,0:T(4,128)}, f32[2336,768]{1,0:T(8,128)}) custom-call(bf16[512,768]{1,0:T(8,128)(2,1)} %refs_0_.1, bf16[4,768]{1,0:T(4,128)(2,1)} %refs_1_.1, s32[4,128]{1,0:T(4,128)} %refs_2_.1, f32[768]{0:T(1024)} %refs_3_.1, f32[768]{0:T(1024)} %refs_4_.1, ...), custom_call_target="tpu_custom_call" | custom-call | flops 6000000000 | bytes 20000000 | tf_op jit(solution)/shard_map/pallas_call | solution.py:872
  151.6 7.0 %shard_map.272 = (bf16[512,768]{1,0:T(8,128)(2,1)}, bf16[512,768]{1,0:T(8,128)(2,1)}, f32[4,768]{1,0:T(4,128)}, f32[3,192,768]{2,1,0:T(8,128)}, f32[192,768]{1,0...) custom-call(bf16[512,768]{1,0:T(8,128)(2,1)} %get-tuple-element.34.r, ...), custom_call_target="tpu_custom_call" | custom-call | tf_op jit(solution)/shard_map/pallas_call | solution.py:900

commit v9 on v8

--- a/solution.py
+++ b/solution.py
@@ -12,6 +12,7 @@
 CH = 8
 W_PIECES = 3
 EACH = 3
+S_FIRST = 30
 SENDS = 4
 MESH = pl.DeviceIdType.MESH
 F32 = jnp.float32
@@ -568,6 +569,8 @@
                 when(last > 0, lambda: self.end(self.outward))
 
     class C(Line):
+        dirs, rows = (0, 1), 2 * CH
+
         def own(self, u, d):
             return rows_at(b_base(u, 1) + d * 2 * CH, 2 * CH)
 
@@ -578,13 +581,13 @@
         def copies(self, d):
             w, up, dn = self.place(d)
             own = lambda u: self.own(u, d)
-            slot = lambda u: self.slot(u, 2 * CH)
+            slot = lambda u: self.slot(u, self.rows)
 
             def send(u):
-                return remote(g.at[own(u)], R["cbuf"].at[d, slot(u)], self.sem("s", d, u), self.sem("r", d, u), dn)
+                return remote(g.at[own(u)], R[self.kind + "buf"].at[d, slot(u)], self.sem("s", d, u), self.sem("r", d, u), dn)
 
             def x_copy(u):
-                return remote(g.at[own(u)], R["cxb"].at[d, slot(u)], self.sem("xs", d, u), self.sem("xr", d, u), to_x)
+                return remote(g.at[own(u)], R[self.kind + "xb"].at[d, slot(u)], self.sem("xs", d, u), self.sem("xr", d, u), to_x)
 
             def spread(u):
                 return remote(f.at[own(u)], f.at[own(u)], self.sem("u", d, u), self.sem("t", d, u), up)
@@ -592,14 +595,14 @@
             return w, send, x_copy, spread
 
         def tick(self, t):
-            for d in (0, 1):
+            for d in self.dirs:
                 w, send, x_copy, spread = self.copies(d)
                 u, valid_u = self.unit(t, (L - 1 - w) * LAG)
 
                 def reduce():
                     def add():
                         send(u).wait_recv()
-                        g[self.own(u, d), :] += R["cbuf"][d, self.slot(u, 2 * CH), :]
+                        g[self.own(u, d), :] += R[self.kind + "buf"][d, self.slot(u, self.rows), :]
 
                     when(w < L - 1, add)
                     when(w > 0, lambda: self.go(send, u))
@@ -612,7 +615,7 @@
                     def turn():
                         x_copy(v).wait_recv()
                         own = self.own(v, d)
-                        f[own, :] = g[own, :] + R["cxb"][d, self.slot(v, 2 * CH), :]
+                        f[own, :] = g[own, :] + R[self.kind + "xb"][d, self.slot(v, self.rows), :]
 
                     when(w == 0, turn)
                     when(w > 0, lambda: spread(v).wait_recv())
@@ -621,13 +624,19 @@
                 when(valid_v, finish)
 
         def drain(self):
-            for d in (0, 1):
+            for d in self.dirs:
                 w, send, x_copy, spread = self.copies(d)
                 when(w > 0, lambda: self.end(send))
                 when(w == 0, lambda: self.end(x_copy))
                 when(w < L - 1, lambda: self.end(spread))
 
-    lines = [C("c", UC, 0, EACH, 2), B("b", UB, 1, EACH, 2), A("a", UA, AF, 1, SENDS)]
+    class S(C):
+        dirs, rows = (0,), CH
+
+        def own(self, u, d):
+            return pl.ds(small, CH)
+
+    lines = [C("c", UC, 0, EACH, 2), A("a", UA, AF, 1, SENDS), B("b", UB, 1, EACH, 2), S("e", 1, S_FIRST, 1, 1)]
 
     def dp_tick(t):
         when(t < UA, lambda: go(x_first, t, SENDS))
@@ -654,7 +663,7 @@
         loads[name].wait()
         R["vecs"][i : i + 1, :] = R[name][...][None, :]
 
-    g[small : small + 4 * CH, :] = jnp.zeros((4 * CH, width), F32)
+    g[small : small + CH, :] = jnp.zeros((CH, width), F32)
     for name in ("tok", "tim"):
         loads[name].wait()
     timf[...] = tim[...].astype(F32)
@@ -709,14 +718,21 @@
     blocks = (2 * ff + 4 * loc) // blk
     a_last = AF + LAG * 2 * H
     b_last, c_last = 1 + LAG * (2 * H + 1), LAG * (2 * L - 1)
-    ticks = max(UA - 1 + a_last, EACH * (UB - 1) + b_last, EACH * (UC - 1) + c_last) + 1
+    ends = [S_FIRST + c_last]
+    for u in range(UA + UB + UC):
+        i, k = u // (EACH + 2), u % (EACH + 2)
+        if k < EACH and u < UA + UB + UC - (UB > UC):
+            ends.append(i * EACH + k + a_last)
+        else:
+            ends.append(i * EACH + c_last if k > EACH else (UB - 1 if k < EACH else i) * EACH + b_last)
+    ticks = max(ends) + 1
+    per = blk // (4 * CH)
 
     def done(j):
-        start = (6 * j + 5) // (EACH + 2) * EACH + EACH - 1
-        return start + max(a_last, b_last, c_last)
+        return ends[0] if j == blocks else max(ends[1 + j * per : 1 + (j + 1) * per])
 
     def out_copy(j):
-        s = pl.ds(j * blk, blk if j < blocks else 4 * CH)
+        s = pl.ds(j * blk, blk if j < blocks else CH)
         return pltpu.make_async_copy(f.at[s], f_out.at[s], R["fin"].at[j])
 
     done_copies = [
@@ -732,46 +748,46 @@
             r = (t - first) // step
             when((t >= first) & ((t - first) % step == 0) & (r < rows_n), lambda: fn(r))
 
-        at(1, 1, lambda r: sum_b(1, r))
-        at(0, 1, feed_on)
+        at(2, 2, lambda r: sum_b(1, r))
+        at(1, 2, feed_on)
         at(5, 3, lambda r: sum_c(1, r))
 
         def second(r):
             sum_d(1, r)
             back2(r)
 
-        at(6, 3, second)
-        at(7, 3, lambda r: sum_b(2, r))
-        at(13, 3, lambda r: sum_c(2, r))
+        at(7, 3, second)
+        at(9, 3, lambda r: sum_b(2, r))
+        at(15, 3, lambda r: sum_c(2, r))
 
         def third(r):
             sum_d(2, r)
             back1(r)
 
-        at(14, 3, third)
-        at(15, 3, down)
-        at(16, 3, lambda r: sum_b(3, r))
-        at(22, 3, lambda r: sum_c(3, r))
+        at(17, 3, third)
+        at(18, 3, down)
+        at(20, 3, lambda r: sum_b(3, r))
+        at(26, 3, lambda r: sum_c(3, r))
 
         def fourth(r):
             sum_d(3, r)
             finish(r)
 
-        at(23, 3, fourth)
-
-        @pl.when(t == 23 + 3 * rows_n)
+        at(28, 3, fourth)
+
+        @pl.when(t == 28 + 3 * rows_n)
         def _():
             for copy in done_copies:
                 copy.start()
 
         when((rem(t, 3) == 1) & (t < 3 * blocks - 2), lambda: weight_grads(div(t + 2, 3)))
-        for j in range(blocks):
-            if done(j) < ticks:
+        for j in range(blocks + 1):
+            if done(j) < ticks - 1:
                 when(t == done(j), lambda: out_copy(j).start())
 
     dp_drain()
     for j in range(blocks + 1):
-        if j == blocks or done(j) >= ticks:
+        if done(j) >= ticks - 1:
             out_copy(j).start()
     for copy in done_copies + [out_copy(j) for j in range(blocks + 1)]:
         copy.wait()
@@ -785,9 +801,9 @@
     heads = loc // HD
     half = width // 2
     big = 2 * ff + 4 * loc
-    count = big // (4 * CH) + 1
+    count = big // (4 * CH)
     UC = count // (EACH + 2)
-    UB = UC + count % (EACH + 2) // EACH
+    UB = UC + min(count % (EACH + 2) // 2, 1)
     UA = count - UB - UC
     L = n_dp // 2
     LAG = hop_ticks(L)
@@ -796,7 +812,7 @@
     W = two_power(max(LAG * (L - 1) + 1, 2 * LAG + 2))
     WB = two_power(LAG * (L + 1) // EACH + 1)
     WC = two_power(LAG * (2 * L - 1) // EACH + 1)
-    total = count * 4 * CH
+    total = big + CH
     flat = lambda n: vm((n,), F32)
     scratch = dict(
         tok=vm((tokens, width), BF16),
@@ -846,6 +862,9 @@
         bxb=vm((WB * 2 * CH, width), F32),
         cbuf=vm((2, WC * 2 * CH, width), F32),
         cxb=vm((2, WC * 2 * CH, width), F32),
+        ebuf=vm((1, CH, width), F32),
+        exb=vm((1, CH, width), F32),
+        **{"e_" + s: dma((1, 1)) for s in ("s", "u", "xs", "r", "t", "xr")},
         wf=vm((4, loc, width), F32),
         wall=vm((4, loc, width), BF16),
         mixa=vm((4, rows_n, loc, seq), F32),

time: 159 us -> 156 us (0.981)
  Pallas kernels: 158 us -> 155 us
    pallas_call x1, Pallas kernels: 151 us -> 148 us  [shards(): pl.pallas_call(functools.partial(kernel, n_dp, (UA, UB, UC), tuple(scratc...]
where the time goes in v9:
time: 156 us
  Pallas kernels  155 us (99%)
    pallas_call x1, Pallas kernels, shards(): pl.pallas_call(functools.partial(kernel, n_dp, (UA, UB, UC), tuple(scratc...  148 us
    pallas_call x1, Pallas kernels, shards(): pl.pallas_call(functools.partial(place, big), out_shape=moved + (f32(2, l...  7.03 us

profile of v9, /device:TPU:0, one launch (start us, length us, event | category | flops | bytes accessed | tf_op | source)
XLA Modules:
  0.0 156.0 jit_solution(10214102965501766879)
XLA Ops:
  0.7 148.3 %shard_map.271 = (bf16[512,768]{1,0:T(8,128)(2,1)}, bf16[512,768]{1,0:T(8,128)(2,1)}, f32[4,768]{1,0:T(4,128)}, f32[2312,768]{1,0:T(8,128)}) custom-call(bf16[512,768]{1,0:T(8,128)(2,1)} %refs_0_.1, bf16[4,768]{1,0:T(4,128)(2,1)} %refs_1_.1, s32[4,128]{1,0:T(4,128)} %refs_2_.1, f32[768]{0:T(1024)} %refs_3_.1, f32[768]{0:T(1024)} %refs_4_.1, ...), custom_call_target="tpu_custom_call" | custom-call | flops 6000000000 | bytes 20000000 | tf_op jit(solution)/shard_map/pallas_call | solution.py:891
  149.0 7.0 %shard_map.272 = (bf16[512,768]{1,0:T(8,128)(2,1)}, bf16[512,768]{1,0:T(8,128)(2,1)}, f32[4,768]{1,0:T(4,128)}, f32[3,192,768]{2,1,0:T(8,128)}, f32[192,768]{1,0...) custom-call(bf16[512,768]{1,0:T(8,128)(2,1)} %get-tuple-element.34.r, ...), custom_call_target="tpu_custom_call" | custom-call | tf_op jit(solution)/shard_map/pallas_call | solution.py:919

commit v10 on v9

--- a/solution.py
+++ b/solution.py
@@ -888,23 +888,27 @@
     )
     any_spec = pl.BlockSpec(memory_space=pl.ANY)
     vm_spec = pl.BlockSpec(memory_space=pltpu.VMEM)
+    operands = (tok, tim, seg, n1g, n1b, wqkv.transpose(0, 2, 1), qvb, wout, outb, n2g, n2b)
+    operands += (wup, upb, wdn, dnb, cot)
+    near = L <= 8
+    result = pltpu.VMEM if near else jax.ShapeDtypeStruct
     out, ig, tg, f = pl.pallas_call(
         functools.partial(kernel, n_dp, (UA, UB, UC), tuple(scratch)),
         out_shape=(
-            jax.ShapeDtypeStruct((tokens, width), BF16),
-            jax.ShapeDtypeStruct((tokens, width), BF16),
-            jax.ShapeDtypeStruct((rows_n, width), F32),
-            jax.ShapeDtypeStruct((total, width), F32),
+            result((tokens, width), BF16),
+            result((tokens, width), BF16),
+            result((rows_n, width), F32),
+            result((total, width), F32),
         ),
         in_specs=[any_spec] * 16,
-        out_specs=(any_spec,) * 4,
+        out_specs=(vm_spec if near else any_spec,) * 4,
         scratch_shapes=list(scratch.values()),
         compiler_params=pltpu.CompilerParams(
-            collective_id=0, has_side_effects=True, vmem_limit_bytes=63 * 2**20
+            collective_id=0, has_side_effects=True, vmem_limit_bytes=(52 if near else 63) * 2**20
         ),
         cost_estimate=pl.CostEstimate(flops=6 * 10**9, bytes_accessed=20 * 10**6, transcendentals=0),
     )(
-        tok, tim, seg, n1g, n1b, wqkv.transpose(0, 2, 1), qvb, wout, outb, n2g, n2b, wup, upb, wdn, dnb, cot
+        *[pltpu.with_memory_space_constraint(v, pltpu.HBM) for v in operands]
     )
     f32 = lambda *shape: jax.ShapeDtypeStruct(shape, F32)
     moved = (
@@ -917,63 +921,55 @@
         f32(ff, width),
     )
     results = pl.pallas_call(
-        functools.partial(place, big),
+        functools.partial(place, big, near),
         out_shape=moved + (f32(2, loc), f32(ff)) + (f32(width),) * 6,
-        in_specs=[any_spec] * 4,
+        in_specs=[vm_spec if near else any_spec] * 4,
         out_specs=(any_spec,) * 15,
         scratch_shapes=[
-            vm((8, width), F32),
-            vm((big, width), F32),
-            vm((tokens, width), BF16),
-            vm((tokens, width), BF16),
-            vm((rows_n, width), F32),
+            *([] if near else [vm((tokens, width), BF16), vm((tokens, width), BF16)]),
+            *([] if near else [vm((rows_n, width), F32), vm((total, width), F32)]),
             vm((2, loc), F32),
             *[vm((width,), F32)] * 7,
-            dma((18,)),
-            dma((26,)),
+            dma((4,)),
+            dma((17,)),
         ],
-        compiler_params=pltpu.CompilerParams(vmem_limit_bytes=63 * 2**20),
+        compiler_params=pltpu.CompilerParams(vmem_limit_bytes=(4 if near else 63) * 2**20),
     )(out, ig, tg, f)
     out, ig, tg, qkv, outw, up, down, qvb, upb, downb, n2g, n2b, outb, n1g, n1b = results
     return out, ig, tg, n1g, n1b, qkv.transpose(0, 2, 1), qvb, outw, outb, n2g, n2b, up, upb, down, downb
 
 
-def place(big, *refs):
-    out, ig, tg, f, out_o, ig_o, tg_o, qkv, outw, up, down, qvb, upb, downb = refs[:14]
-    n2g, n2b, outb, n1g, n1b, sm, buf, vo, vi, vt, vq = refs[14:25]
-    flat = refs[25:32]
-    sem, sem_o = refs[32:]
+def place(big, near, *refs):
+    results, outs = refs[:4], refs[4:19]
+    held = results if near else refs[19:23]
+    vq, *flat, sem, sem_o = refs[19 if near else 23 :]
+    out_o, ig_o, tg_o, qkv, outw, up, down, qvb, upb, downb, n2g, n2b, outb, n1g, n1b = outs
     loc, ff = outw.shape[0], down.shape[0]
-    half = f.shape[1] // 2
-    moves = [(tg, vt, tg_o)]
+    half = down.shape[1] // 2
+    if not near:
+        loads = [pltpu.make_async_copy(a, b, sem.at[i]) for i, (a, b) in enumerate(zip(results, held))]
+        for copy in loads:
+            copy.start()
+        for copy in loads:
+            copy.wait()
+    out, ig, tg, f = held
+    moves = []
     row = 0
     for n, ref in ((ff, down), (ff, up), (loc, outw), (loc, qkv.at[0]), (loc, qkv.at[1]), (loc, qkv.at[2])):
-        step = max(n * 12 // (2 * ff + 4 * loc), 1)
-        for i in range(step):
-            s = pl.ds(row, n // step)
-            moves.append((f.at[s], buf.at[s], ref.at[pl.ds(i * (n // step), n // step)]))
-            row += n // step
-    moves += [(out, vo, out_o), (ig, vi, ig_o)]
-    first = pltpu.make_async_copy(f.at[pl.ds(big, 8)], sm, sem.at[len(moves)])
-    first.start()
-    loads = [pltpu.make_async_copy(a, v, sem.at[i]) for i, (a, v, b) in enumerate(moves)]
-    stores = [pltpu.make_async_copy(v, b, sem_o.at[i]) for i, (a, v, b) in enumerate(moves)]
-    for copy in loads[:20]:
+        moves.append((f.at[pl.ds(row, n)], ref))
+        row += n
+    moves += [(out, out_o), (ig, ig_o), (tg, tg_o)]
+    small = (downb, upb, n2g, n2b, outb, n1g, n1b)
+    moves += [*zip(flat, small), (vq, qvb)]
+    stores = [pltpu.make_async_copy(a, b, sem_o.at[i]) for i, (a, b) in enumerate(moves)]
+    for copy in stores[:9]:
         copy.start()
-    first.wait()
-    small = (downb, upb, n2g, n2b, outb, n1g, n1b)
     for i, ref in enumerate(flat):
-        ref[...] = sm[i : i + 1, :].reshape(ref.shape)
-    vq[0:1, :] = sm[7:8, 0:loc]
-    vq[1:2, :] = sm[7:8, half : half + loc]
-    for ref, o in zip(flat + (vq,), small + (qvb,)):
-        stores.append(pltpu.make_async_copy(ref, o, sem_o.at[len(stores)]))
-        stores[-1].start()
-    for i, load in enumerate(loads):
-        load.wait()
-        if i + 20 < len(loads):
-            loads[i + 20].start()
-        stores[i].start()
+        ref[...] = f[big + i : big + i + 1, :].reshape(ref.shape)
+    vq[0:1, :] = f[big + 7 : big + 8, 0:loc]
+    vq[1:2, :] = f[big + 7 : big + 8, half : half + loc]
+    for copy in stores[9:]:
+        copy.start()
     for copy in stores:
         copy.wait()
 

time: 156 us -> 152 us (0.974)
  Pallas kernels: 155 us -> 151 us
    pallas_call x1, Pallas kernels: 7.03 us -> 3.59 us  [shards(): pl.pallas_call(functools.partial(place, big, near), out_shape=moved + (f3...]
where the time goes in v10:
time: 152 us
  Pallas kernels  151 us (99%)
    pallas_call x1, Pallas kernels, shards(): pl.pallas_call(functools.partial(kernel, n_dp, (UA, UB, UC), tuple(scratc...  148 us
    pallas_call x1, Pallas kernels, shards(): pl.pallas_call(functools.partial(place, big, near), out_shape=moved + (f3...  3.59 us

profile of v10, /device:TPU:0, one launch (start us, length us, event | category | flops | bytes accessed | tf_op | source)
XLA Modules:
  0.0 151.9 jit_solution(18167538937840644852)
XLA Ops:
  0.7 147.7 %shard_map.271 = (bf16[512,768]{1,0:T(8,128)(2,1)S(1)}, bf16[512,768]{1,0:T(8,128)(2,1)S(1)}, f32[4,768]{1,0:T(4,128)S(1)}, f32[2312,768]{1,0:T(8,128)S(1)}) custom-call(bf16[512,768]{1,0:T(8,128)(2,1)} %refs_0_.1, bf16[4,768]{1,0:T(4,128)(2,1)} %refs_1_.1, s32[4,128]{1,0:T(4,128)} %refs_2_.1, f32[768]{0:T(1024)} %refs_3_.1, f32[768]{0:T(1024)} %refs_4_.1, ...), custom_call_target="tpu_custom_call" | custom-call | flops 6000000000 | bytes 20000000 | tf_op jit(solution)/shard_map/pallas_call | solution.py:895
  148.3 3.6 %shard_map.272 = (bf16[512,768]{1,0:T(8,128)(2,1)}, bf16[512,768]{1,0:T(8,128)(2,1)}, f32[4,768]{1,0:T(4,128)}, f32[3,192,768]{2,1,0:T(8,128)}, f32[192,768]{1,0...) custom-call(bf16[512,768]{1,0:T(8,128)(2,1)S(1)} %get-tuple-element., ...), custom_call_target="tpu_custom_call" | custom-call | tf_op jit(solution)/shard_map/pallas_call | solution.py:923

commit v11 on v10

--- a/solution.py
+++ b/solution.py
@@ -66,7 +66,7 @@
     return jnp.sum(v, 0, keepdims=True)
 
 
-def kernel(n_dp, units, names, *refs):
+def kernel(n_dp, near, units, names, *refs):
     out_o, ig_o, tg_o, f_out = refs[16:20]
     R = dict(zip(names, refs[20:]))
     order = ("tok", "tim", "n1g", "n1b", "wqkv", "qvb", "seg", "wout", "outb", "cot", "wdn")
@@ -81,8 +81,9 @@
     timf, start, entry, q_s, k_s, v_s = (R[s] for s in ("timf", "start", "entry", "q", "k", "v"))
     probs, mixed_s, part, cr, ys, yr = (R[s] for s in ("probs", "mixed", "part", "cr", "ys", "yr"))
     tot, mid, e2, hp, act, gp = (R[s] for s in ("tot", "mid", "e2", "hp", "act", "gp"))
-    out, ig, tg = (R[s] for s in ("out", "ig", "tg"))
-    gact, gmid, gbr, lt, g, f = (R[s] for s in ("gact", "gmid", "gbr", "lt", "g", "f"))
+    out, ig, tg = (out_o, ig_o, tg_o) if near else (R[s] for s in ("out", "ig", "tg"))
+    gact, gmid, gbr, lt, g = (R[s] for s in ("gact", "gmid", "gbr", "lt", "g"))
+    f = f_out if near else R["f"]
 
     rows_n, seq = seg.shape
     width = tok.shape[1]
@@ -449,7 +450,7 @@
 
         def outward(self, u):
             own = self.own(u)
-            return remote(f.at[own], f.at[own], self.sem("u", 0, u), self.sem("t", 0, u), to_out)
+            return remote(f.at[own], f.at[own], self.sem("u", 0, u), self.sem("r", 1, u), to_out)
 
         def x_last(self, u):
             own = self.own(u)
@@ -514,7 +515,7 @@
 
         def outward(self, u):
             own = self.all(u)
-            return remote(f.at[own], f.at[own], self.sem("u", 0, u), self.sem("t", 0, u), to_out)
+            return remote(f.at[own], f.at[own], self.sem("u", 0, u), self.sem("r", 1, u), to_out)
 
         def tick(self, t):
             u, valid_u = self.unit(t, last * LAG)
@@ -587,7 +588,7 @@
                 return remote(g.at[own(u)], R[self.kind + "buf"].at[d, slot(u)], self.sem("s", d, u), self.sem("r", d, u), dn)
 
             def x_copy(u):
-                return remote(g.at[own(u)], R[self.kind + "xb"].at[d, slot(u)], self.sem("xs", d, u), self.sem("xr", d, u), to_x)
+                return remote(g.at[own(u)], R[self.kind + "xb"].at[d, slot(u)], self.sem("s", d, u), self.sem("t", d, u), to_x)
 
             def spread(u):
                 return remote(f.at[own(u)], f.at[own(u)], self.sem("u", d, u), self.sem("t", d, u), up)
@@ -735,7 +736,7 @@
         s = pl.ds(j * blk, blk if j < blocks else CH)
         return pltpu.make_async_copy(f.at[s], f_out.at[s], R["fin"].at[j])
 
-    done_copies = [
+    done_copies = [] if near else [
         pltpu.make_async_copy(a, b, R["fin"].at[blocks + 1 + i])
         for i, (a, b) in enumerate(((ig, ig_o), (tg, tg_o), (out, out_o)))
     ]
@@ -781,15 +782,16 @@
                 copy.start()
 
         when((rem(t, 3) == 1) & (t < 3 * blocks - 2), lambda: weight_grads(div(t + 2, 3)))
-        for j in range(blocks + 1):
+        for j in range(0 if near else blocks + 1):
             if done(j) < ticks - 1:
                 when(t == done(j), lambda: out_copy(j).start())
 
     dp_drain()
-    for j in range(blocks + 1):
+    left = 0 if near else blocks + 1
+    for j in range(left):
         if done(j) >= ticks - 1:
             out_copy(j).start()
-    for copy in done_copies + [out_copy(j) for j in range(blocks + 1)]:
+    for copy in done_copies + [out_copy(j) for j in range(left)]:
         copy.wait()
 
 
@@ -807,6 +809,7 @@
     UA = count - UB - UC
     L = n_dp // 2
     LAG = hop_ticks(L)
+    near = L <= 8
     vm = pltpu.VMEM
     dma = pltpu.SemaphoreType.DMA
     W = two_power(max(LAG * (L - 1) + 1, 2 * LAG + 2))
@@ -849,12 +852,11 @@
         gact=vm((tokens, ff), F32),
         gmid=vm((tokens, width), F32),
         gbr=vm((tokens, width), BF16),
-        out=vm((tokens, width), BF16),
-        ig=vm((tokens, width), BF16),
-        tg=vm((rows_n, width), F32),
+        **{n: vm((tokens, width), BF16) for n in (() if near else ("out", "ig"))},
+        **({} if near else dict(tg=vm((rows_n, width), F32))),
         lt=vm((big, tokens), BF16),
         g=vm((total, width), F32),
-        f=vm((total, width), F32),
+        **({} if near else dict(f=vm((total, width), F32))),
         xrb=vm((W * 2 * CH, width), F32),
         abuf=vm((2, W * 2 * CH, width), F32),
         bbuf=vm((WB * 4 * CH, width), F32),
@@ -864,7 +866,7 @@
         cxb=vm((2, WC * 2 * CH, width), F32),
         ebuf=vm((1, CH, width), F32),
         exb=vm((1, CH, width), F32),
-        **{"e_" + s: dma((1, 1)) for s in ("s", "u", "xs", "r", "t", "xr")},
+        **{"e_" + s: dma((1, 1)) for s in ("s", "u", "r", "t")},
         wf=vm((4, loc, width), F32),
         wall=vm((4, loc, width), BF16),
         mixa=vm((4, rows_n, loc, seq), F32),
@@ -874,26 +876,25 @@
         **{s: dma((2,)) for s in ("whs", "whr")},
         **{s: dma((rows_n,)) for s in ("cs", "crs", "yss", "gs", "grs")},
         yrs=dma((2, rows_n)),
-        fin=dma((big // loc + 4,)),
+        **({} if near else dict(fin=dma((big // loc + 4,)))),
         xs=dma((SENDS,)),
         xr=dma((W,)),
         **{"a_" + s: dma((1, SENDS)) for s in ("s", "u", "xs")},
         a_r=dma((2, W)),
-        **{"a_" + s: dma((1, W)) for s in ("t", "xr")},
+        a_xr=dma((1, W)),
         **{"b_" + s: dma((1, 2)) for s in ("s", "u", "d", "xs")},
         b_r=dma((3, WB)),
-        **{"b_" + s: dma((1, WB)) for s in ("t", "xr")},
-        **{"c_" + s: dma((2, 2)) for s in ("s", "u", "xs")},
-        **{"c_" + s: dma((2, WC)) for s in ("r", "t", "xr")},
+        b_xr=dma((1, WB)),
+        **{"c_" + s: dma((2, 2)) for s in ("s", "u")},
+        **{"c_" + s: dma((2, WC)) for s in ("r", "t")},
     )
     any_spec = pl.BlockSpec(memory_space=pl.ANY)
     vm_spec = pl.BlockSpec(memory_space=pltpu.VMEM)
     operands = (tok, tim, seg, n1g, n1b, wqkv.transpose(0, 2, 1), qvb, wout, outb, n2g, n2b)
     operands += (wup, upb, wdn, dnb, cot)
-    near = L <= 8
     result = pltpu.VMEM if near else jax.ShapeDtypeStruct
     out, ig, tg, f = pl.pallas_call(
-        functools.partial(kernel, n_dp, (UA, UB, UC), tuple(scratch)),
+        functools.partial(kernel, n_dp, near, (UA, UB, UC), tuple(scratch)),
         out_shape=(
             result((tokens, width), BF16),
             result((tokens, width), BF16),

time: 152 us -> 151 us (level)
  no operation moved by 1% of the time
where the time goes in v11:
time: 151 us
  Pallas kernels  151 us (100%)
    pallas_call x1, Pallas kernels, shards(): pl.pallas_call(functools.partial(kernel, n_dp, near, (UA, UB, UC), tuple(...  147 us
    pallas_call x1, Pallas kernels, shards(): pl.pallas_call(functools.partial(place, big, near), out_shape=moved + (f3...  3.59 us

profile of v11, /device:TPU:0, one launch (start us, length us, event | category | flops | bytes accessed | tf_op | source)
XLA Modules:
  0.0 151.3 jit_solution(3984955198155457809)
XLA Ops:
  0.7 147.1 %shard_map.271 = (bf16[512,768]{1,0:T(8,128)(2,1)S(1)}, bf16[512,768]{1,0:T(8,128)(2,1)S(1)}, f32[4,768]{1,0:T(4,128)S(1)}, f32[2312,768]{1,0:T(8,128)S(1)}) custom-call(bf16[512,768]{1,0:T(8,128)(2,1)} %refs_0_.1, bf16[4,768]{1,0:T(4,128)(2,1)} %refs_1_.1, s32[4,128]{1,0:T(4,128)} %refs_2_.1, f32[768]{0:T(1024)} %refs_3_.1, f32[768]{0:T(1024)} %refs_4_.1, ...), custom_call_target="tpu_custom_call" | custom-call | flops 6000000000 | bytes 20000000 | tf_op jit(solution)/shard_map/pallas_call | solution.py:896
  147.7 3.6 %shard_map.272 = (bf16[512,768]{1,0:T(8,128)(2,1)}, bf16[512,768]{1,0:T(8,128)(2,1)}, f32[4,768]{1,0:T(4,128)}, f32[3,192,768]{2,1,0:T(8,128)}, f32[192,768]{1,0...) custom-call(bf16[512,768]{1,0:T(8,128)(2,1)S(1)} %get-tuple-element., ...), custom_call_target="tpu_custom_call" | custom-call | tf_op jit(solution)/shard_map/pallas_call | solution.py:924

commit v12 on v11

--- a/solution.py
+++ b/solution.py
@@ -10,7 +10,7 @@
 HD = 64
 SUB = 128
 CH = 8
-W_PIECES = 3
+W_PIECES = 2
 EACH = 3
 S_FIRST = 30
 SENDS = 4
@@ -209,8 +209,11 @@
     wf, wall, mixa = R["wf"], R["wall"], R["mixa"]
     mp_y, mp_c = rem(mp + 2, 4), mp + 1 - 2 * core
     mine_0, other_0 = mp - core, mp_y - core
-    hl = loc // 2
+    hl = loc // 4
     pr_n = hl // W_PIECES
+    zz = rem(z, 2)
+    quarter = zz * 2 + x
+    to_zz = ((z + 1 - 2 * zz) * 2 + x, mp)
 
     def w_core():
         return remote(wf.at[mp], wf.at[mp], R["wcs"], R["wcr"], to_core)
@@ -219,15 +222,20 @@
         return pl.ds(pl.multiple_of(start, CH), n)
 
     def w_y(i):
-        s = w_rows(x * hl + i * pr_n, pr_n)
+        s = w_rows(quarter * hl + i * pr_n, pr_n)
         return remote(wf.at[mp, s], wf.at[mp, s], R["wys"].at[i], R["wyr"].at[i], to_y)
 
     def w_x(i):
-        s = w_rows(x * hl + i * pr_n, pr_n)
+        s = w_rows(quarter * hl + i * pr_n, pr_n)
         return remote(wf.at[mp_y, s], wf.at[mp_y, s], R["wxs"].at[i], R["wxr"].at[i], to_x)
 
+    def w_z(k, i):
+        s = w_rows((zz * 2 + (x + k - 2 * x * k)) * hl + i * pr_n, pr_n)
+        j = k * W_PIECES + i
+        return remote(wf.at[mp_y, s], wf.at[mp_y, s], R["wzs"].at[j], R["wzr"].at[j], to_zz)
+
     def w_share(h):
-        s = w_rows((x + h - 2 * x * h) * hl, hl)
+        s = w_rows((zz + h - 2 * zz * h) * 2 * hl, 2 * hl)
         return remote(wf.at[mp_y, s], wf.at[mp_y, s], R["whs"].at[h], R["whr"].at[h], to_core)
 
     def m_core(r):
@@ -250,6 +258,7 @@
     def weights_on(i):
         w_y(i).wait()
         w_x(i).start()
+        w_z(0, i).start()
 
     def pair_sum(m, r):
         return tn(mixa[m, r].astype(BF16), wall[m]) + tn(mixa[m + 1, r].astype(BF16), wall[m + 1])
@@ -271,21 +280,20 @@
         gact[sl(r), :] = nt(c, wdn[...])
         small_add(0, colsum(c.astype(F32)))
 
-    def feed(r):
-        @pl.loop(0, seq // SUB)
-        def _(i):
-            s = sub(r, i)
+    def feed(k):
+        both = sl(k, 2 * seq)
+        for i in range(2):
+            s = sl(k * 2 + i)
             v = start[s, :] + (tot[s, :] + outb[...])
             mid[s, :] = v
             xhat, _ = normed(v)
             e2[s, :] = (xhat * n2g[...] + n2b[...]).astype(BF16)
 
-        hp[...] = nn(e2[sl(r), :], wup[...])
-
-        @pl.loop(0, seq // SUB)
-        def _(i):
-            s = sub(r, i)
-            u = hp[pl.ds(pl.multiple_of(i * SUB, SUB), SUB), :] + upb[...]
+        hp[...] = nn(e2[both, :], wup[...])
+
+        for i in range(2):
+            s = sl(k * 2 + i)
+            u = hp[i * seq : (i + 1) * seq, :] + upb[...]
             cdf = 0.5 * (1.0 + lax.erf(u * 0.7071067811865476))
             act[s, :] = (u * cdf).astype(BF16)
             slope = cdf + u * (0.3989422804014327 * jnp.exp(-0.5 * u * u))
@@ -293,7 +301,7 @@
             gp[s, :] = pre
             small_add(1, colsum(pre.astype(F32)))
 
-        lt[0:ff, sl(r)] = act[sl(r), :].T
+        lt[0:ff, both] = act[both, :].T
 
     def feed_on(r):
         part[sl(r), :] = nt(gp[sl(r), :], wup[...])
@@ -683,36 +691,41 @@
         project(r)
         when(r == 0, weights_out)
         attend(r)
-        for i in range(W_PIECES - 1):
-            when(r == rows_n - W_PIECES + 1 + i, lambda: weights_on(i))
+        for i in range(W_PIECES):
+            when(r == rows_n - W_PIECES - 1 + i, lambda: weights_on(i))
 
     for name in ("cot", "wdn", "wup"):
         loads[name].wait()
     for i, name in enumerate(("outb", "n2g", "n2b", "upb", "dnb")):
         vector(2 + i, name)
-    pl.loop(0, rows_n)(grad_act)
-    weights_on(W_PIECES - 1)
-    w_share(0).start()
+    w_x(0).wait()
+    w_z(1, 0).start()
     w_core().wait()
     for i in range(2):
         wall[mine_0 + i] = wf[mine_0 + i].astype(BF16)
-    pl.loop(0, rows_n)(near_part)
-    ahead = min(2, rows_n)
-    for r in range(ahead):
-        across(r)
-    for i in range(W_PIECES):
+    pl.loop(0, rows_n // 2)(near_part)
+    for i in range(1, W_PIECES):
         w_x(i).wait()
+        w_z(1, i).start()
+    w_share(0).start()
+    pl.loop(0, rows_n)(grad_act)
+    pl.loop(rows_n // 2, rows_n)(near_part)
+    pl.loop(0, rows_n - 1)(across)
+    for k in range(2):
+        for i in range(W_PIECES):
+            w_z(k, i).wait()
     w_share(1).start()
+    across(rows_n - 1)
     for h in range(2):
         w_share(h).wait()
     for i in range(2):
         wall[other_0 + i] = wf[other_0 + i].astype(BF16)
 
-    @pl.loop(0, rows_n)
-    def _(r):
-        far_part(r)
-        feed(r)
-        when(r + ahead < rows_n, lambda: across(r + ahead))
+    @pl.loop(0, rows_n // 2)
+    def _(k):
+        for i in range(2):
+            far_part(k * 2 + i)
+        feed(k)
 
     weight_grads(jnp.int32(0))
 
@@ -846,7 +859,7 @@
         tot=vm((tokens, width), F32),
         mid=vm((tokens, width), F32),
         e2=vm((tokens, width), BF16),
-        hp=vm((seq, ff), F32),
+        hp=vm((2 * seq, ff), F32),
         act=vm((tokens, ff), BF16),
         gp=vm((tokens, ff), BF16),
         gact=vm((tokens, ff), F32),
@@ -873,6 +886,7 @@
         wcs=dma,
         wcr=dma,
         **{s: dma((W_PIECES,)) for s in ("wys", "wyr", "wxs", "wxr")},
+        **{s: dma((2 * W_PIECES,)) for s in ("wzs", "wzr")},
         **{s: dma((2,)) for s in ("whs", "whr")},
         **{s: dma((rows_n,)) for s in ("cs", "crs", "yss", "gs", "grs")},
         yrs=dma((2, rows_n)),

time: 151 us -> 150 us (level)
  no operation moved by 1% of the time
where the time goes in v12:
time: 150 us
  Pallas kernels  150 us (100%)
    pallas_call x1, Pallas kernels, shards(): pl.pallas_call(functools.partial(kernel, n_dp, near, (UA, UB, UC), tuple(...  146 us
    pallas_call x1, Pallas kernels, shards(): pl.pallas_call(functools.partial(place, big, near), out_shape=moved + (f3...  3.59 us

profile of v12, /device:TPU:0, one launch (start us, length us, event | category | flops | bytes accessed | tf_op | source)
XLA Modules:
  0.0 150.3 jit_solution(8378057416893851576)
XLA Ops:
  0.7 146.1 %shard_map.271 = (bf16[512,768]{1,0:T(8,128)(2,1)S(1)}, bf16[512,768]{1,0:T(8,128)(2,1)S(1)}, f32[4,768]{1,0:T(4,128)S(1)}, f32[2312,768]{1,0:T(8,128)S(1)}) custom-call(bf16[512,768]{1,0:T(8,128)(2,1)} %refs_0_.1, bf16[4,768]{1,0:T(4,128)(2,1)} %refs_1_.1, s32[4,128]{1,0:T(4,128)} %refs_2_.1, f32[768]{0:T(1024)} %refs_3_.1, f32[768]{0:T(1024)} %refs_4_.1, ...), custom_call_target="tpu_custom_call" | custom-call | flops 6000000000 | bytes 20000000 | tf_op jit(solution)/shard_map/pallas_call | solution.py:910
  146.7 3.6 %shard_map.272 = (bf16[512,768]{1,0:T(8,128)(2,1)}, bf16[512,768]{1,0:T(8,128)(2,1)}, f32[4,768]{1,0:T(4,128)}, f32[3,192,768]{2,1,0:T(8,128)}, f32[192,768]{1,0...) custom-call(bf16[512,768]{1,0:T(8,128)(2,1)S(1)} %get-tuple-element., ...), custom_call_target="tpu_custom_call" | custom-call | tf_op jit(solution)/shard_map/pallas_call | solution.py:938

commit v13 on v12

--- a/solution.py
+++ b/solution.py
@@ -281,9 +281,9 @@
         small_add(0, colsum(c.astype(F32)))
 
     def feed(k):
-        both = sl(k, 2 * seq)
-        for i in range(2):
-            s = sl(k * 2 + i)
+        both = sl(k, 4 * seq)
+        for i in range(4):
+            s = sl(k * 4 + i)
             v = start[s, :] + (tot[s, :] + outb[...])
             mid[s, :] = v
             xhat, _ = normed(v)
@@ -291,8 +291,8 @@
 
         hp[...] = nn(e2[both, :], wup[...])
 
-        for i in range(2):
-            s = sl(k * 2 + i)
+        for i in range(4):
+            s = sl(k * 4 + i)
             u = hp[i * seq : (i + 1) * seq, :] + upb[...]
             cdf = 0.5 * (1.0 + lax.erf(u * 0.7071067811865476))
             act[s, :] = (u * cdf).astype(BF16)
@@ -721,10 +721,10 @@
     for i in range(2):
         wall[other_0 + i] = wf[other_0 + i].astype(BF16)
 
-    @pl.loop(0, rows_n // 2)
+    @pl.loop(0, rows_n // 4)
     def _(k):
-        for i in range(2):
-            far_part(k * 2 + i)
+        for i in range(4):
+            far_part(k * 4 + i)
         feed(k)
 
     weight_grads(jnp.int32(0))
@@ -859,7 +859,7 @@
         tot=vm((tokens, width), F32),
         mid=vm((tokens, width), F32),
         e2=vm((tokens, width), BF16),
-        hp=vm((2 * seq, ff), F32),
+        hp=vm((4 * seq, ff), F32),
         act=vm((tokens, ff), BF16),
         gp=vm((tokens, ff), BF16),
         gact=vm((tokens, ff), F32),

time: 150 us -> 150 us (level)
  no operation moved by 1% of the time
where the time goes in v13:
time: 150 us; the launch traced here: 149 us
  Pallas kernels  149 us (99%)
    pallas_call x1, Pallas kernels, shards(): pl.pallas_call(functools.partial(kernel, n_dp, near, (UA, UB, UC), tuple(...  145 us
    pallas_call x1, Pallas kernels, shards(): pl.pallas_call(functools.partial(place, big, near), out_shape=moved + (f3...  3.59 us

profile of v13, /device:TPU:0, one launch (start us, length us, event | category | flops | bytes accessed | tf_op | source)
XLA Modules:
  0.0 149.4 jit_solution(12621448749486684288)
XLA Ops:
  0.7 145.2 %shard_map.271 = (bf16[512,768]{1,0:T(8,128)(2,1)S(1)}, bf16[512,768]{1,0:T(8,128)(2,1)S(1)}, f32[4,768]{1,0:T(4,128)S(1)}, f32[2312,768]{1,0:T(8,128)S(1)}) custom-call(bf16[512,768]{1,0:T(8,128)(2,1)} %refs_0_.1, bf16[4,768]{1,0:T(4,128)(2,1)} %refs_1_.1, s32[4,128]{1,0:T(4,128)} %refs_2_.1, f32[768]{0:T(1024)} %refs_3_.1, f32[768]{0:T(1024)} %refs_4_.1, ...), custom_call_target="tpu_custom_call" | custom-call | flops 6000000000 | bytes 20000000 | tf_op jit(solution)/shard_map/pallas_call | solution.py:910
  145.9 3.6 %shard_map.272 = (bf16[512,768]{1,0:T(8,128)(2,1)}, bf16[512,768]{1,0:T(8,128)(2,1)}, f32[4,768]{1,0:T(4,128)}, f32[3,192,768]{2,1,0:T(8,128)}, f32[192,768]{1,0...) custom-call(bf16[512,768]{1,0:T(8,128)(2,1)S(1)} %get-tuple-element., ...), custom_call_target="tpu_custom_call" | custom-call | tf_op jit(solution)/shard_map/pallas_call | solution.py:938

commit v14 on v13

--- a/solution.py
+++ b/solution.py
@@ -69,7 +69,7 @@
 def kernel(n_dp, near, units, names, *refs):
     out_o, ig_o, tg_o, f_out = refs[16:20]
     R = dict(zip(names, refs[20:]))
-    order = ("tok", "tim", "n1g", "n1b", "wqkv", "qvb", "seg", "wout", "outb", "cot", "wdn")
+    order = ("tok", "wout", "tim", "n1g", "n1b", "wqkv", "qvb", "seg", "outb", "cot", "wdn")
     order += ("n2g", "n2b", "wup", "upb", "dnb")
     tok, tim, wqkv, qvb, seg, wout, cot, wdn, wup = (
         R[s] for s in ("tok", "tim", "wqkv", "qvb", "seg", "wout", "cot", "wdn", "wup")
@@ -688,8 +688,8 @@
             for name in ("wqkv", "qvb", "seg"):
                 loads[name].wait()
 
+        when(r == 0, weights_out)
         project(r)
-        when(r == 0, weights_out)
         attend(r)
         for i in range(W_PIECES):
             when(r == rows_n - W_PIECES - 1 + i, lambda: weights_on(i))

time: 150 us -> 149 us (level)
  no operation moved by 1% of the time
where the time goes in v14:
time: 149 us
  Pallas kernels  148 us (99%)
    pallas_call x1, Pallas kernels, shards(): pl.pallas_call(functools.partial(kernel, n_dp, near, (UA, UB, UC), tuple(...  145 us
    pallas_call x1, Pallas kernels, shards(): pl.pallas_call(functools.partial(place, big, near), out_shape=moved + (f3...  3.59 us

profile of v14, /device:TPU:0, one launch (start us, length us, event | category | flops | bytes accessed | tf_op | source)
XLA Modules:
  0.0 149.0 jit_solution(15155240617262602954)
XLA Ops:
  0.7 144.8 %shard_map.271 = (bf16[512,768]{1,0:T(8,128)(2,1)S(1)}, bf16[512,768]{1,0:T(8,128)(2,1)S(1)}, f32[4,768]{1,0:T(4,128)S(1)}, f32[2312,768]{1,0:T(8,128)S(1)}) custom-call(bf16[512,768]{1,0:T(8,128)(2,1)} %refs_0_.1, bf16[4,768]{1,0:T(4,128)(2,1)} %refs_1_.1, s32[4,128]{1,0:T(4,128)} %refs_2_.1, f32[768]{0:T(1024)} %refs_3_.1, f32[768]{0:T(1024)} %refs_4_.1, ...), custom_call_target="tpu_custom_call" | custom-call | flops 6000000000 | bytes 20000000 | tf_op jit(solution)/shard_map/pallas_call | solution.py:910
  145.4 3.6 %shard_map.272 = (bf16[512,768]{1,0:T(8,128)(2,1)}, bf16[512,768]{1,0:T(8,128)(2,1)}, f32[4,768]{1,0:T(4,128)}, f32[3,192,768]{2,1,0:T(8,128)}, f32[192,768]{1,0...) custom-call(bf16[512,768]{1,0:T(8,128)(2,1)S(1)} %get-tuple-element., ...), custom_call_target="tpu_custom_call" | custom-call | tf_op jit(solution)/shard_map/pallas_call | solution.py:938
